TPU v7x, 128 devices: a whole 4x4x4 slice. The times are simulated.
128 devices in a mesh: gz: 64 (over x, y, z), gy: 2 (over core).
Axes of the slice: x: 4, y: 4, z: 4, core: 2. Of those that a mesh axis runs over, the one named last changes fastest.
Arguments:
- observed: float32 [512, 128, 512], P('gz', 'gy'), may hold values from 0.28 to 10.5, as said below
- psf_taps: float32 [8, 3, 15], replicated, may hold values from 0.05 to 1
- psf_index: int32 [512], replicated, may hold values from 0 to 7
- tissue: int32 [64, 4, 16], P('gz', 'gy'), may hold values from 0 to 1, as said below
- w_first: bfloat16 [32, 27], replicated, may hold values from -1.25 to 1.25
- b_first: float32 [32], replicated, may hold values from -3 to 3
- w_mid: bfloat16 [27, 32, 32], replicated, may hold values from -0.21875 to 0.21875
- b_mid: float32 [32], replicated, may hold values from -3 to 3
- w_last: bfloat16 [32], replicated, may hold values from -1 to 1
- b_last: float32 [1], replicated, may hold values from -2 to 2
Outputs:
- restored: float32 [512, 128, 512], P('gz', 'gy')
Inputs may be any that keep to these rules, and one draw needn't show every extreme that they name: `observed`: recorded intensities are positive. The 2 by 16 bricks of one device hold at most 3 tissue bricks, and some device holds exactly 3. Number the devices by slab times 2 plus row strip; every aligned group of 4 devices (two neighbouring slabs, both strips) holds exactly 4 tissue bricks.
All inputs are finite; a program needn't handle non-finite values.
Results may differ from a plain program's by a relative error of at most 0.0018.
Values may be sent and summed in bfloat16 or wider, within the bound.
No kernel may reach another device: no remote copies, remote signals or barrier semaphores. Data moves between devices by JAX's collectives and lax.ppermute only.
A program may use at most 128 MiB of HBM per device.

v0:
```python
import jax
import jax.numpy as jnp
from jax import lax
from jax.sharding import PartitionSpec as P

BY = 32
BX = 32
ROUNDS = 2
MOST = 3


def with_halo(cells, sides, width):
    for axis, dim in sides:
        count = lax.axis_size(axis)
        ends = count - 1
        head = lax.slice_in_dim(cells, 0, width, axis=dim)
        tail = lax.slice_in_dim(cells, cells.shape[dim] - width, cells.shape[dim], axis=dim)
        cells = jnp.concatenate(
            [
                lax.ppermute(tail, axis, [(i, (i + 1) % count) for i in range(ends)]),
                cells,
                lax.ppermute(head, axis, [((i + 1) % count, i) for i in range(ends)]),
            ],
            axis=dim,
        )
    return cells


def plane_kernels(psf_taps, psf_index):
    normed_taps = psf_taps / jnp.sum(psf_taps, axis=2, keepdims=True)
    models = jnp.arange(psf_taps.shape[0], dtype=jnp.int32)
    picker = (psf_index[:, None] == models[None, :]).astype(jnp.float32)
    return jnp.einsum("zk,kat->zat", picker, normed_taps, precision=lax.Precision.HIGHEST)


def forward_blur(padded, kernels):
    tap_count = kernels.shape[2]
    margin = tap_count // 2
    plane_count = padded.shape[0] - 2 * margin
    row_count = padded.shape[1] - 2 * margin
    column_count = padded.shape[2]
    own_kernels = kernels[margin : margin + plane_count]
    depth_pass = jnp.zeros((plane_count, padded.shape[1], column_count), jnp.float32)
    for tap_index in range(tap_count):
        depth_pass = (
            depth_pass
            + own_kernels[:, 0, tap_index][:, None, None]
            * padded[tap_index : tap_index + plane_count]
        )
    row_pass = jnp.zeros((plane_count, row_count, column_count), jnp.float32)
    for tap_index in range(tap_count):
        row_pass = (
            row_pass
            + own_kernels[:, 1, tap_index][:, None, None]
            * depth_pass[:, tap_index : tap_index + row_count]
        )
    widened = jnp.pad(row_pass, ((0, 0), (0, 0), (margin, margin)))
    result = jnp.zeros((plane_count, row_count, column_count), jnp.float32)
    for tap_index in range(tap_count):
        result = (
            result
            + own_kernels[:, 2, tap_index][:, None, None]
            * widened[:, :, tap_index : tap_index + column_count]
        )
    return result


def adjoint_blur(padded, kernels):
    tap_count = kernels.shape[2]
    margin = tap_count // 2
    plane_count = padded.shape[0] - 2 * margin
    row_count = padded.shape[1] - 2 * margin
    column_count = padded.shape[2]
    widened = jnp.pad(padded, ((0, 0), (0, 0), (margin, margin)))
    across = jnp.zeros(padded.shape, jnp.float32)
    for tap_index in range(tap_count):
        start = 2 * margin - tap_index
        across = (
            across
            + kernels[:, 2, tap_index][:, None, None] * widened[:, :, start : start + column_count]
        )
    along = jnp.zeros((padded.shape[0], row_count, column_count), jnp.float32)
    for tap_index in range(tap_count):
        start = 2 * margin - tap_index
        along = (
            along + kernels[:, 1, tap_index][:, None, None] * across[:, start : start + row_count]
        )
    result = jnp.zeros((plane_count, row_count, column_count), jnp.float32)
    for tap_index in range(tap_count):
        start = 2 * margin - tap_index
        result = (
            result
            + kernels[start : start + plane_count, 0, tap_index][:, None, None]
            * along[start : start + plane_count]
        )
    return result


def neighbour_shifts(brick_planes, brick_rows, brick_columns):
    voxel_index = jnp.arange(brick_planes * brick_rows * brick_columns, dtype=jnp.int32)
    plane_at = voxel_index // (brick_rows * brick_columns)
    row_at = voxel_index // brick_columns % brick_rows
    column_at = voxel_index % brick_columns
    shifts = []
    for step_plane in (-1, 0, 1):
        for step_row in (-1, 0, 1):
            for step_column in (-1, 0, 1):
                inside = (
                    (plane_at + step_plane >= 0)
                    & (plane_at + step_plane < brick_planes)
                    & (row_at + step_row >= 0)
                    & (row_at + step_row < brick_rows)
                    & (column_at + step_column >= 0)
                    & (column_at + step_column < brick_columns)
                )
                offset = (
                    step_plane * brick_rows * brick_columns + step_row * brick_columns + step_column
                )
                shifts.append((offset, inside))
    return shifts


def shifted(values, offset, inside, margin):
    voxels = values.shape[-1]
    padding = [(0, 0)] * (values.ndim - 1) + [(margin, margin)]
    widened = jnp.pad(values, padding)
    moved_values = lax.slice_in_dim(
        widened, margin + offset, margin + offset + voxels, axis=values.ndim - 1
    )
    return moved_values * inside.astype(values.dtype)


def restore_net(inputs, w_first, b_first, w_mid, b_mid, w_last, b_last, shifts, margin):
    stacked = jnp.stack(
        [shifted(inputs, offset, inside, margin) for offset, inside in shifts], axis=1
    )
    first = (
        jnp.einsum("ot,stv->sov", w_first, stacked, preferred_element_type=jnp.float32)
        + b_first[None, :, None]
    )
    hidden_one = jax.nn.relu(first).astype(jnp.bfloat16)
    total = jnp.zeros(first.shape, jnp.float32)
    for tap_index, (offset, inside) in enumerate(shifts):
        moved_hidden = shifted(hidden_one, offset, inside, margin)
        total = total + jnp.einsum(
            "oc,scv->sov", w_mid[tap_index], moved_hidden, preferred_element_type=jnp.float32
        )
    hidden_two = jax.nn.relu(total + b_mid[None, :, None]).astype(jnp.bfloat16)
    return (
        jnp.einsum("c,scv->sv", w_last, hidden_two, preferred_element_type=jnp.float32) + b_last[0]
    )


def body(observed, psf_taps, psf_index, tissue, w_first, b_first, w_mid, b_mid, w_last, b_last):
    plane_count, row_count, column_count = observed.shape
    margin = psf_taps.shape[2] // 2
    slab_total = lax.axis_size("gz")
    strip_total = lax.axis_size("gy")
    slab_id = lax.axis_index("gz")
    kernels = plane_kernels(psf_taps, psf_index)
    extended_all = jnp.pad(kernels, ((margin, margin), (0, 0), (0, 0)))
    extended = lax.dynamic_slice_in_dim(
        extended_all, slab_id * plane_count, plane_count + 2 * margin, 0
    )

    def surround(volume):
        return with_halo(volume.astype(jnp.bfloat16), (("gz", 0), ("gy", 1)), margin).astype(
            volume.dtype
        )

    normalizer = adjoint_blur(surround(jnp.ones_like(observed)), extended)
    estimate = observed
    for round_index in range(ROUNDS):
        blurred = forward_blur(surround(estimate), extended)
        estimate = estimate * adjoint_blur(surround(observed / blurred), extended) / normalizer
    voxel_total = float(plane_count * row_count * column_count * slab_total * strip_total)
    centre = lax.psum(jnp.sum(estimate), ("gz", "gy")) / voxel_total
    deviation = lax.psum(jnp.sum((estimate - centre) ** 2), ("gz", "gy"))
    spread = jnp.sqrt(deviation / voxel_total + 1e-06)
    normed = ((estimate - centre) / spread).astype(jnp.bfloat16)
    bricks_down = row_count // BY
    bricks_across = column_count // BX
    voxels = plane_count * BY * BX

    def to_bricks(volume):
        blocks = volume.reshape(plane_count, bricks_down, BY, bricks_across, BX)
        return blocks.transpose(1, 3, 0, 2, 4).reshape(bricks_down * bricks_across, voxels)

    estimate_bricks = to_bricks(estimate)
    normed_bricks = to_bricks(normed)
    flags = tissue.reshape(-1)
    position = jnp.cumsum(flags) - 1
    listing = jnp.nonzero(flags, size=MOST, fill_value=0)[0].astype(jnp.int32)
    shifts = neighbour_shifts(plane_count, BY, BX)
    margin_voxels = BY * BX + BX + 1
    is_tissue = flags[:, None] > 0
    work = normed_bricks[listing]
    residual = restore_net(
        work, w_first, b_first, w_mid, b_mid, w_last, b_last, shifts, margin_voxels
    )
    local_residual = jnp.where(is_tissue, residual[jnp.clip(position, 0, MOST - 1)], 0.0)
    restored_bricks = estimate_bricks + spread * local_residual
    blocks = restored_bricks.reshape(bricks_down, bricks_across, plane_count, BY, BX)
    return blocks.transpose(2, 0, 3, 1, 4).reshape(plane_count, row_count, column_count)


def solution(mesh):
    return jax.shard_map(
        body,
        mesh=mesh,
        in_specs=(P("gz", "gy", None), P(), P(), P("gz", "gy", None), P(), P(), P(), P(), P(), P()),
        out_specs=P("gz", "gy", None),
        check_vma=False,
    )
```

profile of v0, /device:TPU:1, one launch (start us, length us, event | category | flops | bytes accessed | tf_op | source)
XLA Modules:
  0.0 502.6 jit_solution(13679168773076535677)
XLA Ops:
  0.8 4.4 collective-permute-start.8
  7.9 4.2 collective-permute-start
  24.4 4.2 collective-permute-done.1
  29.9 3.6 collective-permute-start.3
  36.5 2.9 fusion.242
  42.1 4.1 fusion.389
  46.3 3.4 collective-permute-start.4
  54.7 3.0 collective-permute-start.11
  59.9 4.1 collective-permute-done.5
  65.4 3.5 collective-permute-start.7
  68.9 3.5 maximum_convert_fusion.2
  72.6 2.4 maximum_convert_fusion.1
  75.2 52.5 %fusion.60 = (f32[22,78,512]{2,1,0:T(8,128)}, f32[22,78,512]{2,1,0:T(8,128)}) fusion(f32[22,78,512]{2,1,0:T(8,128)} %maximum_convert_fusion.2, f32[22]{0:T(128)S(1)} %copy-done.122, f32[22]{0:T(128)S(1)} %copy-done.120, f32[22]{0:T(128)S(1)} %copy-done.118, f32[22]{0:T(128)S(1)} %copy-done.116, f32[22]{0:T(128)S(1)} %copy-done.114, f32[22]{0:T(128)S(1)} %copy-done.112, ...), kind=kLoop, calls=%fused_computation.133 | loop fusion | flops 50958336 | bytes 14058792 | tf_op jit(solution)/shard_map/add | solution.py:79
  127.9 26.3 %fusion.116 = f32[22,64,512]{2,1,0:T(8,128)} fusion(f32[22,78,512]{2,1,0:T(8,128)} %get-tuple-element.142, f32[22]{0:T(128)S(1)} %copy-done.88, f32[22]{0:T(128)S(1)} %copy-done.86, f32[22]{0:T(128)S(1)} %copy-done.78, f32[22]{0:T(128)S(1)} %copy-done.76, f32[22]{0:T(128)S(1)} %copy-done.74, f32[22]{0:T(128)S(1)} %copy-done.84, f32[22]{0:T(128)S(1)} %copy-done.72, ...), kind=kLoop, calls=%fused_computation.205 | loop fusion | flops 20905984 | bytes 46138664 | tf_op jit(solution)/shard_map/add | solution.py:86
  154.3 7.3 %fusion.130 = f32[22,64,512]{2,1,0:T(8,128)} fusion(f32[22,78,512]{2,1,0:T(8,128)S(1)} %copy-done.2, f32[22]{0:T(128)S(1)} %copy-done.88, f32[22]{0:T(128)S(1)} %copy-done.86, f32[22]{0:T(128)S(1)} %copy-done.78, f32[22]{0:T(128)S(1)} %copy-done.76, f32[22]{0:T(128)S(1)} %copy-done.74, f32[22]{0:T(128)S(1)} %copy-done.84, f32[22]{0:T(128)S(1)} %copy-done.72, ...), kind=kLoop, calls=%fused_computation.234 | loop fusion | flops 20905984 | bytes 46138664 | tf_op jit(solution)/shard_map/add | solution.py:86
  161.7 15.3 %fusion.637 = (bf16[8,64,512]{2,1,0:T(8,128)(2,1)S(1)}, f32[8,64,512]{2,1,0:T(8,128)}, f32[8,64,512]{2,1,0:T(8,128)}) fusion(f32[8,64,512]{2,1,0:T(8,128)S(1)} %copy-done.3, f32[22,64,512]{2,1,0:T(8,128)} %fusion.130, f32[8]{0:T(128)S(1)} %fusion.518, f32[8]{0:T(128)S(1)} %copy-done.141, f32[8]{0:T(128)S(1)} %copy-done.140, f32[8]{0:T(128)S(1)} %copy-done.138, ...), kind=kLoop, calls=%fused_computation.1084 | loop fusion | flops 15990784 | bytes 35127776 | tf_op jit(solution)/shard_map/convert_element_type | solution.py:167
  177.1 3.7 collective-permute-start.12
  185.7 5.3 %collective-permute-done.12 = bf16[7,64,512]{2,1,0:T(8,128)(2,1)S(1)} collective-permute-done((bf16[7,64,512]{2,1,0:T(8,128)(2,1)S(1)}, bf16[7,64,512]{2,1,0:T(8,128)(2,1)S(1)}, u32[]{:S(2)}, u32[]{:S(2)}) %collective-permute-start.12) | collective-permute-done | bytes 458784 | tf_op jit(solution)/shard_map/ppermute | solution.py:20
  191.0 4.3 collective-permute-done.13
  196.8 3.3 collective-permute-start.15
  201.7 2.9 fusion.228
  207.2 4.9 fusion.388
  212.2 3.7 collective-permute-start.16
  217.8 7.5 %collective-permute-done.16 = bf16[7,64,512]{2,1,0:T(8,128)(2,1)S(1)} collective-permute-done((bf16[7,64,512]{2,1,0:T(8,128)(2,1)S(1)}, bf16[7,64,512]{2,1,0:T(8,128)(2,1)S(1)}, u32[]{:S(2)}, u32[]{:S(2)}) %collective-permute-start.16) | collective-permute-done | bytes 458784 | tf_op jit(solution)/shard_map/ppermute | solution.py:20
  225.3 4.2 collective-permute-done.17
  231.0 3.6 collective-permute-start.19
  236.2 15.2 %fusion.88 = f32[22,78,512]{2,1,0:T(8,128)S(1)} fusion(f32[22,78,512]{2,1,0:T(8,128)S(1)} %maximum_convert_fusion.4, f32[22]{0:T(128)S(1)} %copy-done.123, f32[22]{0:T(128)S(1)} %copy-done.121, f32[22]{0:T(128)S(1)} %copy-done.119, f32[22]{0:T(128)S(1)} %copy-done.117, f32[22]{0:T(128)S(1)} %copy-done.115, f32[22]{0:T(128)S(1)} %copy-done.113, ...), kind=kLoop, calls=%fused_computation.161 | loop fusion | flops 25479168 | bytes 7030056 | tf_op jit(solution)/shard_map/add | solution.py:79
  251.6 7.3 %fusion.102 = f32[22,64,512]{2,1,0:T(8,128)} fusion(f32[22,78,512]{2,1,0:T(8,128)S(1)} %fusion.88, f32[22]{0:T(128)S(1)} %copy-done.89, f32[22]{0:T(128)S(1)} %copy-done.87, f32[22]{0:T(128)S(1)} %copy-done.79, f32[22]{0:T(128)S(1)} %copy-done.77, f32[22]{0:T(128)S(1)} %copy-done.75, f32[22]{0:T(128)S(1)} %copy-done.85, f32[22]{0:T(128)S(1)} %copy-done.73, ...), kind=kLoop, calls=%fused_computation.176 | loop fusion | flops 20905984 | bytes 46138664 | tf_op jit(solution)/shard_map/add | solution.py:86
  259.0 9.1 %fusion.635 = (f32[]{:T(128)}, f32[8,64,512]{2,1,0:T(8,128)S(1)}) fusion(f32[8,64,512]{2,1,0:T(8,128)} %get-tuple-element.9, f32[8,64,512]{2,1,0:T(8,128)} %get-tuple-element.8, f32[22,64,512]{2,1,0:T(8,128)} %fusion.102, f32[8]{0:T(128)} %copy-done.225, f32[8]{0:T(128)} %get-tuple-element.85, f32[8]{0:T(128)} %get-tuple-element.84, f32[8]{0:T(128)S(1)} %copy-done.139, ...), kind=kLoop, calls=%fused_computation.1083 | loop fusion | flops 8388607 | bytes 18874852 | tf_op jit(solution)/shard_map/reduce_sum | solution.py:177
  268.1 77.8 %psum.14 = f32[]{:T(128)} all-reduce(f32[]{:T(128)} %get-tuple-element.5), channel_id=1, replica_groups=mesh['gz'=64,'gy'=2] {'gz','gy'}, use_global_device_ids=true, to_apply=%region_2.3 | all-reduce | flops 1 | bytes 8 | tf_op jit(solution)/shard_map/psum | solution.py:177
  348.1 63.7 %psum.15 = f32[]{:T(128)} all-reduce(f32[]{:T(128)} %multiply_reduce_fusion), channel_id=1, replica_groups=mesh['gz'=64,'gy'=2] {'gz','gy'}, use_global_device_ids=true, to_apply=%region_4.5 | all-reduce | flops 1 | bytes 8 | tf_op jit(solution)/shard_map/psum | solution.py:178
  412.6 2.2 reshape.614
  414.8 3.5 copy.853
  418.5 3.6 reshape.615
  428.9 10.5 %stack.108 = bf16[3,27,8192]{2,1,0:T(8,128)(2,1)} concatenate(bf16[3,1,8192]{2,1,0:T(2,128)(2,1)} %copy.820, bf16[3,1,8192]{2,1,0:T(2,128)(2,1)S(1)} %copy.821, bf16[3,1,8192]{2,1,0:T(2,128)(2,1)S(1)} %copy.822, bf16[3,1,8192]{2,1,0:T(2,128)(2,1)S(1)} %copy.823, bf16[3,1,8192]{2,1,0:T(2,128)(2,1)S(1)} %copy.824, bf16[3,1,8192]{2,1,0:T(2,128)(2,1)S(1)} %copy.825, ...), dimensions={1} | concatenate | bytes 2654208 | tf_op jit(solution)/shard_map/stack | solution.py:134
  441.5 2.3 fusion.195
  443.8 2.4 convolution_bitcast_fusion.7
  446.2 2.4 convolution_bitcast_fusion.8
  448.7 2.4 convolution_bitcast_fusion.9
  451.0 2.3 convolution_bitcast_fusion.6
  453.3 2.9 reshape.613
  456.2 2.7 convolution_add_fusion.15
  478.3 2.5 fusion.9
  480.8 3.1 fusion.199
  485.0 2.7 gather.13
  487.7 5.1 %fusion.17 = f32[8,2,32,16,32]{4,2,0,3,1:T(8,128)S(1)} fusion(f32[8,2,32,16,32]{4,3,2,1,0:T(8,128)} %reshape.613, f32[2,16,8,32,32]{4,3,2,1,0:T(8,128)} %gather.13, f32[]{:T(128)S(6)} %sqrt.3, pred[2,16]{1,0:T(4,128)(4,1)S(1)} %copy-done.231), kind=kLoop, calls=%fused_computation.90 | loop fusion | flops 786432 | bytes 3145764 | tf_op jit(solution)/shard_map/transpose | solution.py:204
  492.8 5.2 %copy.847 = f32[8,2,32,16,32]{4,3,2,1,0:T(8,128)} copy(f32[8,2,32,16,32]{4,2,0,3,1:T(8,128)S(1)} %fusion.17) | data formatting | bytes 2097152 | tf_op jit(solution)/shard_map/transpose | solution.py:204
  498.0 4.4 reshape.617
  (611 shorter events, 75.0 us)
Async XLA Ops:
  0.0 439.4 %copy-start = (bf16[32,27]{1,0:T(8,128)(2,1)S(1)}, bf16[32,27]{1,0:T(8,128)(2,1)}, u32[]{:S(2)}) copy-start(bf16[32,27]{1,0:T(8,128)(2,1)} %param.14) | copy-start | bytes 5188
  0.0 22.6 %copy-start.229 = (s32[1,2,16]{2,1,0:T(2,128)S(1)}, s32[1,2,16]{2,1,0:T(2,128)}, u32[]{:S(2)}) copy-start(s32[1,2,16]{2,1,0:T(2,128)} %param.13) | copy-start | bytes 388
  0.8 51.6 %collective-permute-start.8 = (bf16[7,64,512]{2,1,0:T(8,128)(2,1)}, bf16[7,64,512]{2,1,0:T(8,128)(2,1)S(1)}, u32[]{:S(2)}, u32[]{:S(2)}) collective-permute-start(bf16[7,64,512]{2,1,0:T(8,128)(2,1)} %slice.1597), channel_id=1, source_target_pairs={{0,2},{2,4},{4,6},{6,8},{8,10},{10,12},{12,14},{14,16},{16,18},{18... | collective-permute-start | bytes 1376264 | tf_op jit(solution)/shard_map/ppermute | solution.py:20
  5.2 47.2 %collective-permute-start.9 = (bf16[7,64,512]{2,1,0:T(8,128)(2,1)}, bf16[7,64,512]{2,1,0:T(8,128)(2,1)}, u32[]{:S(2)}, u32[]{:S(2)}) collective-permute-start(bf16[7,64,512]{2,1,0:T(8,128)(2,1)} %slice.1597), channel_id=1, source_target_pairs={{2,0},{4,2},{6,4},{8,6},{10,8},{12,10},{14,12},{16,14},{18,16},{20... | collective-permute-start | bytes 1376264 | tf_op jit(solution)/shard_map/ppermute | solution.py:22
  7.9 16.5 %collective-permute-start = (bf16[7,64,512]{2,1,0:T(8,128)(2,1)S(1)}, bf16[7,64,512]{2,1,0:T(8,128)(2,1)S(1)}, u32[]{:S(2)}, u32[]{:S(2)}) collective-permute-start(bf16[7,64,512]{2,1,0:T(8,128)(2,1)S(1)} %get-tuple-element.26), channel_id=1, source_target_pairs={{0,2},{2,4},{4,6},{6,8},{8,10},{10,12},{12,14},{14,16},{16,18},{18... | collective-permute-start | bytes 1376264 | tf_op jit(solution)/shard_map/ppermute | solution.py:20
  12.1 16.5 %collective-permute-start.1 = (bf16[7,64,512]{2,1,0:T(8,128)(2,1)S(1)}, bf16[7,64,512]{2,1,0:T(8,128)(2,1)S(1)}, u32[]{:S(2)}, u32[]{:S(2)}) collective-permute-start(bf16[7,64,512]{2,1,0:T(8,128)(2,1)S(1)} %get-tuple-element.27), channel_id=1, source_target_pairs={{2,0},{4,2},{6,4},{8,6},{10,8},{12,10},{14,12},{16,14},{18,16},{20... | collective-permute-start | bytes 1376264 | tf_op jit(solution)/shard_map/ppermute | solution.py:22
  28.6 7.0 %collective-permute-start.2 = (bf16[22,7,512]{2,1,0:T(8,128)(2,1)S(1)}, bf16[22,7,512]{2,1,0:T(8,128)(2,1)S(1)}, u32[]{:S(2)}, u32[]{:S(2)}) collective-permute-start(bf16[22,7,512]{2,1,0:T(8,128)(2,1)S(1)} %get-tuple-element.18), channel_id=1, source_target_pairs={{0,1},{2,3},{4,5},{6,7},{8,9},{10,11},{12,13},{14,15},{16,17},{18,... | collective-permute-start | bytes 473096 | tf_op jit(solution)/shard_map/ppermute | solution.py:20
  29.9 5.7 %collective-permute-start.3 = (bf16[22,7,512]{2,1,0:T(8,128)(2,1)S(1)}, bf16[22,7,512]{2,1,0:T(8,128)(2,1)S(1)}, u32[]{:S(2)}, u32[]{:S(2)}) collective-permute-start(bf16[22,7,512]{2,1,0:T(8,128)(2,1)S(1)} %get-tuple-element.19), channel_id=1, source_target_pairs={{1,0},{3,2},{5,4},{7,6},{9,8},{11,10},{13,12},{15,14},{17,16},{19,... | collective-permute-start | bytes 473096 | tf_op jit(solution)/shard_map/ppermute | solution.py:22
  46.3 13.6 %collective-permute-start.4 = (bf16[7,64,512]{2,1,0:T(8,128)(2,1)S(1)}, bf16[7,64,512]{2,1,0:T(8,128)(2,1)S(1)}, u32[]{:S(2)}, u32[]{:S(2)}) collective-permute-start(bf16[7,64,512]{2,1,0:T(8,128)(2,1)S(1)} %get-tuple-element.24), channel_id=1, source_target_pairs={{0,2},{2,4},{4,6},{6,8},{8,10},{10,12},{12,14},{14,16},{16,18},{18... | collective-permute-start | bytes 1376264 | tf_op jit(solution)/shard_map/ppermute | solution.py:20
  49.7 14.3 %collective-permute-start.5 = (bf16[7,64,512]{2,1,0:T(8,128)(2,1)S(1)}, bf16[7,64,512]{2,1,0:T(8,128)(2,1)S(1)}, u32[]{:S(2)}, u32[]{:S(2)}) collective-permute-start(bf16[7,64,512]{2,1,0:T(8,128)(2,1)S(1)} %get-tuple-element.25), channel_id=1, source_target_pairs={{2,0},{4,2},{6,4},{8,6},{10,8},{12,10},{14,12},{16,14},{18,16},{20... | collective-permute-start | bytes 1376264 | tf_op jit(solution)/shard_map/ppermute | solution.py:22
  51.7 23.2 %copy-start.226 = (f32[22]{0:T(128)}, f32[22]{0:T(128)S(1)}, u32[]{:S(2)}) copy-start(f32[22]{0:T(128)S(1)} %get-tuple-element.115) | copy-start | bytes 268
  53.4 15.6 %collective-permute-start.10 = (bf16[22,7,512]{2,1,0:T(8,128)(2,1)S(1)}, bf16[22,7,512]{2,1,0:T(8,128)(2,1)S(1)}, u32[]{:S(2)}, u32[]{:S(2)}) collective-permute-start(bf16[22,7,512]{2,1,0:T(8,128)(2,1)S(1)} %get-tuple-element.14), channel_id=1, source_target_pairs={{0,1},{2,3},{4,5},{6,7},{8,9},{10,11},{12,13},{14,15},{16,17},{18,... | collective-permute-start | bytes 473096 | tf_op jit(solution)/shard_map/ppermute | solution.py:20
  54.7 14.3 %collective-permute-start.11 = (bf16[22,7,512]{2,1,0:T(8,128)(2,1)S(1)}, bf16[22,7,512]{2,1,0:T(8,128)(2,1)S(1)}, u32[]{:S(2)}, u32[]{:S(2)}) collective-permute-start(bf16[22,7,512]{2,1,0:T(8,128)(2,1)S(1)} %get-tuple-element.15), channel_id=1, source_target_pairs={{1,0},{3,2},{5,4},{7,6},{9,8},{11,10},{13,12},{15,14},{17,16},{19,... | collective-permute-start | bytes 473096 | tf_op jit(solution)/shard_map/ppermute | solution.py:22
  57.8 103.8 %copy-start.225 = (f32[8]{0:T(128)}, f32[8]{0:T(128)S(1)}, u32[]{:S(2)}) copy-start(f32[8]{0:T(128)S(1)} %fusion.518) | copy-start | bytes 100
  64.1 8.5 %collective-permute-start.6 = (bf16[22,7,512]{2,1,0:T(8,128)(2,1)S(1)}, bf16[22,7,512]{2,1,0:T(8,128)(2,1)S(1)}, u32[]{:S(2)}, u32[]{:S(2)}) collective-permute-start(bf16[22,7,512]{2,1,0:T(8,128)(2,1)S(1)} %get-tuple-element.16), channel_id=1, source_target_pairs={{0,1},{2,3},{4,5},{6,7},{8,9},{10,11},{12,13},{14,15},{16,17},{18,... | collective-permute-start | bytes 473096 | tf_op jit(solution)/shard_map/ppermute | solution.py:20
  65.4 7.2 %collective-permute-start.7 = (bf16[22,7,512]{2,1,0:T(8,128)(2,1)S(1)}, bf16[22,7,512]{2,1,0:T(8,128)(2,1)S(1)}, u32[]{:S(2)}, u32[]{:S(2)}) collective-permute-start(bf16[22,7,512]{2,1,0:T(8,128)(2,1)S(1)} %get-tuple-element.17), channel_id=1, source_target_pairs={{1,0},{3,2},{5,4},{7,6},{9,8},{11,10},{13,12},{15,14},{17,16},{19,... | collective-permute-start | bytes 473096 | tf_op jit(solution)/shard_map/ppermute | solution.py:22
  75.1 52.7 %copy-start.61 = (f32[22]{0:T(128)S(1)}, f32[22]{0:T(128)}, u32[]{:S(2)}) copy-start(f32[22]{0:T(128)} %get-tuple-element.86) | copy-start | bytes 268
  75.1 52.7 %copy-start.62 = (f32[22]{0:T(128)S(1)}, f32[22]{0:T(128)}, u32[]{:S(2)}) copy-start(f32[22]{0:T(128)} %get-tuple-element.95) | copy-start | bytes 268
  75.1 52.7 %copy-start.64 = (f32[22]{0:T(128)S(1)}, f32[22]{0:T(128)}, u32[]{:S(2)}) copy-start(f32[22]{0:T(128)} %get-tuple-element.105) | copy-start | bytes 268
  75.1 52.7 %copy-start.66 = (f32[22]{0:T(128)S(1)}, f32[22]{0:T(128)}, u32[]{:S(2)}) copy-start(f32[22]{0:T(128)} %get-tuple-element.106) | copy-start | bytes 268
  75.1 52.7 %copy-start.68 = (f32[22]{0:T(128)S(1)}, f32[22]{0:T(128)}, u32[]{:S(2)}) copy-start(f32[22]{0:T(128)} %get-tuple-element.107) | copy-start | bytes 268
  75.1 52.7 %copy-start.70 = (f32[22]{0:T(128)S(1)}, f32[22]{0:T(128)}, u32[]{:S(2)}) copy-start(f32[22]{0:T(128)} %get-tuple-element.108) | copy-start | bytes 268
  75.1 52.7 %copy-start.72 = (f32[22]{0:T(128)S(1)}, f32[22]{0:T(128)}, u32[]{:S(2)}) copy-start(f32[22]{0:T(128)} %get-tuple-element.109) | copy-start | bytes 268
  75.1 52.7 %copy-start.74 = (f32[22]{0:T(128)S(1)}, f32[22]{0:T(128)}, u32[]{:S(2)}) copy-start(f32[22]{0:T(128)} %get-tuple-element.110) | copy-start | bytes 268
  75.1 52.7 %copy-start.76 = (f32[22]{0:T(128)S(1)}, f32[22]{0:T(128)}, u32[]{:S(2)}) copy-start(f32[22]{0:T(128)} %get-tuple-element.111) | copy-start | bytes 268
  75.1 52.7 %copy-start.78 = (f32[22]{0:T(128)S(1)}, f32[22]{0:T(128)}, u32[]{:S(2)}) copy-start(f32[22]{0:T(128)} %get-tuple-element.112) | copy-start | bytes 268
  75.2 52.7 %copy-start.80 = (f32[22]{0:T(128)S(1)}, f32[22]{0:T(128)}, u32[]{:S(2)}) copy-start(f32[22]{0:T(128)} %get-tuple-element.96) | copy-start | bytes 268
  75.2 52.7 %copy-start.82 = (f32[22]{0:T(128)S(1)}, f32[22]{0:T(128)}, u32[]{:S(2)}) copy-start(f32[22]{0:T(128)} %get-tuple-element.103) | copy-start | bytes 268
  75.2 52.7 %copy-start.84 = (f32[22]{0:T(128)S(1)}, f32[22]{0:T(128)}, u32[]{:S(2)}) copy-start(f32[22]{0:T(128)} %get-tuple-element.104) | copy-start | bytes 268
  75.2 52.7 %copy-start.86 = (f32[22]{0:T(128)S(1)}, f32[22]{0:T(128)}, u32[]{:S(2)}) copy-start(f32[22]{0:T(128)} %get-tuple-element.113) | copy-start | bytes 268
  75.2 52.7 %copy-start.88 = (f32[22]{0:T(128)S(1)}, f32[22]{0:T(128)}, u32[]{:S(2)}) copy-start(f32[22]{0:T(128)} %get-tuple-element.114) | copy-start | bytes 268
  127.9 26.3 %copy-start.2 = (f32[22,78,512]{2,1,0:T(8,128)S(1)}, f32[22,78,512]{2,1,0:T(8,128)}, u32[]{:S(2)}) copy-start(f32[22,78,512]{2,1,0:T(8,128)} %get-tuple-element.143) | copy-start | bytes 10543108
  161.7 20.4 %copy-start.230 = (s32[1,2,16]{2,1,0:T(2,128)S(1)}, s32[1,2,16]{2,1,0:T(2,128)}, u32[]{:S(2)}) copy-start(s32[1,2,16]{2,1,0:T(2,128)} %param.13) | copy-start | bytes 388
  177.1 13.9 %collective-permute-start.12 = (bf16[7,64,512]{2,1,0:T(8,128)(2,1)S(1)}, bf16[7,64,512]{2,1,0:T(8,128)(2,1)S(1)}, u32[]{:S(2)}, u32[]{:S(2)}) collective-permute-start(bf16[7,64,512]{2,1,0:T(8,128)(2,1)S(1)} %get-tuple-element.22), channel_id=1, source_target_pairs={{0,2},{2,4},{4,6},{6,8},{8,10},{10,12},{12,14},{14,16},{16,18},{18... | collective-permute-start | bytes 1376264 | tf_op jit(solution)/shard_map/ppermute | solution.py:20
  180.8 14.5 %collective-permute-start.13 = (bf16[7,64,512]{2,1,0:T(8,128)(2,1)S(1)}, bf16[7,64,512]{2,1,0:T(8,128)(2,1)S(1)}, u32[]{:S(2)}, u32[]{:S(2)}) collective-permute-start(bf16[7,64,512]{2,1,0:T(8,128)(2,1)S(1)} %get-tuple-element.23), channel_id=1, source_target_pairs={{2,0},{4,2},{6,4},{8,6},{10,8},{12,10},{14,12},{16,14},{18,16},{20... | collective-permute-start | bytes 1376264 | tf_op jit(solution)/shard_map/ppermute | solution.py:22
  195.5 5.2 %collective-permute-start.14 = (bf16[22,7,512]{2,1,0:T(8,128)(2,1)S(1)}, bf16[22,7,512]{2,1,0:T(8,128)(2,1)S(1)}, u32[]{:S(2)}, u32[]{:S(2)}) collective-permute-start(bf16[22,7,512]{2,1,0:T(8,128)(2,1)S(1)} %get-tuple-element.12), channel_id=1, source_target_pairs={{0,1},{2,3},{4,5},{6,7},{8,9},{10,11},{12,13},{14,15},{16,17},{18,... | collective-permute-start | bytes 473096 | tf_op jit(solution)/shard_map/ppermute | solution.py:20
  196.8 4.1 collective-permute-start.15
  200.7 224.7 %copy-start.41 = (bf16[8192]{0:T(1024)(128)(2,1)}, bf16[8192]{0:T(1024)(128)(2,1)S(1)}, u32[]{:S(2)}) copy-start(bf16[8192]{0:T(1024)(128)(2,1)S(1)} %get-tuple-element.166) | copy-start | bytes 49156
  200.7 224.7 %copy-start.43 = (bf16[8192]{0:T(1024)(128)(2,1)}, bf16[8192]{0:T(1024)(128)(2,1)S(1)}, u32[]{:S(2)}) copy-start(bf16[8192]{0:T(1024)(128)(2,1)S(1)} %get-tuple-element.167) | copy-start | bytes 49156
  212.1 22.6 %copy-start.228 = (s32[32]{0:T(128)S(1)}, s32[32]{0:T(128)}, u32[]{:S(2)}) copy-start(s32[32]{0:T(128)} %get-tuple-element.145) | copy-start | bytes 388
  212.2 13.1 %collective-permute-start.16 = (bf16[7,64,512]{2,1,0:T(8,128)(2,1)S(1)}, bf16[7,64,512]{2,1,0:T(8,128)(2,1)S(1)}, u32[]{:S(2)}, u32[]{:S(2)}) collective-permute-start(bf16[7,64,512]{2,1,0:T(8,128)(2,1)S(1)} %get-tuple-element.20), channel_id=1, source_target_pairs={{0,2},{2,4},{4,6},{6,8},{8,10},{10,12},{12,14},{14,16},{16,18},{18... | collective-permute-start | bytes 1376264 | tf_op jit(solution)/shard_map/ppermute | solution.py:20
  215.8 13.7 %collective-permute-start.17 = (bf16[7,64,512]{2,1,0:T(8,128)(2,1)S(1)}, bf16[7,64,512]{2,1,0:T(8,128)(2,1)S(1)}, u32[]{:S(2)}, u32[]{:S(2)}) collective-permute-start(bf16[7,64,512]{2,1,0:T(8,128)(2,1)S(1)} %get-tuple-element.21), channel_id=1, source_target_pairs={{2,0},{4,2},{6,4},{8,6},{10,8},{12,10},{14,12},{16,14},{18,16},{20... | collective-permute-start | bytes 1376264 | tf_op jit(solution)/shard_map/ppermute | solution.py:22
  217.2 208.2 %copy-start.45 = (bf16[8192]{0:T(1024)(128)(2,1)}, bf16[8192]{0:T(1024)(128)(2,1)S(1)}, u32[]{:S(2)}) copy-start(bf16[8192]{0:T(1024)(128)(2,1)S(1)} %get-tuple-element.168) | copy-start | bytes 49156
  217.2 208.2 %copy-start.47 = (bf16[8192]{0:T(1024)(128)(2,1)}, bf16[8192]{0:T(1024)(128)(2,1)S(1)}, u32[]{:S(2)}) copy-start(bf16[8192]{0:T(1024)(128)(2,1)S(1)} %get-tuple-element.169) | copy-start | bytes 49156
  217.2 208.2 %copy-start.49 = (bf16[8192]{0:T(1024)(128)(2,1)}, bf16[8192]{0:T(1024)(128)(2,1)S(1)}, u32[]{:S(2)}) copy-start(bf16[8192]{0:T(1024)(128)(2,1)S(1)} %get-tuple-element.171) | copy-start | bytes 49156
  217.2 208.2 %copy-start.51 = (bf16[8192]{0:T(1024)(128)(2,1)}, bf16[8192]{0:T(1024)(128)(2,1)S(1)}, u32[]{:S(2)}) copy-start(bf16[8192]{0:T(1024)(128)(2,1)S(1)} %get-tuple-element.170) | copy-start | bytes 49156
  229.7 5.6 %collective-permute-start.18 = (bf16[22,7,512]{2,1,0:T(8,128)(2,1)S(1)}, bf16[22,7,512]{2,1,0:T(8,128)(2,1)S(1)}, u32[]{:S(2)}, u32[]{:S(2)}) collective-permute-start(bf16[22,7,512]{2,1,0:T(8,128)(2,1)S(1)} %get-tuple-element.10), channel_id=1, source_target_pairs={{0,1},{2,3},{4,5},{6,7},{8,9},{10,11},{12,13},{14,15},{16,17},{18,... | collective-permute-start | bytes 473096 | tf_op jit(solution)/shard_map/ppermute | solution.py:20
  231.0 4.3 collective-permute-start.19
  (208 other events, 1231.2 us)
where the time goes:
time: 511 us; the launch traced here: 503 us
  other arithmetic  182 us (36%)
  blocking collectives  141 us (28%)
  local copies, waits for them, and re-layouts  53.5 us (10%)
  starting transfers between devices  49.3 us (10%)
  matrix products  37.8 us (7%)
  waiting for transfers between devices  32.3 us (6%)
  between operations  6.28 us (1%)
    psum x1, blocking collectives, body(): centre = lax.psum(jnp.sum(estimate), ('gz', 'gy')) / voxel_total  77.8 us
    add x2, other arithmetic, adjoint_blur(): across + kernels[:, 2, tap_index][:, None, None] * widened[:, :, start:st...  67.7 us
    psum x1, blocking collectives, body(): deviation = lax.psum(jnp.sum((estimate - centre) ** 2), ('gz', 'gy'))  63.7 us
    add x3, other arithmetic, adjoint_blur(): along + kernels[:, 1, tap_index][:, None, None] * across[:, start:start +...  40.8 us
    dot_general x26, matrix products, restore_net(): jnp.einsum('oc,scv->sov', w_mid[tap_index], moved_hidden, preferred_eleme...  32.5 us
    ppermute x10, starting transfers between devices, with_halo(): lax.ppermute(tail, axis, [(i, (i + 1) % count) for i in range(ends)])  25.8 us
    convert_element_type x4, other arithmetic, surround(): volume.astype(jnp.bfloat16)  25.6 us
    ppermute x10, starting transfers between devices, with_halo(): lax.ppermute(head, axis, [((i + 1) % count, i) for i in range(ends)])  23.5 us
  transfers between devices with their start and end apart: 20, of which 9 were waited for; matrix products, arithmetic and copies ran while one was open for 7% of the time, Pallas kernels for 0%

commit v1 on v0

v1 whole, which is shorter than its diff:
```python
import jax
import jax.numpy as jnp
from jax import lax
from jax.experimental import pallas as pl
from jax.experimental.pallas import tpu as pltpu
from jax.sharding import PartitionSpec as P

F32 = jnp.float32
BF16 = jnp.bfloat16
SZ, SY, NX = 8, 64, 512
NZ, NY = 512, 128
TAPS, R = 15, 7
HALO = 16
EXT = SY + HALO
MODELS = 8
BY, BX = 32, 32
CH = 32
SPAN = SZ + 2 * R
COUNT = float(NZ * NY * NX)
LOCAL = float(SZ * SY * NX)
DEVICES = 128
AT_FORWARD = 0
AT_ADJOINT = SZ * SPAN
AT_ROWS = 2 * SZ * SPAN
AT_COLUMNS = AT_ROWS + SZ * TAPS
MIB = 1024 * 1024

VMEM = pl.BlockSpec(memory_space=pltpu.VMEM)
SMEM = pl.BlockSpec(memory_space=pltpu.SMEM)


def iota(shape, axis):
    return lax.broadcasted_iota(jnp.int32, shape, axis)


def call(kernel, outs, ins, specs, scratch=(), flops=0, limit=24):
    moved = sum(x.size * x.dtype.itemsize for x in list(ins) + list(outs))
    return pl.pallas_call(
        kernel,
        out_shape=outs,
        in_specs=specs,
        out_specs=[VMEM] * len(outs),
        scratch_shapes=scratch,
        compiler_params=pltpu.CompilerParams(vmem_limit_bytes=limit * MIB),
        cost_estimate=pl.CostEstimate(flops=flops, bytes_accessed=moved, transcendentals=0),
    )(*ins)


def shape(dims, dtype):
    return jax.ShapeDtypeStruct(dims, dtype)


def send_planes(volume_ref, first_ref, second_ref):
    even = 1 - lax.axis_index("gz") % 2

    @pl.loop(0, R)
    def _(k):
        first_ref[k] = volume_ref[k + even].astype(BF16)
        second_ref[k] = volume_ref[k + 1 - even].astype(BF16)


def edge_rows(volume, rows, gy):
    start = pl.multiple_of((1 - gy) * (SY - rows), rows)
    return volume[:, pl.ds(start, rows), :]


def prepare_kernel(observed_ref, first_ref, second_ref, edge_ref):
    gy = lax.axis_index("gy")
    send_planes(observed_ref, first_ref, second_ref)
    edge_ref[...] = edge_rows(observed_ref, HALO, gy)


def split(value):
    high = value.astype(BF16)
    return high, (value - high.astype(F32)).astype(BF16)


def setup_kernel(
    table_ref, kx_ref, kyt_ref, weight_ref, rows_f_ref, rows_a_ref, cols_f_ref, cols_a_ref, inverse_ref
):
    gy = lax.axis_index("gy")

    def place(index):
        return jnp.where(index < SY, index, jnp.where(gy == 0, index, index - EXT))

    lane = iota((EXT, 256), 1)
    piece = lane // EXT
    inside = place(lane - piece * EXT)
    outside = place(iota((EXT, 256), 0))
    used = piece < 3
    tap_f = jnp.where(used, inside - outside + R, -1)
    tap_a = jnp.where(used, outside - inside + R, -1)[:SY]
    low = piece == 1
    source = iota((256, 128), 0)
    target = iota((256, 128), 1)
    tap_cf = source - target - (64 - R)
    tap_ca = target - source + (64 + R)

    @pl.loop(0, SZ)
    def _(z):
        def table(taps, at):
            total = jnp.zeros(taps.shape, F32)
            for t in range(TAPS):
                total = jnp.where(taps == t, table_ref[at + z * TAPS + t], total)
            return total

        def halves(value, is_low):
            high = value.astype(BF16).astype(F32)
            return jnp.where(is_low, value - high, high).astype(BF16)

        rows_f_ref[z] = halves(table(tap_f, AT_ROWS), low)
        rows_a_ref[z] = halves(table(tap_a, AT_ROWS), low[:SY])
        for taps, out in ((tap_cf, cols_f_ref), (tap_ca, cols_a_ref)):
            high, rest = split(table(taps, AT_COLUMNS))
            out[z, :, :128] = high
            out[z, :, 128:] = rest

    column = iota((1, NX), 1)
    row = iota((SY, 1), 0) + gy * SY
    across = jnp.zeros((24, NX), F32)
    along = jnp.zeros((SY, 128), F32)
    for t in range(TAPS):
        at_x = column + R - t
        at_y = row + R - t
        across += jnp.where((at_x >= 0) & (at_x < NX), kx_ref[:, t : t + 1], 0.0)
        along += jnp.where((at_y >= 0) & (at_y < NY), kyt_ref[t : t + 1, :], 0.0)
    across = jnp.concatenate([across, jnp.zeros((104, NX), F32)], axis=0)
    for z in range(SZ):
        norm = jnp.dot(
            along * weight_ref[z : z + 1, :],
            across,
            precision=lax.Precision.HIGHEST,
            preferred_element_type=F32,
        )
        inverse_ref[z] = 1.0 / norm


def plane_pass(coefficient, own_ref, first_ref, second_ref, emit):
    even = lax.axis_index("gz") % 2 == 0
    high, wide = 16, 256

    def run(low_ref, high_ref):
        @pl.loop(0, SY // high)
        def _(block):
            rows = pl.ds(pl.multiple_of(block * high, high), high)
            for part in range(NX // wide):
                lanes = pl.ds(part * wide, wide)
                planes = [low_ref[k, rows, lanes].astype(F32) for k in range(R)]
                planes += [own_ref[k, rows, lanes] for k in range(SZ)]
                planes += [high_ref[k, rows, lanes].astype(F32) for k in range(R)]
                for z in range(SZ):
                    terms = [coefficient(z, j) * planes[j] for j in range(z, z + TAPS)]
                    while len(terms) > 1:
                        terms = [sum(terms[i : i + 2]) for i in range(0, len(terms), 2)]
                    emit(z, rows, lanes, terms[0])

    @pl.when(even)
    def _():
        run(second_ref, first_ref)

    @pl.when(jnp.logical_not(even))
    def _():
        run(first_ref, second_ref)


def forward_planes_kernel(table_ref, own_ref, first_ref, second_ref, out_ref, edge_ref):
    def emit(z, rows, lanes, value):
        out_ref[z, rows, lanes] = value

    plane_pass(
        lambda z, j: table_ref[AT_FORWARD + z * SPAN + j], own_ref, first_ref, second_ref, emit
    )
    edge_ref[...] = edge_rows(out_ref, HALO, lax.axis_index("gy")).astype(BF16)


def adjoint_coefficient(table_ref):
    return lambda z, j: table_ref[AT_ADJOINT + j * SZ + z]


def update_kernel(
    table_ref, own_ref, first_ref, second_ref, before_ref, inverse_ref, out_ref, to_first_ref, to_second_ref
):
    def emit(z, rows, lanes, value):
        out_ref[z, rows, lanes] = (
            before_ref[z, rows, lanes] * value * inverse_ref[z, rows, lanes]
        )

    plane_pass(adjoint_coefficient(table_ref), own_ref, first_ref, second_ref, emit)
    send_planes(out_ref, to_first_ref, to_second_ref)


def last_update_kernel(
    table_ref, own_ref, first_ref, second_ref, before_ref, inverse_ref, out_ref, moments_ref
):
    def emit(z, rows, lanes, value):
        out_ref[z, rows, lanes] = (
            before_ref[z, rows, lanes] * value * inverse_ref[z, rows, lanes]
        )

    plane_pass(adjoint_coefficient(table_ref), own_ref, first_ref, second_ref, emit)
    total = jnp.zeros((SY, NX), F32)
    for z in range(SZ):
        total += out_ref[z]
    mean = jnp.sum(total, keepdims=True) / LOCAL
    squares = jnp.zeros((SY, NX), F32)
    for z in range(SZ):
        squares += (out_ref[z] - mean) ** 2
    deviation = jnp.sum(squares, keepdims=True)
    moments_ref[...] = jnp.where(iota((DEVICES, 128), 1) == 0, mean, deviation)


def column_pass(value, matrix):
    left = iota((EXT, 128), 1) < 64
    turned = pltpu.roll(value, 64, axis=1)
    edge = turned[:, :128]
    blocks = [jnp.where(left, 0.0, edge)]
    blocks += [turned[:, 128 * j : 128 * (j + 1)] for j in range(1, NX // 128)]
    blocks += [jnp.where(left, edge, 0.0)]
    blocks = [b.astype(BF16) for b in blocks]
    windows = [jnp.concatenate(blocks[j : j + 2], axis=1) for j in range(NX // 128)]
    product = jnp.dot(jnp.concatenate(windows, axis=0), matrix, preferred_element_type=F32)
    product = product[:, :128] + product[:, 128:]
    return jnp.concatenate(
        [product[EXT * j : EXT * (j + 1)] for j in range(NX // 128)], axis=1
    )


def row_pass(matrix, value):
    high, rest = split(value)
    stacked = jnp.concatenate([high, high, rest, jnp.zeros((16, NX), BF16)], axis=0)
    return jnp.dot(matrix, stacked, preferred_element_type=F32)


def ratio_kernel(
    u_ref, u_edge_ref, observed_ref, observed_edge_ref,
    rows_f_ref, rows_a_ref, cols_f_ref, cols_a_ref,
    out_ref, to_first_ref, to_second_ref,
):
    for z in range(SZ):
        extended = jnp.concatenate([u_ref[z], u_edge_ref[z].astype(F32)], axis=0)
        blurred = column_pass(row_pass(rows_f_ref[z], extended), cols_f_ref[z])
        seen = jnp.concatenate([observed_ref[z], observed_edge_ref[z]], axis=0)
        back = column_pass(seen / blurred, cols_a_ref[z])
        out_ref[z] = row_pass(rows_a_ref[z], back)
    send_planes(out_ref, to_first_ref, to_second_ref)


def bricks_kernel(
    tissue_ref, estimate_ref, moments_ref, w1_ref, b1_ref, w2_ref, b2_ref, w3_ref, b3_ref,
    out_ref, listing, stack, hidden, partial, result,
):
    means = moments_ref[:, 0:1]
    centre = jnp.sum(means, axis=0, keepdims=True) / DEVICES
    deviation = jnp.sum(moments_ref[:, 1:2] + LOCAL * (means - centre) ** 2, axis=0, keepdims=True)
    spread = jnp.sqrt(deviation / COUNT + 1e-06)
    out_ref[...] = estimate_ref[...]
    stack[...] = jnp.zeros(stack.shape, F32)

    def note(b, count):
        listing[count] = b
        return count + jnp.where(tissue_ref[b] > 0, 1, 0)

    bricks_across = NX // BX
    many = lax.fori_loop(0, (SY // BY) * bricks_across, note, 0)

    lane = iota((8, 128), 1)
    row = iota((8, 128), 0)
    group = lane // BX
    column = lane % BX
    tall_column = iota((CH, 128), 1) % BX
    tall_group = iota((CH, 128), 1) // BX

    def beside(value, at):
        return (
            jnp.where(at == 0, 0.0, pltpu.roll(value, 1, axis=1)),
            value,
            jnp.where(at == BX - 1, 0.0, pltpu.roll(value, 127, axis=1)),
        )

    @pl.loop(0, many)
    def _(n):
        brick = listing[n]
        down = brick // bricks_across
        over = brick % bricks_across
        lanes = pl.ds(pl.multiple_of(over // 4 * 128, 128), 128)
        quarter = over % 4

        def rows_of(g):
            return pl.ds(pl.multiple_of(down * BY + 8 * g, 8), 8)

        for z in range(SZ):
            brick_plane = jnp.zeros((8, 128), F32)
            for g in range(4):
                block = estimate_ref[z, rows_of(g), lanes]
                turned = pltpu.roll(block, (BX * (g - quarter)) % 128, axis=1)
                brick_plane = jnp.where(group == g, turned, brick_plane)
            normed = ((brick_plane - centre) / spread).astype(BF16).astype(F32)
            before = pltpu.roll(normed, 1, axis=0)
            after = pltpu.roll(normed, 7, axis=0)
            wrapped_before = jnp.where(group == 0, 0.0, pltpu.roll(before, BX, axis=1))
            wrapped_after = jnp.where(group == 3, 0.0, pltpu.roll(after, 128 - BX, axis=1))
            versions = (
                jnp.where(row == 0, wrapped_before, before),
                normed,
                jnp.where(row == 7, wrapped_after, after),
            )
            for b, version in enumerate(versions):
                for c, moved in enumerate(beside(version, column)):
                    for a in range(3):
                        to = z - (a - 1)
                        if 0 <= to < SZ:
                            tap = 9 * a + 3 * b + c
                            stack[pl.ds(to * 256 + tap, 8, stride=32), :] = moved

        @pl.loop(0, SZ)
        def _(z):
            for pair in range(4):
                taps = [
                    stack[pl.ds(pl.multiple_of(z * 256 + (2 * pair + e) * 32, 32), 32), :].astype(BF16)
                    for e in range(2)
                ]
                first = jnp.dot(
                    w1_ref[...], jnp.concatenate(taps, axis=1), preferred_element_type=F32
                )
                first = jnp.maximum(first + b1_ref[...], 0.0)
                for e in range(2):
                    r = 2 * pair + e
                    value = first[:, 128 * e : 128 * (e + 1)]
                    places = [(r + 1, value)]
                    if r == 7:
                        places.append(
                            (0, jnp.where(tall_group == 0, 0.0, pltpu.roll(value, BX, axis=1)))
                        )
                    if r == 0:
                        places.append(
                            (9, jnp.where(tall_group == 3, 0.0, pltpu.roll(value, 128 - BX, axis=1)))
                        )
                    for at, placed in places:
                        moved = jnp.concatenate(beside(placed, tall_column), axis=0)
                        hidden[z, at] = moved.astype(BF16)

        for pair in range(4):
            @pl.loop(0, SZ)
            def _(z):
                taps = [
                    hidden[z, 2 * pair + e : 2 * pair + e + 3].reshape(9 * CH, 128) for e in range(2)
                ]
                partial[z] = jnp.dot(
                    w2_ref[...], jnp.concatenate(taps, axis=1), preferred_element_type=F32
                )

            for z in range(SZ):
                total = partial[z, CH : 2 * CH] + b2_ref[...]
                if z > 0:
                    total += partial[z - 1, :CH]
                if z < SZ - 1:
                    total += partial[z + 1, 2 * CH :]
                second = jnp.maximum(total, 0.0).astype(BF16).astype(F32)
                last = jnp.sum(w3_ref[...] * second, axis=0, keepdims=True) + b3_ref[...]
                result[z, 2 * pair : 2 * pair + 1, :] = last[:, :128]
                result[z, 2 * pair + 1 : 2 * pair + 2, :] = last[:, 128:]

        for z in range(SZ):
            change = result[z] * spread
            for g in range(4):
                turned = pltpu.roll(change, (BX * (quarter - g)) % 128, axis=1)
                out_ref[z, rows_of(g), lanes] += jnp.where(group == quarter, turned, 0.0)


def kernel_tables(psf_taps, psf_index, slab):
    normed = psf_taps / jnp.sum(psf_taps, axis=2, keepdims=True)
    index = lax.dynamic_slice_in_dim(jnp.pad(psf_index, (R, R)), slab * SZ, SPAN, 0)
    plane = slab * SZ - R + jnp.arange(SPAN, dtype=jnp.int32)
    valid = (plane >= 0) & (plane < NZ)
    picked = (index[:, None] == jnp.arange(MODELS, dtype=jnp.int32)[None, :]) & valid[:, None]
    kernels = jnp.sum(jnp.where(picked[:, :, None, None], normed[None], 0.0), axis=1)
    own = kernels[R : R + SZ]
    forward = jnp.pad(own[:, 0], ((0, 0), (0, SZ))).reshape(-1)[: SZ * SPAN].reshape(SZ, SPAN)
    forward = jnp.where(valid[None, :], forward, 0.0)
    wide = SPAN + TAPS - 1
    skewed = jnp.pad(kernels[:, 0], ((0, 0), (0, SPAN))).reshape(-1)[: SPAN * wide]
    adjoint = skewed.reshape(SPAN, wide)[:, TAPS - 1 : TAPS - 1 + SZ]
    table = jnp.concatenate(
        [forward.reshape(-1), adjoint.reshape(-1), own[:, 1].reshape(-1), own[:, 2].reshape(-1)]
    )
    across = jnp.pad(kernels[:, 2], ((0, 2), (0, 1)))
    along = jnp.pad(kernels[:, 1].T, ((0, 1), (0, 128 - SPAN)))
    weight = jnp.pad(adjoint.T, ((0, 0), (0, 128 - SPAN)))
    return table, across, along, weight


def body(observed, psf_taps, psf_index, tissue, w_first, b_first, w_mid, b_mid, w_last, b_last):
    slabs = NZ // SZ
    first_pairs = [(i, i ^ 1) for i in range(slabs)]
    second_pairs = [(i, ((((i + 1) % slabs) ^ 1) - 1) % slabs) for i in range(slabs)]
    swap = [(0, 1), (1, 0)]
    volume = shape((SZ, SY, NX), F32)
    planes = shape((R, SY, NX), BF16)

    def beside(first, second):
        return lax.ppermute(first, "gz", first_pairs), lax.ppermute(second, "gz", second_pairs)

    first, second, edge = call(
        prepare_kernel, [planes, planes, shape((SZ, HALO, NX), F32)], [observed], [VMEM]
    )
    first, second = beside(first, second)
    observed_edge = lax.ppermute(edge, "gy", swap)

    table, across, along, weight = kernel_tables(psf_taps, psf_index, lax.axis_index("gz"))
    rows_f, rows_a, cols_f, cols_a, inverse = call(
        setup_kernel,
        [
            shape((SZ, EXT, 256), BF16),
            shape((SZ, SY, 256), BF16),
            shape((SZ, 256, 256), BF16),
            shape((SZ, 256, 256), BF16),
            volume,
        ],
        [table, across, along, weight],
        [SMEM, VMEM, VMEM, VMEM],
        flops=100_000_000,
    )

    estimate = observed
    for turn in range(2):
        u, u_edge = call(
            forward_planes_kernel,
            [volume, shape((SZ, HALO, NX), BF16)],
            [table, estimate, first, second],
            [SMEM, VMEM, VMEM, VMEM],
            flops=30 * SZ * SY * NX,
        )
        u_edge = lax.ppermute(u_edge, "gy", swap)
        q, first, second = call(
            ratio_kernel,
            [volume, planes, planes],
            [u, u_edge, observed, observed_edge, rows_f, rows_a, cols_f, cols_a],
            [VMEM] * 8,
            flops=1_000_000_000,
        )
        first, second = beside(first, second)
        ins = [table, q, first, second, estimate, inverse]
        specs = [SMEM] + [VMEM] * 5
        if turn == 0:
            estimate, first, second = call(
                update_kernel, [volume, planes, planes], ins, specs, flops=30 * SZ * SY * NX
            )
            first, second = beside(first, second)
        else:
            estimate, moments = call(
                last_update_kernel,
                [volume, shape((DEVICES, 128), F32)],
                ins,
                specs,
                flops=30 * SZ * SY * NX,
            )
    moments = lax.all_to_all(moments, ("gz", "gy"), 0, 0, tiled=True)

    w1 = jnp.pad(w_first, ((0, 0), (0, CH - 27)))
    w2 = w_mid.reshape(3, 9, CH, CH).transpose(0, 2, 1, 3).reshape(3 * CH, 9 * CH)
    (restored,) = call(
        bricks_kernel,
        [volume],
        [
            tissue.reshape(-1), estimate, moments, w1, b_first[:, None], w2, b_mid[:, None],
            w_last.astype(F32)[:, None], b_last[:, None],
        ],
        [SMEM] + [VMEM] * 8,
        scratch=[
            pltpu.SMEM((64,), jnp.int32),
            pltpu.VMEM((SZ * 256, 128), F32),
            pltpu.VMEM((SZ, 10, 3 * CH, 128), BF16),
            pltpu.VMEM((SZ, 3 * CH, 256), F32),
            pltpu.VMEM((SZ, 8, 128), F32),
        ],
        flops=1_000_000_000,
    )
    return restored


def solution(mesh):
    return jax.shard_map(
        body,
        mesh=mesh,
        in_specs=(P("gz", "gy", None), P(), P(), P("gz", "gy", None), P(), P(), P(), P(), P(), P()),
        out_specs=P("gz", "gy", None),
        check_vma=False,
    )
```

time: 511 us -> 152 us (0.30)
  the two profiles are of different devices: /device:TPU:1 before, /device:TPU:3 now
where the time goes in v1:
time: 152 us
  Pallas kernels  56.7 us (37%)
  waiting for transfers between devices  46.6 us (31%)
  starting transfers between devices  39.9 us (26%)
  local copies, waits for them, and re-layouts  7.54 us (5%)
    pallas_call x9, Pallas kernels, call(): pl.pallas_call(kernel, out_shape=outs, in_specs=specs, out_specs=[VMEM] *...  56.7 us
    ppermute x4, waiting for transfers between devices, beside(): lax.ppermute(second, 'gz', second_pairs)  25.1 us
    ppermute x4, starting transfers between devices, beside(): lax.ppermute(second, 'gz', second_pairs)  18.9 us
    ppermute x4, waiting for transfers between devices, beside(): lax.ppermute(first, 'gz', first_pairs)  15.2 us
    all_to_all x1, starting transfers between devices, body(): moments = lax.all_to_all(moments, ('gz', 'gy'), 0, 0, tiled=True)  14.1 us
    all_to_all x1, waiting for transfers between devices, body(): moments = lax.all_to_all(moments, ('gz', 'gy'), 0, 0, tiled=True)  5.31 us
    unnamed x27, local copies, waits for them, and re-layouts  4.91 us
    ppermute x2, starting transfers between devices, body(): u_edge = lax.ppermute(u_edge, 'gy', swap)  3.79 us
  transfers between devices with their start and end apart: 12, of which 10 were waited for; matrix products, arithmetic and copies ran while one was open for 2% of the time, Pallas kernels for 5%

profile of v1, /device:TPU:3, one launch (start us, length us, event | category | flops | bytes accessed | tf_op | source)
XLA Modules:
  0.0 152.0 jit_solution(15138187191430143670)
XLA Ops:
  0.0 1.2 copy-done
  1.2 0.1 shard_map.100
  1.4 1.7 %collective-permute-start = (bf16[7,64,512]{2,1,0:T(8,128)(2,1)S(1)}, bf16[7,64,512]{2,1,0:T(8,128)(2,1)S(1)}, u32[]{:S(2)}, u32[]{:S(2)}) collective-permute-start(bf16[7,64,512]{2,1,0:T(8,128)(2,1)S(1)} %get-tuple-element.28), channel_id=1, source_target_pairs={{0,2},{2,0},{4,6},{6,4},{8,10},{10,8},{12,14},{14,12},{16,18},{18,... | collective-permute-start | bytes 1376264 | tf_op jit(solution)/shard_map/ppermute | solution.py:401
  3.1 4.7 %collective-permute-start.1 = (bf16[7,64,512]{2,1,0:T(8,128)(2,1)S(1)}, bf16[7,64,512]{2,1,0:T(8,128)(2,1)S(1)}, u32[]{:S(2)}, u32[]{:S(2)}) collective-permute-start(bf16[7,64,512]{2,1,0:T(8,128)(2,1)S(1)} %get-tuple-element.29), channel_id=1, source_target_pairs={{0,126},{2,4},{4,2},{6,8},{8,6},{10,12},{12,10},{14,16},{16,14},{1... | collective-permute-start | bytes 1376264 | tf_op jit(solution)/shard_map/ppermute | solution.py:401
  7.8 1.2 collective-permute-start.3
  9.0 0.1 reduce_sum.18
  9.2 0.1 copy.47
  9.3 0.7 copy-done.7
  10.0 0.1 select_reduce_fusion
  10.5 0.6 slice_bitcast_fusion
  11.1 0.1 copy.63
  11.2 0.1 reshape.80
  11.3 0.1 reshape.81
  11.5 0.1 reshape.82
  12.0 1.2 collective-permute-done.first_ref
  13.2 5.2 %collective-permute-done.1.second_ref = bf16[7,64,512]{2,1,0:T(8,128)(2,1)S(1)} collective-permute-done((bf16[7,64,512]{2,1,0:T(8,128)(2,1)S(1)}, bf16[7,64,512]{2,1,0:T(8,128)(2,1)S(1)}, u32[]{:S(2)}, u32[]{:S(2)}) %collective-permute-start.1) | collective-permute-done | bytes 458784 | tf_op jit(solution)/shard_map/ppermute | solution.py:401
  18.4 2.5 %shard_map.101 = (f32[8,64,512]{2,1,0:T(8,128)S(1)}, bf16[8,16,512]{2,1,0:T(8,128)(2,1)}) custom-call(f32[592]{0:T(1024)S(1)} %pad_maximum_fusion.table_ref, f32[8,64,512]{2,1,0:T(8,128)S(1)} %copy-done.1, bf16[7,64,512]{2,1,0:T(8,128)(2,1)S(1)} %collective-permute-done.first_ref, bf16[7,64,512]{2,1,0:T(8,128)(2,1)S(1)} %collective-permute-done.1.second_ref), custom_call_target="tpu_custom_call" | custom-call | flops 7864320 | bytes 3148096 | tf_op jit(solution)/shard_map/pallas_call | solution.py:38
  20.9 1.9 %collective-permute-start.2 = (bf16[8,16,512]{2,1,0:T(8,128)(2,1)}, bf16[8,16,512]{2,1,0:T(8,128)(2,1)S(1)}, u32[]{:S(2)}, u32[]{:S(2)}) collective-permute-start(bf16[8,16,512]{2,1,0:T(8,128)(2,1)} %get-tuple-element.31), channel_id=1, source_target_pairs={{0,1},{1,0},{2,3},{3,2},{4,5},{5,4},{6,7},{7,6},{8,9},{9,8},{10,11... | collective-permute-start | bytes 393224 | tf_op jit(solution)/shard_map/ppermute | solution.py:433
  22.8 0.7 copy-done.5
  23.5 0.1 copy.62
  23.6 0.7 copy-done.4
  24.3 5.1 %shard_map.102 = (bf16[8,80,256]{2,1,0:T(8,128)(2,1)S(1)}, bf16[8,64,256]{2,1,0:T(8,128)(2,1)S(1)}, bf16[8,256,256]{2,1,0:T(8,128)(2,1)S(1)}, bf16[8,256,256]{2,1,0:T(8,128)(2,1)S(1)}, f32[8,64,512]{2,1,0:T(8,128)S(1)}) custom-call(f32[592]{0:T(1024)S(1)} %pad_maximum_fusion.table_ref, f32[24,16]{1,0:T(8,128)S(1)} %pad.31.kx_ref, ...), custom_call_target="tpu_custom_call" | custom-call | flops 100000000 | bytes 3751744 | tf_op jit(solution)/shard_map/pallas_call | solution.py:38
  29.4 6.0 %shard_map.103 = (f32[8,64,512]{2,1,0:T(8,128)S(1)}, bf16[7,64,512]{2,1,0:T(8,128)(2,1)S(1)}, bf16[7,64,512]{2,1,0:T(8,128)(2,1)S(1)}) custom-call(f32[8,64,512]{2,1,0:T(8,128)S(1)} %get-tuple-element.30.u_ref, bf16[8,16,512]{2,1,0:T(8,128)(2,1)S(1)} %collective-permute-done.2.u_edge_ref, f32[8,64,512]{2,1,0:T(8,128)S(1)} %copy-done.1, ...), custom_call_target="tpu_custom_call" | custom-call | flops 1000000000 | bytes 7143424 | tf_op jit(solution)/shard_map/pallas_call | solution.py:38
  35.5 4.7 %collective-permute-start.5 = (bf16[7,64,512]{2,1,0:T(8,128)(2,1)S(1)}, bf16[7,64,512]{2,1,0:T(8,128)(2,1)S(1)}, u32[]{:S(2)}, u32[]{:S(2)}) collective-permute-start(bf16[7,64,512]{2,1,0:T(8,128)(2,1)S(1)} %get-tuple-element.39), channel_id=1, source_target_pairs={{0,126},{2,4},{4,2},{6,8},{8,6},{10,12},{12,10},{14,16},{16,14},{1... | collective-permute-start | bytes 1376264 | tf_op jit(solution)/shard_map/ppermute | solution.py:401
  40.3 7.4 %collective-permute-done.4.first_ref = bf16[7,64,512]{2,1,0:T(8,128)(2,1)S(1)} collective-permute-done((bf16[7,64,512]{2,1,0:T(8,128)(2,1)S(1)}, bf16[7,64,512]{2,1,0:T(8,128)(2,1)S(1)}, u32[]{:S(2)}, u32[]{:S(2)}) %collective-permute-start.4) | collective-permute-done | bytes 458784 | tf_op jit(solution)/shard_map/ppermute | solution.py:401
  47.7 4.3 %collective-permute-done.5.second_ref = bf16[7,64,512]{2,1,0:T(8,128)(2,1)S(1)} collective-permute-done((bf16[7,64,512]{2,1,0:T(8,128)(2,1)S(1)}, bf16[7,64,512]{2,1,0:T(8,128)(2,1)S(1)}, u32[]{:S(2)}, u32[]{:S(2)}) %collective-permute-start.5) | collective-permute-done | bytes 458784 | tf_op jit(solution)/shard_map/ppermute | solution.py:401
  52.0 2.1 %shard_map.104 = (f32[8,64,512]{2,1,0:T(8,128)S(1)}, bf16[7,64,512]{2,1,0:T(8,128)(2,1)S(1)}, bf16[7,64,512]{2,1,0:T(8,128)(2,1)S(1)}) custom-call(f32[592]{0:T(1024)S(1)} %pad_maximum_fusion.table_ref, f32[8,64,512]{2,1,0:T(8,128)S(1)} %get-tuple-element.37.own_ref, bf16[7,64,512]{2,1,0:T(8,128)(2,1)S(1)} %collective-permute-done.4.first_ref, ...), custom_call_target="tpu_custom_call" | custom-call | flops 7864320 | bytes 6031680 | tf_op jit(solution)/shard_map/pallas_call | solution.py:38
  54.1 4.7 %collective-permute-start.7 = (bf16[7,64,512]{2,1,0:T(8,128)(2,1)S(1)}, bf16[7,64,512]{2,1,0:T(8,128)(2,1)S(1)}, u32[]{:S(2)}, u32[]{:S(2)}) collective-permute-start(bf16[7,64,512]{2,1,0:T(8,128)(2,1)S(1)} %get-tuple-element.43), channel_id=1, source_target_pairs={{0,126},{2,4},{4,2},{6,8},{8,6},{10,12},{12,10},{14,16},{16,14},{1... | collective-permute-start | bytes 1376264 | tf_op jit(solution)/shard_map/ppermute | solution.py:401
  58.9 6.5 %collective-permute-done.6.first_ref = bf16[7,64,512]{2,1,0:T(8,128)(2,1)S(1)} collective-permute-done((bf16[7,64,512]{2,1,0:T(8,128)(2,1)S(1)}, bf16[7,64,512]{2,1,0:T(8,128)(2,1)S(1)}, u32[]{:S(2)}, u32[]{:S(2)}) %collective-permute-start.6) | collective-permute-done | bytes 458784 | tf_op jit(solution)/shard_map/ppermute | solution.py:401
  65.4 4.3 %collective-permute-done.7.second_ref = bf16[7,64,512]{2,1,0:T(8,128)(2,1)S(1)} collective-permute-done((bf16[7,64,512]{2,1,0:T(8,128)(2,1)S(1)}, bf16[7,64,512]{2,1,0:T(8,128)(2,1)S(1)}, u32[]{:S(2)}, u32[]{:S(2)}) %collective-permute-start.7) | collective-permute-done | bytes 458784 | tf_op jit(solution)/shard_map/ppermute | solution.py:401
  69.7 1.8 %shard_map.105 = (f32[8,64,512]{2,1,0:T(8,128)S(1)}, bf16[8,16,512]{2,1,0:T(8,128)(2,1)S(1)}) custom-call(f32[592]{0:T(1024)S(1)} %pad_maximum_fusion.table_ref, f32[8,64,512]{2,1,0:T(8,128)S(1)} %get-tuple-element.41.own_ref.before_ref, bf16[7,64,512]{2,1,0:T(8,128)(2,1)S(1)} %collective-permute-done.6.first_ref, ...), custom_call_target="tpu_custom_call" | custom-call | flops 7864320 | bytes 3148096 | tf_op jit(solution)/shard_map/pallas_call | solution.py:38
  71.5 1.9 %collective-permute-start.8 = (bf16[8,16,512]{2,1,0:T(8,128)(2,1)S(1)}, bf16[8,16,512]{2,1,0:T(8,128)(2,1)S(1)}, u32[]{:S(2)}, u32[]{:S(2)}) collective-permute-start(bf16[8,16,512]{2,1,0:T(8,128)(2,1)S(1)} %get-tuple-element.45), channel_id=1, source_target_pairs={{0,1},{1,0},{2,3},{3,2},{4,5},{5,4},{6,7},{7,6},{8,9},{9,8},{10,11... | collective-permute-start | bytes 393224 | tf_op jit(solution)/shard_map/ppermute | solution.py:433
  73.5 1.0 collective-permute-done.8.u_edge_ref
  74.5 6.0 %shard_map.106 = (f32[8,64,512]{2,1,0:T(8,128)S(1)}, bf16[7,64,512]{2,1,0:T(8,128)(2,1)S(1)}, bf16[7,64,512]{2,1,0:T(8,128)(2,1)S(1)}) custom-call(f32[8,64,512]{2,1,0:T(8,128)S(1)} %get-tuple-element.44.u_ref, bf16[8,16,512]{2,1,0:T(8,128)(2,1)S(1)} %collective-permute-done.8.u_edge_ref, f32[8,64,512]{2,1,0:T(8,128)S(1)} %copy-done.1, ...), custom_call_target="tpu_custom_call" | custom-call | flops 1000000000 | bytes 7143424 | tf_op jit(solution)/shard_map/pallas_call | solution.py:38
  80.5 4.7 %collective-permute-start.10 = (bf16[7,64,512]{2,1,0:T(8,128)(2,1)S(1)}, bf16[7,64,512]{2,1,0:T(8,128)(2,1)S(1)}, u32[]{:S(2)}, u32[]{:S(2)}) collective-permute-start(bf16[7,64,512]{2,1,0:T(8,128)(2,1)S(1)} %get-tuple-element.48), channel_id=1, source_target_pairs={{0,126},{2,4},{4,2},{6,8},{8,6},{10,12},{12,10},{14,16},{16,14},{1... | collective-permute-start | bytes 1376264 | tf_op jit(solution)/shard_map/ppermute | solution.py:401
  85.2 11.3 %collective-permute-done.10.second_ref = bf16[7,64,512]{2,1,0:T(8,128)(2,1)S(1)} collective-permute-done((bf16[7,64,512]{2,1,0:T(8,128)(2,1)S(1)}, bf16[7,64,512]{2,1,0:T(8,128)(2,1)S(1)}, u32[]{:S(2)}, u32[]{:S(2)}) %collective-permute-start.10) | collective-permute-done | bytes 458784 | tf_op jit(solution)/shard_map/ppermute | solution.py:401
  96.5 0.1 collective-permute-done.9.first_ref
  96.6 2.9 %shard_map.107 = (f32[8,64,512]{2,1,0:T(8,128)S(1)}, f32[128,128]{1,0:T(8,128)}) custom-call(f32[592]{0:T(1024)S(1)} %pad_maximum_fusion.table_ref, f32[8,64,512]{2,1,0:T(8,128)S(1)} %get-tuple-element.46.own_ref, bf16[7,64,512]{2,1,0:T(8,128)(2,1)S(1)} %collective-permute-done.9.first_ref, bf16[7,64,512]{2,1,0:T(8,128)(2,1)S(1)} %collective-permute-done.10.second_ref, ...), custom_call_target="tpu_custom_call" | custom-call | flops 7864320 | bytes 5179712 | tf_op jit(solution)/shard_map/pallas_call | solution.py:38
  99.5 14.1 %all-to-all-start = ((f32[128,1,128]{2,1,0:T(1,128)}), f32[128,1,128]{2,1,0:T(1,128)S(1)}, u32[]{:S(2)}, u32[]{:S(2)}) async-start(f32[128,1,128]{2,1,0:T(1,128)} %bitcast.7), calls=%async_computation | async-start | bytes 131072 | tf_op jit(solution)/shard_map/all_to_all | solution.py:457
  113.6 0.2 copy.56
  113.9 0.2 reshape.84
  114.0 0.1 copy.58.w2_ref
  114.1 0.1 copy.60.w3_ref
  114.2 0.7 copy-done.8
  114.9 0.1 copy.57.b1_ref
  115.0 0.7 copy-done.9
  116.5 5.3 %all-to-all-done = f32[128,1,128]{2,1,0:T(1,128)S(1)} async-done(((f32[128,1,128]{2,1,0:T(1,128)}), f32[128,1,128]{2,1,0:T(1,128)S(1)}, u32[]{:S(2)}, u32[]{:S(2)}) %all-to-all-start) | async-done | bytes 65568 | tf_op jit(solution)/shard_map/all_to_all | solution.py:457
  121.8 30.2 %shard_map.108 = f32[8,64,512]{2,1,0:T(8,128)} custom-call(s32[32]{0:T(128)S(1)} %reshape.78.tissue_ref, f32[8,64,512]{2,1,0:T(8,128)S(1)} %get-tuple-element.49.estimate_ref, f32[128,128]{1,0:T(8,128)S(1)} %bitcast.29, bf16[32,32]{1,0:T(8,128)(2,1)S(1)} %pad.34.w1_ref, f32[32,1]{1,0:T(8,128)S(1)} %copy.57.b1_ref, bf16[96,288]{1,0:T(8,128)(2,1)S(1)} %copy.58.w2_ref, ...), custom_call_target="tpu_custom_call" | custom-call | flops 1000000000 | bytes 2220548 | tf_op jit(solution)/shard_map/pallas_call | solution.py:38
  (49 shorter events, 1.5 us)
Async XLA Ops:
  0.0 1.2 copy-start
  1.2 17.2 %copy-start.1 = (f32[8,64,512]{2,1,0:T(8,128)S(1)}, f32[8,64,512]{2,1,0:T(8,128)}, u32[]{:S(2)}) copy-start(f32[8,64,512]{2,1,0:T(8,128)} %observed_ref.5) | copy-start | bytes 3145732
  1.4 7.6 %copy-start.3 = (f32[8,3,15]{2,0,1:T(8,128)S(1)}, f32[8,3,15]{2,0,1:T(8,128)}, u32[]{:S(2)}) copy-start(f32[8,3,15]{2,0,1:T(8,128)} %param.11) | copy-start | bytes 4324
  1.4 11.8 %collective-permute-start = (bf16[7,64,512]{2,1,0:T(8,128)(2,1)S(1)}, bf16[7,64,512]{2,1,0:T(8,128)(2,1)S(1)}, u32[]{:S(2)}, u32[]{:S(2)}) collective-permute-start(bf16[7,64,512]{2,1,0:T(8,128)(2,1)S(1)} %get-tuple-element.28), channel_id=1, source_target_pairs={{0,2},{2,0},{4,6},{6,4},{8,10},{10,8},{12,14},{14,12},{16,18},{18,... | collective-permute-start | bytes 1376264 | tf_op jit(solution)/shard_map/ppermute | solution.py:401
  3.1 15.3 %collective-permute-start.1 = (bf16[7,64,512]{2,1,0:T(8,128)(2,1)S(1)}, bf16[7,64,512]{2,1,0:T(8,128)(2,1)S(1)}, u32[]{:S(2)}, u32[]{:S(2)}) collective-permute-start(bf16[7,64,512]{2,1,0:T(8,128)(2,1)S(1)} %get-tuple-element.29), channel_id=1, source_target_pairs={{0,126},{2,4},{4,2},{6,8},{8,6},{10,12},{12,10},{14,16},{16,14},{1... | collective-permute-start | bytes 1376264 | tf_op jit(solution)/shard_map/ppermute | solution.py:401
  7.8 21.6 %collective-permute-start.3 = (f32[8,16,512]{2,1,0:T(8,128)S(1)}, f32[8,16,512]{2,1,0:T(8,128)S(1)}, u32[]{:S(2)}, u32[]{:S(2)}) collective-permute-start(f32[8,16,512]{2,1,0:T(8,128)S(1)} %get-tuple-element.32), channel_id=1, source_target_pairs={{0,1},{1,0},{2,3},{3,2},{4,5},{5,4},{6,7},{7,6},{8,9},{9,8},{10,11... | collective-permute-start | bytes 786440 | tf_op jit(solution)/shard_map/ppermute | solution.py:407
  9.3 0.7 copy-start.7
  20.9 8.6 %collective-permute-start.2 = (bf16[8,16,512]{2,1,0:T(8,128)(2,1)}, bf16[8,16,512]{2,1,0:T(8,128)(2,1)S(1)}, u32[]{:S(2)}, u32[]{:S(2)}) collective-permute-start(bf16[8,16,512]{2,1,0:T(8,128)(2,1)} %get-tuple-element.31), channel_id=1, source_target_pairs={{0,1},{1,0},{2,3},{3,2},{4,5},{5,4},{6,7},{7,6},{8,9},{9,8},{10,11... | collective-permute-start | bytes 393224 | tf_op jit(solution)/shard_map/ppermute | solution.py:433
  22.8 0.7 copy-start.5
  23.6 0.7 copy-start.4
  35.4 12.2 %collective-permute-start.4 = (bf16[7,64,512]{2,1,0:T(8,128)(2,1)S(1)}, bf16[7,64,512]{2,1,0:T(8,128)(2,1)S(1)}, u32[]{:S(2)}, u32[]{:S(2)}) collective-permute-start(bf16[7,64,512]{2,1,0:T(8,128)(2,1)S(1)} %get-tuple-element.38), channel_id=1, source_target_pairs={{0,2},{2,0},{4,6},{6,4},{8,10},{10,8},{12,14},{14,12},{16,18},{18,... | collective-permute-start | bytes 1376264 | tf_op jit(solution)/shard_map/ppermute | solution.py:401
  35.5 16.5 %collective-permute-start.5 = (bf16[7,64,512]{2,1,0:T(8,128)(2,1)S(1)}, bf16[7,64,512]{2,1,0:T(8,128)(2,1)S(1)}, u32[]{:S(2)}, u32[]{:S(2)}) collective-permute-start(bf16[7,64,512]{2,1,0:T(8,128)(2,1)S(1)} %get-tuple-element.39), channel_id=1, source_target_pairs={{0,126},{2,4},{4,2},{6,8},{8,6},{10,12},{12,10},{14,16},{16,14},{1... | collective-permute-start | bytes 1376264 | tf_op jit(solution)/shard_map/ppermute | solution.py:401
  54.0 11.3 %collective-permute-start.6 = (bf16[7,64,512]{2,1,0:T(8,128)(2,1)S(1)}, bf16[7,64,512]{2,1,0:T(8,128)(2,1)S(1)}, u32[]{:S(2)}, u32[]{:S(2)}) collective-permute-start(bf16[7,64,512]{2,1,0:T(8,128)(2,1)S(1)} %get-tuple-element.42), channel_id=1, source_target_pairs={{0,2},{2,0},{4,6},{6,4},{8,10},{10,8},{12,14},{14,12},{16,18},{18,... | collective-permute-start | bytes 1376264 | tf_op jit(solution)/shard_map/ppermute | solution.py:401
  54.1 15.6 %collective-permute-start.7 = (bf16[7,64,512]{2,1,0:T(8,128)(2,1)S(1)}, bf16[7,64,512]{2,1,0:T(8,128)(2,1)S(1)}, u32[]{:S(2)}, u32[]{:S(2)}) collective-permute-start(bf16[7,64,512]{2,1,0:T(8,128)(2,1)S(1)} %get-tuple-element.43), channel_id=1, source_target_pairs={{0,126},{2,4},{4,2},{6,8},{8,6},{10,12},{12,10},{14,16},{16,14},{1... | collective-permute-start | bytes 1376264 | tf_op jit(solution)/shard_map/ppermute | solution.py:401
  71.5 2.9 %collective-permute-start.8 = (bf16[8,16,512]{2,1,0:T(8,128)(2,1)S(1)}, bf16[8,16,512]{2,1,0:T(8,128)(2,1)S(1)}, u32[]{:S(2)}, u32[]{:S(2)}) collective-permute-start(bf16[8,16,512]{2,1,0:T(8,128)(2,1)S(1)} %get-tuple-element.45), channel_id=1, source_target_pairs={{0,1},{1,0},{2,3},{3,2},{4,5},{5,4},{6,7},{7,6},{8,9},{9,8},{10,11... | collective-permute-start | bytes 393224 | tf_op jit(solution)/shard_map/ppermute | solution.py:433
  80.5 16.0 %collective-permute-start.10 = (bf16[7,64,512]{2,1,0:T(8,128)(2,1)S(1)}, bf16[7,64,512]{2,1,0:T(8,128)(2,1)S(1)}, u32[]{:S(2)}, u32[]{:S(2)}) collective-permute-start(bf16[7,64,512]{2,1,0:T(8,128)(2,1)S(1)} %get-tuple-element.48), channel_id=1, source_target_pairs={{0,126},{2,4},{4,2},{6,8},{8,6},{10,12},{12,10},{14,16},{16,14},{1... | collective-permute-start | bytes 1376264 | tf_op jit(solution)/shard_map/ppermute | solution.py:401
  85.2 11.4 %collective-permute-start.9 = (bf16[7,64,512]{2,1,0:T(8,128)(2,1)S(1)}, bf16[7,64,512]{2,1,0:T(8,128)(2,1)S(1)}, u32[]{:S(2)}, u32[]{:S(2)}) collective-permute-start(bf16[7,64,512]{2,1,0:T(8,128)(2,1)S(1)} %get-tuple-element.47), channel_id=1, source_target_pairs={{0,2},{2,0},{4,6},{6,4},{8,10},{10,8},{12,14},{14,12},{16,18},{18,... | collective-permute-start | bytes 1376264 | tf_op jit(solution)/shard_map/ppermute | solution.py:401
  96.6 17.0 %copy-start.2 = (bf16[27,32,32]{2,1,0:T(8,128)(2,1)S(1)}, bf16[27,32,32]{2,1,0:T(8,128)(2,1)}, u32[]{:S(2)}) copy-start(bf16[27,32,32]{2,1,0:T(8,128)(2,1)} %param.16) | copy-start | bytes 165892
  99.5 14.1 %copy-start.11 = (bf16[32]{0:T(256)(128)(2,1)S(1)}, bf16[32]{0:T(256)(128)(2,1)}, u32[]{:S(2)}) copy-start(bf16[32]{0:T(256)(128)(2,1)} %param.18) | copy-start | bytes 196
  99.5 22.3 %all-to-all-start = ((f32[128,1,128]{2,1,0:T(1,128)}), f32[128,1,128]{2,1,0:T(1,128)S(1)}, u32[]{:S(2)}, u32[]{:S(2)}) async-start(f32[128,1,128]{2,1,0:T(1,128)} %bitcast.7), calls=%async_computation | async-start | bytes 131072 | tf_op jit(solution)/shard_map/all_to_all | solution.py:457
  114.2 0.7 copy-start.8
  115.0 0.7 copy-start.9
  115.6 0.9 copy-start.6
  115.7 0.7 copy-start.10

commit v2 on v1

--- a/solution.py
+++ b/solution.py
@@ -15,6 +15,9 @@
 MODELS = 8
 BY, BX = 32, 32
 CH = 32
+ACROSS = NX // BX
+BRICKS = (SY // BY) * ACROSS
+MOST = 3
 SPAN = SZ + 2 * R
 COUNT = float(NZ * NY * NX)
 LOCAL = float(SZ * SY * NX)
@@ -163,7 +166,10 @@
         run(first_ref, second_ref)
 
 
-def forward_planes_kernel(table_ref, own_ref, first_ref, second_ref, out_ref, edge_ref):
+def forward_planes_kernel(
+    table_ref, own_ref, first_ref, second_ref, inverse_ref, out_ref, edge_ref
+):
+    del inverse_ref
     def emit(z, rows, lanes, value):
         out_ref[z, rows, lanes] = value
 
@@ -245,84 +251,122 @@
     send_planes(out_ref, to_first_ref, to_second_ref)
 
 
+def beside(value, at):
+    return (
+        jnp.where(at == 0, 0.0, pltpu.roll(value, 1, axis=1)),
+        value,
+        jnp.where(at == BX - 1, 0.0, pltpu.roll(value, 127, axis=1)),
+    )
+
+
+def note_bricks(tissue_ref, listing):
+    def note(b, count):
+        listing[count] = b
+        return count + jnp.where(tissue_ref[b] > 0, 1, 0)
+
+    return lax.fori_loop(0, BRICKS, note, 0)
+
+
+def place_of(brick):
+    down = brick // ACROSS
+    over = brick % ACROSS
+
+    def rows_of(g):
+        return pl.ds(pl.multiple_of(down * BY + 8 * g, 8), 8)
+
+    return rows_of, pl.ds(pl.multiple_of(over // 4 * 128, 128), 128), over % 4
+
+
+def first_kernel(tissue_ref, estimate_ref, mean_ref, w1_ref, raw_ref, ones_ref, listing, stack):
+    many = note_bricks(tissue_ref, listing)
+    mean = mean_ref[0:1, 0:1]
+    stack[...] = jnp.zeros(stack.shape, F32)
+    lane = iota((8, 128), 1)
+    row = iota((8, 128), 0)
+    group = lane // BX
+    column = lane % BX
+
+    def fill(z, plane):
+        before = pltpu.roll(plane, 1, axis=0)
+        after = pltpu.roll(plane, 7, axis=0)
+        wrapped_before = jnp.where(group == 0, 0.0, pltpu.roll(before, BX, axis=1))
+        wrapped_after = jnp.where(group == 3, 0.0, pltpu.roll(after, 128 - BX, axis=1))
+        versions = (
+            jnp.where(row == 0, wrapped_before, before),
+            plane,
+            jnp.where(row == 7, wrapped_after, after),
+        )
+        for b, version in enumerate(versions):
+            for c, moved in enumerate(beside(version, column)):
+                for a in range(3):
+                    to = z - (a - 1)
+                    if 0 <= to < SZ:
+                        tap = 9 * a + 3 * b + c
+                        stack[pl.ds(to * 256 + tap, 8, stride=32), :] = moved
+
+    def convolve(store):
+        for z in range(SZ):
+            for pair in range(4):
+                at = z * 256 + 2 * pair * 32
+                taps = [stack[at + 32 * e : at + 32 * (e + 1), :].astype(BF16) for e in range(2)]
+                store(
+                    z,
+                    pair,
+                    jnp.dot(
+                        w1_ref[...], jnp.concatenate(taps, axis=1), preferred_element_type=F32
+                    ),
+                )
+
+    for z in range(SZ):
+        fill(z, jnp.ones((8, 128), F32))
+
+    def keep_ones(z, pair, value):
+        ones_ref[z, pair] = value
+
+    convolve(keep_ones)
+
+    @pl.loop(0, many)
+    def _(n):
+        rows_of, lanes, quarter = place_of(listing[n])
+        for z in range(SZ):
+            plane = jnp.zeros((8, 128), F32)
+            for g in range(4):
+                block = estimate_ref[z, rows_of(g), lanes]
+                turned = pltpu.roll(block, (BX * (g - quarter)) % 128, axis=1)
+                plane = jnp.where(group == g, turned, plane)
+            fill(z, plane - mean)
+
+        def keep(z, pair, value):
+            raw_ref[n, z, pair] = value
+
+        convolve(keep)
+
+
 def bricks_kernel(
-    tissue_ref, estimate_ref, moments_ref, w1_ref, b1_ref, w2_ref, b2_ref, w3_ref, b3_ref,
-    out_ref, listing, stack, hidden, partial, result,
+    tissue_ref, estimate_ref, mean_ref, moments_ref, raw_ref, ones_ref,
+    b1_ref, w2_ref, b2_ref, w3_ref, b3_ref,
+    out_ref, listing, hidden, partial, result,
 ):
     means = moments_ref[:, 0:1]
     centre = jnp.sum(means, axis=0, keepdims=True) / DEVICES
     deviation = jnp.sum(moments_ref[:, 1:2] + LOCAL * (means - centre) ** 2, axis=0, keepdims=True)
     spread = jnp.sqrt(deviation / COUNT + 1e-06)
+    scale = 1.0 / spread
+    offset = mean_ref[0:1, 0:1] - centre
     out_ref[...] = estimate_ref[...]
-    stack[...] = jnp.zeros(stack.shape, F32)
-
-    def note(b, count):
-        listing[count] = b
-        return count + jnp.where(tissue_ref[b] > 0, 1, 0)
-
-    bricks_across = NX // BX
-    many = lax.fori_loop(0, (SY // BY) * bricks_across, note, 0)
-
-    lane = iota((8, 128), 1)
-    row = iota((8, 128), 0)
-    group = lane // BX
-    column = lane % BX
+    many = note_bricks(tissue_ref, listing)
+    group = iota((8, 128), 1) // BX
     tall_column = iota((CH, 128), 1) % BX
     tall_group = iota((CH, 128), 1) // BX
 
-    def beside(value, at):
-        return (
-            jnp.where(at == 0, 0.0, pltpu.roll(value, 1, axis=1)),
-            value,
-            jnp.where(at == BX - 1, 0.0, pltpu.roll(value, 127, axis=1)),
-        )
-
     @pl.loop(0, many)
     def _(n):
-        brick = listing[n]
-        down = brick // bricks_across
-        over = brick % bricks_across
-        lanes = pl.ds(pl.multiple_of(over // 4 * 128, 128), 128)
-        quarter = over % 4
-
-        def rows_of(g):
-            return pl.ds(pl.multiple_of(down * BY + 8 * g, 8), 8)
+        rows_of, lanes, quarter = place_of(listing[n])
 
         for z in range(SZ):
-            brick_plane = jnp.zeros((8, 128), F32)
-            for g in range(4):
-                block = estimate_ref[z, rows_of(g), lanes]
-                turned = pltpu.roll(block, (BX * (g - quarter)) % 128, axis=1)
-                brick_plane = jnp.where(group == g, turned, brick_plane)
-            normed = ((brick_plane - centre) / spread).astype(BF16).astype(F32)
-            before = pltpu.roll(normed, 1, axis=0)
-            after = pltpu.roll(normed, 7, axis=0)
-            wrapped_before = jnp.where(group == 0, 0.0, pltpu.roll(before, BX, axis=1))
-            wrapped_after = jnp.where(group == 3, 0.0, pltpu.roll(after, 128 - BX, axis=1))
-            versions = (
-                jnp.where(row == 0, wrapped_before, before),
-                normed,
-                jnp.where(row == 7, wrapped_after, after),
-            )
-            for b, version in enumerate(versions):
-                for c, moved in enumerate(beside(version, column)):
-                    for a in range(3):
-                        to = z - (a - 1)
-                        if 0 <= to < SZ:
-                            tap = 9 * a + 3 * b + c
-                            stack[pl.ds(to * 256 + tap, 8, stride=32), :] = moved
-
-        @pl.loop(0, SZ)
-        def _(z):
             for pair in range(4):
-                taps = [
-                    stack[pl.ds(pl.multiple_of(z * 256 + (2 * pair + e) * 32, 32), 32), :].astype(BF16)
-                    for e in range(2)
-                ]
-                first = jnp.dot(
-                    w1_ref[...], jnp.concatenate(taps, axis=1), preferred_element_type=F32
-                )
-                first = jnp.maximum(first + b1_ref[...], 0.0)
+                first = (raw_ref[n, z, pair] + offset * ones_ref[z, pair]) * scale + b1_ref[...]
+                first = jnp.maximum(first, 0.0)
                 for e in range(2):
                     r = 2 * pair + e
                     value = first[:, 128 * e : 128 * (e + 1)]
@@ -339,22 +383,22 @@
                         moved = jnp.concatenate(beside(placed, tall_column), axis=0)
                         hidden[z, at] = moved.astype(BF16)
 
-        for pair in range(4):
-            @pl.loop(0, SZ)
-            def _(z):
+        for z in range(SZ):
+            for pair in range(4):
                 taps = [
                     hidden[z, 2 * pair + e : 2 * pair + e + 3].reshape(9 * CH, 128) for e in range(2)
                 ]
-                partial[z] = jnp.dot(
+                partial[z, pair] = jnp.dot(
                     w2_ref[...], jnp.concatenate(taps, axis=1), preferred_element_type=F32
                 )
 
-            for z in range(SZ):
-                total = partial[z, CH : 2 * CH] + b2_ref[...]
+        for z in range(SZ):
+            for pair in range(4):
+                total = partial[z, pair, CH : 2 * CH] + b2_ref[...]
                 if z > 0:
-                    total += partial[z - 1, :CH]
+                    total += partial[z - 1, pair, :CH]
                 if z < SZ - 1:
-                    total += partial[z + 1, 2 * CH :]
+                    total += partial[z + 1, pair, 2 * CH :]
                 second = jnp.maximum(total, 0.0).astype(BF16).astype(F32)
                 last = jnp.sum(w3_ref[...] * second, axis=0, keepdims=True) + b3_ref[...]
                 result[z, 2 * pair : 2 * pair + 1, :] = last[:, :128]
@@ -392,7 +436,7 @@
 def body(observed, psf_taps, psf_index, tissue, w_first, b_first, w_mid, b_mid, w_last, b_last):
     slabs = NZ // SZ
     first_pairs = [(i, i ^ 1) for i in range(slabs)]
-    second_pairs = [(i, ((((i + 1) % slabs) ^ 1) - 1) % slabs) for i in range(slabs)]
+    second_pairs = [(i, ((i + 1) ^ 1) - 1) for i in range(1, slabs - 1)]
     swap = [(0, 1), (1, 0)]
     volume = shape((SZ, SY, NX), F32)
     planes = shape((R, SY, NX), BF16)
@@ -426,8 +470,8 @@
         u, u_edge = call(
             forward_planes_kernel,
             [volume, shape((SZ, HALO, NX), BF16)],
-            [table, estimate, first, second],
-            [SMEM, VMEM, VMEM, VMEM],
+            [table, estimate, first, second, inverse],
+            [SMEM] + [VMEM] * 4,
             flops=30 * SZ * SY * NX,
         )
         u_edge = lax.ppermute(u_edge, "gy", swap)
@@ -447,30 +491,38 @@
             )
             first, second = beside(first, second)
         else:
-            estimate, moments = call(
+            estimate, own_moments = call(
                 last_update_kernel,
                 [volume, shape((DEVICES, 128), F32)],
                 ins,
                 specs,
                 flops=30 * SZ * SY * NX,
             )
-    moments = lax.all_to_all(moments, ("gz", "gy"), 0, 0, tiled=True)
+    moments = lax.all_to_all(own_moments, ("gz", "gy"), 0, 0, tiled=True)
 
     w1 = jnp.pad(w_first, ((0, 0), (0, CH - 27)))
     w2 = w_mid.reshape(3, 9, CH, CH).transpose(0, 2, 1, 3).reshape(3 * CH, 9 * CH)
+    flags = tissue.reshape(-1)
+    raw, ones = call(
+        first_kernel,
+        [shape((MOST, SZ, 4, CH, 256), F32), shape((SZ, 4, CH, 256), F32)],
+        [flags, estimate, own_moments, w1],
+        [SMEM] + [VMEM] * 3,
+        scratch=[pltpu.SMEM((64,), jnp.int32), pltpu.VMEM((SZ * 256, 128), F32)],
+        flops=100_000_000,
+    )
     (restored,) = call(
         bricks_kernel,
         [volume],
         [
-            tissue.reshape(-1), estimate, moments, w1, b_first[:, None], w2, b_mid[:, None],
+            flags, estimate, own_moments, moments, raw, ones, b_first[:, None], w2, b_mid[:, None],
             w_last.astype(F32)[:, None], b_last[:, None],
         ],
-        [SMEM] + [VMEM] * 8,
+        [SMEM] + [VMEM] * 10,
         scratch=[
             pltpu.SMEM((64,), jnp.int32),
-            pltpu.VMEM((SZ * 256, 128), F32),
             pltpu.VMEM((SZ, 10, 3 * CH, 128), BF16),
-            pltpu.VMEM((SZ, 3 * CH, 256), F32),
+            pltpu.VMEM((SZ, 4, 3 * CH, 256), F32),
             pltpu.VMEM((SZ, 8, 128), F32),
         ],
         flops=1_000_000_000,

time: 152 us -> 136 us (0.89)
  the two profiles are of different devices: /device:TPU:3 before, /device:TPU:6 now
where the time goes in v2:
time: 136 us; the launch traced here: 135 us
  Pallas kernels  44.5 us (33%)
  waiting for transfers between devices  39.6 us (29%)
  starting transfers between devices  39.3 us (29%)
  local copies, waits for them, and re-layouts  8.98 us (7%)
  other arithmetic  1.81 us (1%)
    pallas_call x10, Pallas kernels, call(): pl.pallas_call(kernel, out_shape=outs, in_specs=specs, out_specs=[VMEM] *...  44.5 us
    ppermute x4, starting transfers between devices, beside(): lax.ppermute(second, 'gz', second_pairs)  28.7 us
    ppermute x4, waiting for transfers between devices, beside(): lax.ppermute(second, 'gz', second_pairs)  25.4 us
    ppermute x4, waiting for transfers between devices, beside(): lax.ppermute(first, 'gz', first_pairs)  10.8 us
    all_to_all x1, starting transfers between devices, body(): moments = lax.all_to_all(own_moments, ('gz', 'gy'), 0, 0, tiled=True)  7.94 us
    unnamed x25, local copies, waits for them, and re-layouts  6.27 us
  transfers between devices with their start and end apart: 12, of which 10 were waited for; matrix products, arithmetic and copies ran while one was open for 4% of the time, Pallas kernels for 8%

profile of v2, /device:TPU:6, one launch (start us, length us, event | category | flops | bytes accessed | tf_op | source)
XLA Modules:
  0.0 135.2 jit_solution(3739978700553902246)
XLA Ops:
  0.0 1.2 copy-done
  1.2 0.1 shard_map.100
  1.4 2.0 %collective-permute-start = (bf16[7,64,512]{2,1,0:T(8,128)(2,1)S(1)}, bf16[7,64,512]{2,1,0:T(8,128)(2,1)S(1)}, u32[]{:S(2)}, u32[]{:S(2)}) collective-permute-start(bf16[7,64,512]{2,1,0:T(8,128)(2,1)S(1)} %get-tuple-element.30), channel_id=1, source_target_pairs={{0,2},{2,0},{4,6},{6,4},{8,10},{10,8},{12,14},{14,12},{16,18},{18,... | collective-permute-start | bytes 1376264 | tf_op jit(solution)/shard_map/ppermute | solution.py:445
  3.4 7.1 %collective-permute-start.1 = (bf16[7,64,512]{2,1,0:T(8,128)(2,1)S(1)}, bf16[7,64,512]{2,1,0:T(8,128)(2,1)S(1)}, u32[]{:S(2)}, u32[]{:S(2)}) collective-permute-start(bf16[7,64,512]{2,1,0:T(8,128)(2,1)S(1)} %get-tuple-element.31), channel_id=1, source_target_pairs={{2,4},{4,2},{6,8},{8,6},{10,12},{12,10},{14,16},{16,14},{18,20},{2... | collective-permute-start | bytes 1376264 | tf_op jit(solution)/shard_map/ppermute | solution.py:445
  10.6 0.8 reduce_sum.18
  11.4 0.8 broadcast_divide_fusion
  12.2 0.1 copy.47
  12.3 0.8 pad_dynamic-slice_fusion
  13.1 0.1 select_reduce_fusion
  13.5 0.1 copy.63
  13.7 0.1 reshape.80
  13.8 0.1 reshape.81
  13.9 0.1 reshape.82
  14.4 0.1 copy.62
  14.6 5.1 %shard_map.101 = (bf16[8,80,256]{2,1,0:T(8,128)(2,1)S(1)}, bf16[8,64,256]{2,1,0:T(8,128)(2,1)S(1)}, bf16[8,256,256]{2,1,0:T(8,128)(2,1)S(1)}, bf16[8,256,256]{2,1,0:T(8,128)(2,1)S(1)}, f32[8,64,512]{2,1,0:T(8,128)S(1)}) custom-call(f32[592]{0:T(1024)S(1)} %pad_maximum_fusion.table_ref, f32[24,16]{1,0:T(8,128)S(1)} %pad.31.kx_ref, ...), custom_call_target="tpu_custom_call" | custom-call | flops 100000000 | bytes 3751744 | tf_op jit(solution)/shard_map/pallas_call | solution.py:41
  19.7 1.7 %collective-permute-done.1.second_ref = bf16[7,64,512]{2,1,0:T(8,128)(2,1)S(1)} collective-permute-done((bf16[7,64,512]{2,1,0:T(8,128)(2,1)S(1)}, bf16[7,64,512]{2,1,0:T(8,128)(2,1)S(1)}, u32[]{:S(2)}, u32[]{:S(2)}) %collective-permute-start.1) | collective-permute-done | bytes 458784 | tf_op jit(solution)/shard_map/ppermute | solution.py:445
  21.4 1.2 copy-done.1
  22.7 1.8 %shard_map.102 = (f32[8,64,512]{2,1,0:T(8,128)S(1)}, bf16[8,16,512]{2,1,0:T(8,128)(2,1)S(1)}) custom-call(f32[592]{0:T(1024)S(1)} %pad_maximum_fusion.table_ref, f32[8,64,512]{2,1,0:T(8,128)S(1)} %copy-done.1, bf16[7,64,512]{2,1,0:T(8,128)(2,1)S(1)} %collective-permute-done.first_ref, bf16[7,64,512]{2,1,0:T(8,128)(2,1)S(1)} %collective-permute-done.1.second_ref, ...), custom_call_target="tpu_custom_call" | custom-call | flops 7864320 | bytes 4196672 | tf_op jit(solution)/shard_map/pallas_call | solution.py:41
  24.6 1.3 collective-permute-done.2.u_edge_ref
  25.9 6.0 %shard_map.103 = (f32[8,64,512]{2,1,0:T(8,128)S(1)}, bf16[7,64,512]{2,1,0:T(8,128)(2,1)S(1)}, bf16[7,64,512]{2,1,0:T(8,128)(2,1)S(1)}) custom-call(f32[8,64,512]{2,1,0:T(8,128)S(1)} %get-tuple-element.33.u_ref, bf16[8,16,512]{2,1,0:T(8,128)(2,1)S(1)} %collective-permute-done.2.u_edge_ref, f32[8,64,512]{2,1,0:T(8,128)S(1)} %copy-done.1, ...), custom_call_target="tpu_custom_call" | custom-call | flops 1000000000 | bytes 7143424 | tf_op jit(solution)/shard_map/pallas_call | solution.py:41
  32.0 7.1 %collective-permute-start.5 = (bf16[7,64,512]{2,1,0:T(8,128)(2,1)S(1)}, bf16[7,64,512]{2,1,0:T(8,128)(2,1)S(1)}, u32[]{:S(2)}, u32[]{:S(2)}) collective-permute-start(bf16[7,64,512]{2,1,0:T(8,128)(2,1)S(1)} %get-tuple-element.42), channel_id=1, source_target_pairs={{2,4},{4,2},{6,8},{8,6},{10,12},{12,10},{14,16},{16,14},{18,20},{2... | collective-permute-start | bytes 1376264 | tf_op jit(solution)/shard_map/ppermute | solution.py:445
  39.2 5.4 %collective-permute-done.4.first_ref = bf16[7,64,512]{2,1,0:T(8,128)(2,1)S(1)} collective-permute-done((bf16[7,64,512]{2,1,0:T(8,128)(2,1)S(1)}, bf16[7,64,512]{2,1,0:T(8,128)(2,1)S(1)}, u32[]{:S(2)}, u32[]{:S(2)}) %collective-permute-start.4) | collective-permute-done | bytes 458784 | tf_op jit(solution)/shard_map/ppermute | solution.py:445
  44.6 6.1 %collective-permute-done.5.second_ref = bf16[7,64,512]{2,1,0:T(8,128)(2,1)S(1)} collective-permute-done((bf16[7,64,512]{2,1,0:T(8,128)(2,1)S(1)}, bf16[7,64,512]{2,1,0:T(8,128)(2,1)S(1)}, u32[]{:S(2)}, u32[]{:S(2)}) %collective-permute-start.5) | collective-permute-done | bytes 458784 | tf_op jit(solution)/shard_map/ppermute | solution.py:445
  50.7 2.0 %shard_map.104 = (f32[8,64,512]{2,1,0:T(8,128)S(1)}, bf16[7,64,512]{2,1,0:T(8,128)(2,1)S(1)}, bf16[7,64,512]{2,1,0:T(8,128)(2,1)S(1)}) custom-call(f32[592]{0:T(1024)S(1)} %pad_maximum_fusion.table_ref, f32[8,64,512]{2,1,0:T(8,128)S(1)} %get-tuple-element.40.own_ref, bf16[7,64,512]{2,1,0:T(8,128)(2,1)S(1)} %collective-permute-done.4.first_ref, ...), custom_call_target="tpu_custom_call" | custom-call | flops 7864320 | bytes 6031680 | tf_op jit(solution)/shard_map/pallas_call | solution.py:41
  52.8 7.1 %collective-permute-start.7 = (bf16[7,64,512]{2,1,0:T(8,128)(2,1)S(1)}, bf16[7,64,512]{2,1,0:T(8,128)(2,1)S(1)}, u32[]{:S(2)}, u32[]{:S(2)}) collective-permute-start(bf16[7,64,512]{2,1,0:T(8,128)(2,1)S(1)} %get-tuple-element.45), channel_id=1, source_target_pairs={{2,4},{4,2},{6,8},{8,6},{10,12},{12,10},{14,16},{16,14},{18,20},{2... | collective-permute-start | bytes 1376264 | tf_op jit(solution)/shard_map/ppermute | solution.py:445
  60.0 4.6 %collective-permute-done.6.first_ref = bf16[7,64,512]{2,1,0:T(8,128)(2,1)S(1)} collective-permute-done((bf16[7,64,512]{2,1,0:T(8,128)(2,1)S(1)}, bf16[7,64,512]{2,1,0:T(8,128)(2,1)S(1)}, u32[]{:S(2)}, u32[]{:S(2)}) %collective-permute-start.6) | collective-permute-done | bytes 458784 | tf_op jit(solution)/shard_map/ppermute | solution.py:445
  64.6 6.1 %collective-permute-done.7.second_ref = bf16[7,64,512]{2,1,0:T(8,128)(2,1)S(1)} collective-permute-done((bf16[7,64,512]{2,1,0:T(8,128)(2,1)S(1)}, bf16[7,64,512]{2,1,0:T(8,128)(2,1)S(1)}, u32[]{:S(2)}, u32[]{:S(2)}) %collective-permute-start.7) | collective-permute-done | bytes 458784 | tf_op jit(solution)/shard_map/ppermute | solution.py:445
  70.7 1.8 %shard_map.105 = (f32[8,64,512]{2,1,0:T(8,128)S(1)}, bf16[8,16,512]{2,1,0:T(8,128)(2,1)S(1)}) custom-call(f32[592]{0:T(1024)S(1)} %pad_maximum_fusion.table_ref, f32[8,64,512]{2,1,0:T(8,128)S(1)} %get-tuple-element.43.own_ref.before_ref, bf16[7,64,512]{2,1,0:T(8,128)(2,1)S(1)} %collective-permute-done.6.first_ref, ...), custom_call_target="tpu_custom_call" | custom-call | flops 7864320 | bytes 4196672 | tf_op jit(solution)/shard_map/pallas_call | solution.py:41
  72.5 0.3 collective-permute-start.8
  72.8 1.3 collective-permute-done.8.u_edge_ref
  74.1 6.0 %shard_map.106 = (f32[8,64,512]{2,1,0:T(8,128)S(1)}, bf16[7,64,512]{2,1,0:T(8,128)(2,1)S(1)}, bf16[7,64,512]{2,1,0:T(8,128)(2,1)S(1)}) custom-call(f32[8,64,512]{2,1,0:T(8,128)S(1)} %get-tuple-element.46.u_ref, bf16[8,16,512]{2,1,0:T(8,128)(2,1)S(1)} %collective-permute-done.8.u_edge_ref, f32[8,64,512]{2,1,0:T(8,128)S(1)} %copy-done.2, ...), custom_call_target="tpu_custom_call" | custom-call | flops 1000000000 | bytes 7143424 | tf_op jit(solution)/shard_map/pallas_call | solution.py:41
  80.2 7.3 %collective-permute-start.10 = (bf16[7,64,512]{2,1,0:T(8,128)(2,1)S(1)}, bf16[7,64,512]{2,1,0:T(8,128)(2,1)S(1)}, u32[]{:S(2)}, u32[]{:S(2)}) collective-permute-start(bf16[7,64,512]{2,1,0:T(8,128)(2,1)S(1)} %get-tuple-element.50), channel_id=1, source_target_pairs={{2,4},{4,2},{6,8},{8,6},{10,12},{12,10},{14,16},{16,14},{18,20},{2... | collective-permute-start | bytes 1376264 | tf_op jit(solution)/shard_map/ppermute | solution.py:445
  87.5 0.1 collective-permute-start.9
  87.6 11.4 %collective-permute-done.10.second_ref = bf16[7,64,512]{2,1,0:T(8,128)(2,1)S(1)} collective-permute-done((bf16[7,64,512]{2,1,0:T(8,128)(2,1)S(1)}, bf16[7,64,512]{2,1,0:T(8,128)(2,1)S(1)}, u32[]{:S(2)}, u32[]{:S(2)}) %collective-permute-start.10) | collective-permute-done | bytes 458784 | tf_op jit(solution)/shard_map/ppermute | solution.py:445
  99.0 0.8 collective-permute-done.9.first_ref
  99.8 2.9 %shard_map.107 = (f32[8,64,512]{2,1,0:T(8,128)S(1)}, f32[128,128]{1,0:T(8,128)}) custom-call(f32[592]{0:T(1024)S(1)} %pad_maximum_fusion.table_ref, f32[8,64,512]{2,1,0:T(8,128)S(1)} %get-tuple-element.48.own_ref, bf16[7,64,512]{2,1,0:T(8,128)(2,1)S(1)} %collective-permute-done.9.first_ref, bf16[7,64,512]{2,1,0:T(8,128)(2,1)S(1)} %collective-permute-done.10.second_ref, ...), custom_call_target="tpu_custom_call" | custom-call | flops 7864320 | bytes 5179712 | tf_op jit(solution)/shard_map/pallas_call | solution.py:41
  102.7 7.9 %all-to-all-start = ((f32[128,1,128]{2,1,0:T(1,128)}), f32[128,1,128]{2,1,0:T(1,128)S(1)}, u32[]{:S(2)}, u32[]{:S(2)}) async-start(f32[128,1,128]{2,1,0:T(1,128)} %bitcast.7), calls=%async_computation | async-start | bytes 131072 | tf_op jit(solution)/shard_map/all_to_all | solution.py:501
  110.8 0.2 copy.56
  111.0 0.2 reshape.84
  111.2 0.1 copy.58.w2_ref
  111.3 0.1 copy.60.w3_ref
  111.4 0.1 copy.57.b1_ref
  111.5 0.1 copy.59.b2_ref
  112.3 4.5 %shard_map.108 = (f32[3,8,4,32,256]{4,3,2,1,0:T(8,128)S(1)}, f32[8,4,32,256]{3,2,1,0:T(8,128)S(1)}) custom-call(s32[32]{0:T(128)S(1)} %reshape.78.tissue_ref, f32[8,64,512]{2,1,0:T(8,128)S(1)} %get-tuple-element.51.estimate_ref, f32[128,128]{1,0:T(8,128)} %get-tuple-element.52.mean_ref, bf16[32,32]{1,0:T(8,128)(2,1)S(1)} %pad.34.w1_ref), custom_call_target="tpu_custom_call" | custom-call | flops 100000000 | bytes 5310592 | tf_op jit(solution)/shard_map/pallas_call | solution.py:41
  116.8 1.6 %copy-done.3 = f32[3,8,4,32,256]{4,3,2,1,0:T(8,128)} copy-done((f32[3,8,4,32,256]{4,3,2,1,0:T(8,128)}, f32[3,8,4,32,256]{4,3,2,1,0:T(8,128)S(1)}, u32[]{:S(2)}) %copy-start.3) | copy-done | bytes 3145752
  118.4 0.8 all-to-all-done
  119.2 1.9 %copy-done.4 = f32[3,8,4,32,256]{4,3,2,1,0:T(8,128)S(1)} copy-done((f32[3,8,4,32,256]{4,3,2,1,0:T(8,128)S(1)}, f32[3,8,4,32,256]{4,3,2,1,0:T(8,128)}, u32[]{:S(2)}) %copy-start.4) | copy-done | bytes 3145752
  121.1 14.2 %shard_map.109 = f32[8,64,512]{2,1,0:T(8,128)} custom-call(s32[32]{0:T(128)S(1)} %reshape.78.tissue_ref, f32[8,64,512]{2,1,0:T(8,128)S(1)} %get-tuple-element.51.estimate_ref, f32[128,128]{1,0:T(8,128)} %get-tuple-element.52.mean_ref, f32[128,128]{1,0:T(8,128)S(1)} %bitcast.29, f32[3,8,4,32,256]{4,3,2,1,0:T(8,128)S(1)} %copy-done.4, ...), custom_call_target="tpu_custom_call" | custom-call | flops 1000000000 | bytes 6478340 | tf_op jit(solution)/shard_map/pallas_call | solution.py:41
  (48 shorter events, 1.4 us)
Async XLA Ops:
  0.0 1.2 copy-start
  1.4 18.4 %collective-permute-start = (bf16[7,64,512]{2,1,0:T(8,128)(2,1)S(1)}, bf16[7,64,512]{2,1,0:T(8,128)(2,1)S(1)}, u32[]{:S(2)}, u32[]{:S(2)}) collective-permute-start(bf16[7,64,512]{2,1,0:T(8,128)(2,1)S(1)} %get-tuple-element.30), channel_id=1, source_target_pairs={{0,2},{2,0},{4,6},{6,4},{8,10},{10,8},{12,14},{14,12},{16,18},{18,... | collective-permute-start | bytes 1376264 | tf_op jit(solution)/shard_map/ppermute | solution.py:445
  3.4 18.1 %collective-permute-start.1 = (bf16[7,64,512]{2,1,0:T(8,128)(2,1)S(1)}, bf16[7,64,512]{2,1,0:T(8,128)(2,1)S(1)}, u32[]{:S(2)}, u32[]{:S(2)}) collective-permute-start(bf16[7,64,512]{2,1,0:T(8,128)(2,1)S(1)} %get-tuple-element.31), channel_id=1, source_target_pairs={{2,4},{4,2},{6,8},{8,6},{10,12},{12,10},{14,16},{16,14},{18,20},{2... | collective-permute-start | bytes 1376264 | tf_op jit(solution)/shard_map/ppermute | solution.py:445
  10.5 14.1 %collective-permute-start.3 = (f32[8,16,512]{2,1,0:T(8,128)S(1)}, f32[8,16,512]{2,1,0:T(8,128)S(1)}, u32[]{:S(2)}, u32[]{:S(2)}) collective-permute-start(f32[8,16,512]{2,1,0:T(8,128)S(1)} %get-tuple-element.35), channel_id=1, source_target_pairs={{0,1},{1,0},{2,3},{3,2},{4,5},{5,4},{6,7},{7,6},{8,9},{9,8},{10,11... | collective-permute-start | bytes 786440 | tf_op jit(solution)/shard_map/ppermute | solution.py:451
  21.4 1.2 copy-start.1
  24.5 1.4 %collective-permute-start.2 = (bf16[8,16,512]{2,1,0:T(8,128)(2,1)S(1)}, bf16[8,16,512]{2,1,0:T(8,128)(2,1)S(1)}, u32[]{:S(2)}, u32[]{:S(2)}) collective-permute-start(bf16[8,16,512]{2,1,0:T(8,128)(2,1)S(1)} %get-tuple-element.34), channel_id=1, source_target_pairs={{0,1},{1,0},{2,3},{3,2},{4,5},{5,4},{6,7},{7,6},{8,9},{9,8},{10,11... | collective-permute-start | bytes 393224 | tf_op jit(solution)/shard_map/ppermute | solution.py:477
  31.9 12.7 %collective-permute-start.4 = (bf16[7,64,512]{2,1,0:T(8,128)(2,1)S(1)}, bf16[7,64,512]{2,1,0:T(8,128)(2,1)S(1)}, u32[]{:S(2)}, u32[]{:S(2)}) collective-permute-start(bf16[7,64,512]{2,1,0:T(8,128)(2,1)S(1)} %get-tuple-element.41), channel_id=1, source_target_pairs={{0,2},{2,0},{4,6},{6,4},{8,10},{10,8},{12,14},{14,12},{16,18},{18,... | collective-permute-start | bytes 1376264 | tf_op jit(solution)/shard_map/ppermute | solution.py:445
  32.0 18.7 %collective-permute-start.5 = (bf16[7,64,512]{2,1,0:T(8,128)(2,1)S(1)}, bf16[7,64,512]{2,1,0:T(8,128)(2,1)S(1)}, u32[]{:S(2)}, u32[]{:S(2)}) collective-permute-start(bf16[7,64,512]{2,1,0:T(8,128)(2,1)S(1)} %get-tuple-element.42), channel_id=1, source_target_pairs={{2,4},{4,2},{6,8},{8,6},{10,12},{12,10},{14,16},{16,14},{18,20},{2... | collective-permute-start | bytes 1376264 | tf_op jit(solution)/shard_map/ppermute | solution.py:445
  50.7 23.4 %copy-start.2 = (f32[8,64,512]{2,1,0:T(8,128)S(1)}, f32[8,64,512]{2,1,0:T(8,128)}, u32[]{:S(2)}) copy-start(f32[8,64,512]{2,1,0:T(8,128)} %observed_ref.5) | copy-start | bytes 3145732
  52.7 11.8 %collective-permute-start.6 = (bf16[7,64,512]{2,1,0:T(8,128)(2,1)S(1)}, bf16[7,64,512]{2,1,0:T(8,128)(2,1)S(1)}, u32[]{:S(2)}, u32[]{:S(2)}) collective-permute-start(bf16[7,64,512]{2,1,0:T(8,128)(2,1)S(1)} %get-tuple-element.44), channel_id=1, source_target_pairs={{0,2},{2,0},{4,6},{6,4},{8,10},{10,8},{12,14},{14,12},{16,18},{18,... | collective-permute-start | bytes 1376264 | tf_op jit(solution)/shard_map/ppermute | solution.py:445
  52.8 17.9 %collective-permute-start.7 = (bf16[7,64,512]{2,1,0:T(8,128)(2,1)S(1)}, bf16[7,64,512]{2,1,0:T(8,128)(2,1)S(1)}, u32[]{:S(2)}, u32[]{:S(2)}) collective-permute-start(bf16[7,64,512]{2,1,0:T(8,128)(2,1)S(1)} %get-tuple-element.45), channel_id=1, source_target_pairs={{2,4},{4,2},{6,8},{8,6},{10,12},{12,10},{14,16},{16,14},{18,20},{2... | collective-permute-start | bytes 1376264 | tf_op jit(solution)/shard_map/ppermute | solution.py:445
  72.5 1.6 %collective-permute-start.8 = (bf16[8,16,512]{2,1,0:T(8,128)(2,1)S(1)}, bf16[8,16,512]{2,1,0:T(8,128)(2,1)S(1)}, u32[]{:S(2)}, u32[]{:S(2)}) collective-permute-start(bf16[8,16,512]{2,1,0:T(8,128)(2,1)S(1)} %get-tuple-element.47), channel_id=1, source_target_pairs={{0,1},{1,0},{2,3},{3,2},{4,5},{5,4},{6,7},{7,6},{8,9},{9,8},{10,11... | collective-permute-start | bytes 393224 | tf_op jit(solution)/shard_map/ppermute | solution.py:477
  80.1 30.6 %copy-start.10 = (bf16[32]{0:T(256)(128)(2,1)S(1)}, bf16[32]{0:T(256)(128)(2,1)}, u32[]{:S(2)}) copy-start(bf16[32]{0:T(256)(128)(2,1)} %param.18) | copy-start | bytes 196
  80.1 30.6 %copy-start.9 = (s32[1,2,16]{2,1,0:T(2,128)S(1)}, s32[1,2,16]{2,1,0:T(2,128)}, u32[]{:S(2)}) copy-start(s32[1,2,16]{2,1,0:T(2,128)} %param.13) | copy-start | bytes 388
  80.1 30.7 %copy-start.5 = (bf16[27,32,32]{2,1,0:T(8,128)(2,1)S(1)}, bf16[27,32,32]{2,1,0:T(8,128)(2,1)}, u32[]{:S(2)}) copy-start(bf16[27,32,32]{2,1,0:T(8,128)(2,1)} %param.16) | copy-start | bytes 165892
  80.1 31.3 %copy-start.7 = (f32[32]{0:T(128)S(1)}, f32[32]{0:T(128)}, u32[]{:S(2)}) copy-start(f32[32]{0:T(128)} %param.15) | copy-start | bytes 388
  80.2 31.3 %copy-start.8 = (f32[32]{0:T(128)S(1)}, f32[32]{0:T(128)}, u32[]{:S(2)}) copy-start(f32[32]{0:T(128)} %param.17) | copy-start | bytes 388
  80.2 32.1 %copy-start.6 = (bf16[32,27]{1,0:T(8,128)(2,1)S(1)}, bf16[32,27]{1,0:T(8,128)(2,1)}, u32[]{:S(2)}) copy-start(bf16[32,27]{1,0:T(8,128)(2,1)} %param.14) | copy-start | bytes 5188
  80.2 18.8 %collective-permute-start.10 = (bf16[7,64,512]{2,1,0:T(8,128)(2,1)S(1)}, bf16[7,64,512]{2,1,0:T(8,128)(2,1)S(1)}, u32[]{:S(2)}, u32[]{:S(2)}) collective-permute-start(bf16[7,64,512]{2,1,0:T(8,128)(2,1)S(1)} %get-tuple-element.50), channel_id=1, source_target_pairs={{2,4},{4,2},{6,8},{8,6},{10,12},{12,10},{14,16},{16,14},{18,20},{2... | collective-permute-start | bytes 1376264 | tf_op jit(solution)/shard_map/ppermute | solution.py:445
  87.5 12.4 %collective-permute-start.9 = (bf16[7,64,512]{2,1,0:T(8,128)(2,1)S(1)}, bf16[7,64,512]{2,1,0:T(8,128)(2,1)S(1)}, u32[]{:S(2)}, u32[]{:S(2)}) collective-permute-start(bf16[7,64,512]{2,1,0:T(8,128)(2,1)S(1)} %get-tuple-element.49), channel_id=1, source_target_pairs={{0,2},{2,0},{4,6},{6,4},{8,10},{10,8},{12,14},{14,12},{16,18},{18,... | collective-permute-start | bytes 1376264 | tf_op jit(solution)/shard_map/ppermute | solution.py:445
  102.7 16.4 %all-to-all-start = ((f32[128,1,128]{2,1,0:T(1,128)}), f32[128,1,128]{2,1,0:T(1,128)S(1)}, u32[]{:S(2)}, u32[]{:S(2)}) async-start(f32[128,1,128]{2,1,0:T(1,128)} %bitcast.7), calls=%async_computation | async-start | bytes 131072 | tf_op jit(solution)/shard_map/all_to_all | solution.py:501
  116.8 1.6 %copy-start.3 = (f32[3,8,4,32,256]{4,3,2,1,0:T(8,128)}, f32[3,8,4,32,256]{4,3,2,1,0:T(8,128)S(1)}, u32[]{:S(2)}) copy-start(f32[3,8,4,32,256]{4,3,2,1,0:T(8,128)S(1)} %get-tuple-element.53.raw_ref) | copy-start | bytes 9437188
  119.2 1.9 %copy-start.4 = (f32[3,8,4,32,256]{4,3,2,1,0:T(8,128)S(1)}, f32[3,8,4,32,256]{4,3,2,1,0:T(8,128)}, u32[]{:S(2)}) copy-start(f32[3,8,4,32,256]{4,3,2,1,0:T(8,128)} %copy-done.3) | copy-start | bytes 9437188

commit v3 on v1

v3 whole, which is shorter than its diff:
```python
import jax
import jax.numpy as jnp
from jax import lax
from jax.experimental import pallas as pl
from jax.experimental.pallas import tpu as pltpu
from jax.sharding import PartitionSpec as P

F32 = jnp.float32
BF16 = jnp.bfloat16
SZ, SY, NX = 8, 64, 512
NZ, NY = 512, 128
TAPS, R = 15, 7
HALO = 16
EXT = SY + HALO
MODELS = 8
BY, BX = 32, 32
CH = 32
ACROSS = NX // BX
BRICKS = (SY // BY) * ACROSS
TALL = 64
WIDE = NX + 128
SPAN = SZ + 2 * R
COUNT = float(NZ * NY * NX)
LOCAL = float(SZ * SY * NX)
DEVICES = 128
AT_FORWARD = 0
AT_ADJOINT = SZ * SPAN
MIB = 1024 * 1024

VMEM = pl.BlockSpec(memory_space=pltpu.VMEM)
SMEM = pl.BlockSpec(memory_space=pltpu.SMEM)


def iota(shape, axis):
    return lax.broadcasted_iota(jnp.int32, shape, axis)


def call(kernel, outs, ins, specs, out_specs=None, scratch=(), flops=0, limit=24):
    moved = sum(x.size * x.dtype.itemsize for x in list(ins) + list(outs))
    return pl.pallas_call(
        kernel,
        out_shape=outs,
        in_specs=specs,
        out_specs=out_specs or [VMEM] * len(outs),
        scratch_shapes=scratch,
        compiler_params=pltpu.CompilerParams(vmem_limit_bytes=limit * MIB),
        cost_estimate=pl.CostEstimate(flops=flops, bytes_accessed=moved, transcendentals=0),
    )(*ins)


def shape(dims, dtype):
    return jax.ShapeDtypeStruct(dims, dtype)


def send_planes(volume_ref, first_ref, second_ref):
    even = 1 - lax.axis_index("gz") % 2

    @pl.loop(0, R)
    def _(k):
        first_ref[k] = volume_ref[k + even].astype(BF16)
        second_ref[k] = volume_ref[k + 1 - even].astype(BF16)


def edge_rows(volume, rows, gy):
    start = pl.multiple_of((1 - gy) * (SY - rows), rows)
    return volume[:, pl.ds(start, rows), :]


def shift_columns(plane):
    left = iota((plane.shape[0], 128), 1) < 64
    turned = pltpu.roll(plane, 64, axis=1)
    edge = turned[:, :128]
    return jnp.concatenate(
        [jnp.where(left, 0.0, edge), turned[:, 128:], jnp.where(left, edge, 0.0)], axis=1
    )


def prepare_kernel(observed_ref, first_ref, second_ref, edge_ref):
    gy = lax.axis_index("gy")
    send_planes(observed_ref, first_ref, second_ref)
    edge = edge_rows(observed_ref, HALO, gy)
    for z in range(SZ):
        edge_ref[z] = shift_columns(edge[z])


def split(value):
    high = value.astype(BF16)
    return high, (value - high.astype(F32)).astype(BF16)


def setup_kernel(
    taps_ref, index_ref, rows_ref, observed_ref,
    table_ref, rows_f_ref, rows_a_ref, cols_f_ref, cols_a_ref, inverse_ref, shifted_ref,
    picked_y, picked_x, scaled,
):
    gy = lax.axis_index("gy")
    base = lax.axis_index("gz") * SZ - R

    def model(j):
        plane = base + j
        valid = (plane >= 0) & (plane < NZ)
        return index_ref[jnp.clip(plane, 0, NZ - 1)], valid

    picked_y[...] = jnp.zeros(picked_y.shape, F32)
    picked_x[...] = jnp.zeros(picked_x.shape, F32)
    for j in range(SPAN):
        which, valid = model(j)
        keep = jnp.where(valid, 1.0, 0.0)
        picked_y[j : j + 1, :] = rows_ref[pl.ds(MODELS + which, 1), :] * keep
        picked_x[j : j + 1, :] = rows_ref[pl.ds(2 * MODELS + which, 1), :] * keep
        for z in range(SZ):
            if 0 <= j - z < TAPS:
                own, _ = model(z + R)
                table_ref[AT_FORWARD + z * SPAN + j] = taps_ref[own * TAPS + j - z] * keep
                table_ref[AT_ADJOINT + j * SZ + z] = (
                    taps_ref[which * TAPS + z + TAPS - 1 - j] * keep
                )

    def place(index):
        return jnp.where(index < SY, index, jnp.where(gy == 0, index, index - EXT))

    lane = iota((EXT, 256), 1)
    piece = lane // EXT
    inside = place(lane - piece * EXT)
    outside = place(iota((EXT, 256), 0))
    used = piece < 3
    tap_f = jnp.where(used, inside - outside + R, -1)
    tap_a = jnp.where(used, outside - inside + R, -1)[:SY]
    low = piece == 1
    source = iota((256, 128), 0)
    target = iota((256, 128), 1)
    tap_cf = source - target - (64 - R)
    tap_ca = target - source + (64 + R)

    @pl.loop(0, SZ)
    def _(z):
        own, _ = model(z + R)

        def table(taps, axis):
            at = (axis * MODELS + own) * TAPS
            total = jnp.zeros(taps.shape, F32)
            for t in range(TAPS):
                total = jnp.where(taps == t, taps_ref[at + t], total)
            return total

        def halves(value, is_low):
            high = value.astype(BF16).astype(F32)
            return jnp.where(is_low, value - high, high).astype(BF16)

        rows_f_ref[z] = halves(table(tap_f, 1), low)
        rows_a_ref[z] = halves(table(tap_a, 1), low[:SY])
        for taps, out in ((tap_cf, cols_f_ref), (tap_ca, cols_a_ref)):
            high, rest = split(table(taps, 2))
            out[z, :, :128] = high
            out[z, :, 128:] = rest
        shifted_ref[z] = shift_columns(observed_ref[z])

    def exact(left, right, contract):
        return lax.dot_general(
            left, right, (contract, ((), ())),
            precision=lax.Precision.HIGHEST, preferred_element_type=F32,
        )

    at_y = iota((SY, 128), 0) + gy * SY + R - iota((SY, 128), 1)
    at_x = iota((128, NX), 1) + R - iota((128, NX), 0)
    along = exact(
        jnp.where((at_y >= 0) & (at_y < NY), 1.0, 0.0), picked_y[...], ((1,), (1,))
    )
    across = exact(picked_x[...], jnp.where((at_x >= 0) & (at_x < NX), 1.0, 0.0), ((1,), (0,)))
    for z in range(SZ):
        scaled[...] = jnp.zeros(scaled.shape, F32)
        for j in range(z, z + TAPS):
            scaled[j : j + 1, :] = across[j : j + 1, :] * table_ref[AT_ADJOINT + j * SZ + z]
        inverse_ref[z] = 1.0 / exact(along, scaled[...], ((1,), (0,)))


def plane_pass(coefficient, own_ref, first_ref, second_ref, emit):
    even = lax.axis_index("gz") % 2 == 0
    high, wide = 16, 256

    def run(low_ref, high_ref):
        @pl.loop(0, SY // high)
        def _(block):
            rows = pl.ds(pl.multiple_of(block * high, high), high)
            for part in range(NX // wide):
                lanes = pl.ds(part * wide, wide)
                planes = [low_ref[k, rows, lanes].astype(F32) for k in range(R)]
                planes += [own_ref[k, rows, lanes] for k in range(SZ)]
                planes += [high_ref[k, rows, lanes].astype(F32) for k in range(R)]
                for z in range(SZ):
                    terms = [coefficient(z, j) * planes[j] for j in range(z, z + TAPS)]
                    while len(terms) > 1:
                        terms = [sum(terms[i : i + 2]) for i in range(0, len(terms), 2)]
                    emit(z, rows, lanes, terms[0])

    @pl.when(even)
    def _():
        run(second_ref, first_ref)

    @pl.when(jnp.logical_not(even))
    def _():
        run(first_ref, second_ref)


def forward_planes_kernel(
    table_ref, own_ref, first_ref, second_ref, inverse_ref, out_ref, edge_ref
):
    del inverse_ref
    def emit(z, rows, lanes, value):
        out_ref[z, rows, lanes] = value

    plane_pass(
        lambda z, j: table_ref[AT_FORWARD + z * SPAN + j], own_ref, first_ref, second_ref, emit
    )
    edge_ref[...] = edge_rows(out_ref, HALO, lax.axis_index("gy")).astype(BF16)


def adjoint_coefficient(table_ref):
    return lambda z, j: table_ref[AT_ADJOINT + j * SZ + z]


def update_kernel(
    table_ref, own_ref, first_ref, second_ref, before_ref, inverse_ref, out_ref, to_first_ref, to_second_ref
):
    def emit(z, rows, lanes, value):
        out_ref[z, rows, lanes] = (
            before_ref[z, rows, lanes] * value * inverse_ref[z, rows, lanes]
        )

    plane_pass(adjoint_coefficient(table_ref), own_ref, first_ref, second_ref, emit)
    send_planes(out_ref, to_first_ref, to_second_ref)


def last_update_kernel(
    table_ref, own_ref, first_ref, second_ref, before_ref, inverse_ref, out_ref, moments_ref
):
    def emit(z, rows, lanes, value):
        out_ref[z, rows, lanes] = (
            before_ref[z, rows, lanes] * value * inverse_ref[z, rows, lanes]
        )

    plane_pass(adjoint_coefficient(table_ref), own_ref, first_ref, second_ref, emit)
    total = jnp.zeros((SY, NX), F32)
    for z in range(SZ):
        total += out_ref[z]
    mean = jnp.sum(total, keepdims=True) / LOCAL
    squares = jnp.zeros((SY, NX), F32)
    for z in range(SZ):
        squares += (out_ref[z] - mean) ** 2
    deviation = jnp.sum(squares, keepdims=True)
    moments_ref[...] = jnp.where(iota((DEVICES, 128), 1) == 0, mean, deviation)


def windows_of(blocks):
    blocks = [b.astype(BF16) for b in blocks]
    pairs = [jnp.concatenate(blocks[j : j + 2], axis=1) for j in range(len(blocks) - 1)]
    return jnp.concatenate(pairs, axis=0)


def column_pass(blocks, matrix):
    product = jnp.dot(windows_of(blocks), matrix, preferred_element_type=F32)
    product = product[:, :128] + product[:, 128:]
    return [product[EXT * j : EXT * (j + 1)] for j in range(len(blocks) - 1)]


def row_pass(matrix, value):
    high, rest = split(value)
    stacked = jnp.concatenate([high, high, rest, jnp.zeros((16, NX), BF16)], axis=0)
    return jnp.dot(matrix, stacked, preferred_element_type=F32)


def ratio_kernel(
    u_ref, u_edge_ref, observed_ref, observed_edge_ref,
    rows_f_ref, rows_a_ref, cols_f_ref, cols_a_ref,
    out_ref, to_first_ref, to_second_ref,
    wide, wider,
):
    columns = NX // 128
    left = iota((EXT, 128), 1) < 64
    none = jnp.zeros((EXT, 128), F32)
    for z in range(SZ):
        extended = jnp.concatenate([u_ref[z], u_edge_ref[z].astype(F32)], axis=0)
        wide[z] = row_pass(rows_f_ref[z], extended)
    for z in range(SZ):
        blocks = [wide[z, :, 128 * j : 128 * (j + 1)] for j in range(columns)]
        blurred = column_pass([none] + blocks + [none], cols_f_ref[z])
        blurred[0] = jnp.where(left, 1.0, blurred[0])
        blurred[-1] = jnp.where(left, blurred[-1], 1.0)
        for j, block in enumerate(blurred):
            lanes = slice(128 * j, 128 * (j + 1))
            wider[z, :SY, lanes] = observed_ref[z, :, lanes] / block[:SY]
            wider[z, SY:, lanes] = observed_edge_ref[z, :, lanes] / block[SY:]
    for z in range(SZ):
        blocks = [wider[z, :, 128 * j : 128 * (j + 1)] for j in range(columns + 1)]
        wide[z] = jnp.concatenate(column_pass(blocks, cols_a_ref[z]), axis=1)
    for z in range(SZ):
        out_ref[z] = row_pass(rows_a_ref[z], wide[z])
    send_planes(out_ref, to_first_ref, to_second_ref)


def note_bricks(tissue_ref, listing):
    def note(b, count):
        listing[count] = b
        return count + jnp.where(tissue_ref[b] > 0, 1, 0)

    return lax.fori_loop(0, BRICKS, note, 0)


def place_of(brick):
    down = brick // ACROSS
    over = brick % ACROSS

    def rows_of(g):
        return pl.ds(pl.multiple_of(down * BY + 8 * g, 8), 8)

    return rows_of, pl.ds(pl.multiple_of(over // 4 * 128, 128), 128), over % 4


def bricks_kernel(
    tissue_ref, estimate_ref, moments_ref, w1_ref, w2_ref, w3_ref, b3_ref,
    out_ref, listing, stack, hidden, partial, result,
):
    means = moments_ref[:, 0:1]
    centre = jnp.sum(means, axis=0, keepdims=True) / DEVICES
    deviation = jnp.sum(moments_ref[:, 1:2] + LOCAL * (means - centre) ** 2, axis=0, keepdims=True)
    spread = jnp.sqrt(deviation / COUNT + 1e-06)
    out_ref[...] = estimate_ref[...]
    many = note_bricks(tissue_ref, listing)
    lane = iota((8, 128), 1)
    row = iota((8, 128), 0)
    group = lane // BX
    column = lane % BX
    tall_group = iota((3 * CH, 128), 1) // BX

    tall_row = iota((TALL, 128), 0)
    tall_column = iota((TALL, 128), 1) % BX
    fixed = (tall_row == 45) | (tall_row == 46)
    fixed |= (tall_row == 47) & (tall_column == 0)
    fixed |= (tall_row == 48) & (tall_column == BX - 1)
    fixed = jnp.where(fixed, 1.0, 0.0)

    @pl.when(many > 0)
    def _():
        @pl.loop(0, SZ * 8)
        def _(k):
            stack[pl.ds(pl.multiple_of(k * TALL, TALL), TALL), :] = fixed

    @pl.loop(0, many)
    def _(n):
        rows_of, lanes, quarter = place_of(listing[n])

        for z in range(SZ):
            plane = jnp.zeros((8, 128), F32)
            for g in range(4):
                block = estimate_ref[z, rows_of(g), lanes]
                turned = pltpu.roll(block, (BX * (g - quarter)) % 128, axis=1)
                plane = jnp.where(group == g, turned, plane)
            plane = (plane - centre) / spread
            before = pltpu.roll(plane, 1, axis=0)
            after = pltpu.roll(plane, 7, axis=0)
            wrapped_before = jnp.where(group == 0, 0.0, pltpu.roll(before, BX, axis=1))
            wrapped_after = jnp.where(group == 3, 0.0, pltpu.roll(after, 128 - BX, axis=1))
            versions = (
                jnp.where(row == 0, wrapped_before, before),
                plane,
                jnp.where(row == 7, wrapped_after, after),
            )
            for b, version in enumerate(versions):
                for c in range(-2, 3):
                    moved = version
                    if c != 0:
                        moved = pltpu.roll(version, -c % 128, axis=1)
                        inside = (column + c >= 0) & (column + c < BX)
                        moved = jnp.where(inside, moved, 0.0)
                    for a in range(3):
                        to = z - (a - 1)
                        if 0 <= to < SZ:
                            at = to * 8 * TALL + 15 * a + 5 * b + c + 2
                            stack[pl.ds(at, 8, stride=TALL), :] = moved

        for z in range(SZ):
            for pair in range(4):
                at = (z * 8 + 2 * pair) * TALL
                taps = [
                    stack[at + TALL * e : at + TALL * (e + 1), :].astype(BF16) for e in range(2)
                ]
                first = jnp.dot(
                    w1_ref[...], jnp.concatenate(taps, axis=1), preferred_element_type=F32
                )
                first = jnp.maximum(first, 0.0)
                for e in range(2):
                    r = 2 * pair + e
                    value = first[:, 128 * e : 128 * (e + 1)]
                    hidden[z, r + 1] = value.astype(BF16)
                    if r == 7:
                        turned = pltpu.roll(value, BX, axis=1)
                        hidden[z, 0] = jnp.where(tall_group == 0, 0.0, turned).astype(BF16)
                    if r == 0:
                        turned = pltpu.roll(value, 128 - BX, axis=1)
                        hidden[z, 9] = jnp.where(tall_group == 3, 0.0, turned).astype(BF16)

        ones = jnp.ones((16, 256), BF16)
        for z in range(SZ):
            for pair in range(4):
                taps = [
                    hidden[z, 2 * pair + e : 2 * pair + e + 3].reshape(9 * CH, 128) for e in range(2)
                ]
                taps = jnp.concatenate([jnp.concatenate(taps, axis=1), ones], axis=0)
                partial[z, pair] = jnp.dot(w2_ref[...], taps, preferred_element_type=F32)

        for z in range(SZ):
            for pair in range(4):
                total = partial[z, pair, CH : 2 * CH]
                if z > 0:
                    total += partial[z - 1, pair, :CH]
                if z < SZ - 1:
                    total += partial[z + 1, pair, 2 * CH :]
                second = jnp.maximum(total, 0.0).astype(BF16)
                last = jnp.dot(w3_ref[...], second, preferred_element_type=F32)
                result[z, 2 * pair : 2 * pair + 1, :] = last[0:1, :128]
                result[z, 2 * pair + 1 : 2 * pair + 2, :] = last[0:1, 128:]

        for z in range(SZ):
            change = (result[z] + b3_ref[...]) * spread
            for g in range(4):
                turned = pltpu.roll(change, (BX * (quarter - g)) % 128, axis=1)
                out_ref[z, rows_of(g), lanes] += jnp.where(group == quarter, turned, 0.0)


def block_weights(w_first, b_first, w_mid, b_mid, w_last):
    taps = w_first.reshape(CH, 9, 3)
    closed = jnp.full((CH,), -1e30, BF16)
    open_ = jnp.zeros((CH,), BF16)
    parts = []

    def two(value):
        high = lax.reduce_precision(value, 8, 7)
        return high.astype(BF16), (value - high).astype(BF16)

    high, rest = two(b_first)
    for c in range(3):
        spread_taps = jnp.pad(taps, ((0, 0), (0, 0), (c, 2 - c))).reshape(CH, 45)
        ends = [high, rest, closed if c == 0 else open_, closed if c == 2 else open_]
        parts.append(jnp.concatenate([spread_taps, jnp.stack(ends, axis=1)], axis=1))
    w1 = jnp.pad(jnp.concatenate(parts, axis=0), ((0, 0), (0, TALL - 49)))
    w2 = w_mid.reshape(3, 9, CH, CH).transpose(0, 2, 1, 3).reshape(3 * CH, 9 * CH)
    high, rest = two(b_mid)
    bias = jnp.pad(jnp.stack([high, rest], axis=1), ((CH, CH), (0, 14)))
    w2 = jnp.concatenate([w2, bias], axis=1)
    w3 = jnp.pad(w_last[None, :], ((0, 15), (0, 0)))
    return w1, w2, w3


def body(observed, psf_taps, psf_index, tissue, w_first, b_first, w_mid, b_mid, w_last, b_last):
    slabs = NZ // SZ
    first_pairs = [(i, i ^ 1) for i in range(slabs)]
    second_pairs = [(i, ((i + 1) ^ 1) - 1) for i in range(1, slabs - 1)]
    swap = [(0, 1), (1, 0)]
    volume = shape((SZ, SY, NX), F32)
    planes = shape((R, SY, NX), BF16)

    def beside(first, second):
        return lax.ppermute(first, "gz", first_pairs), lax.ppermute(second, "gz", second_pairs)

    wide = shape((SZ, SY, WIDE), F32)
    first, second, edge = call(
        prepare_kernel, [planes, planes, shape((SZ, HALO, WIDE), F32)], [observed], [VMEM], limit=8
    )
    first, second = beside(first, second)
    observed_edge = lax.ppermute(edge, "gy", swap)

    normed = psf_taps.transpose(1, 0, 2)
    normed = normed / jnp.sum(normed, axis=2, keepdims=True)
    table, rows_f, rows_a, cols_f, cols_a, inverse, shifted = call(
        setup_kernel,
        [
            shape((2 * SZ * SPAN,), F32),
            shape((SZ, EXT, 256), BF16),
            shape((SZ, SY, 256), BF16),
            shape((SZ, 256, 256), BF16),
            shape((SZ, 256, 256), BF16),
            volume,
            wide,
        ],
        [
            normed.reshape(-1), psf_index,
            jnp.pad(normed.reshape(3 * MODELS, TAPS), ((0, 0), (0, 128 - TAPS))), observed,
        ],
        [SMEM, SMEM, VMEM, VMEM],
        out_specs=[SMEM] + [VMEM] * 6,
        scratch=[
            pltpu.VMEM((128, 128), F32), pltpu.VMEM((128, 128), F32), pltpu.VMEM((128, NX), F32)
        ],
        flops=100_000_000,
        limit=24,
    )

    estimate = observed
    for turn in range(2):
        u, u_edge = call(
            forward_planes_kernel,
            [volume, shape((SZ, HALO, NX), BF16)],
            [table, estimate, first, second, inverse],
            [SMEM] + [VMEM] * 4,
            flops=30 * SZ * SY * NX,
        )
        u_edge = lax.ppermute(u_edge, "gy", swap)
        q, first, second = call(
            ratio_kernel,
            [volume, planes, planes],
            [u, u_edge, shifted, observed_edge, rows_f, rows_a, cols_f, cols_a],
            [VMEM] * 8,
            scratch=[pltpu.VMEM((SZ, EXT, NX), F32), pltpu.VMEM((SZ, EXT, WIDE), F32)],
            flops=1_000_000_000,
            limit=24,
        )
        first, second = beside(first, second)
        ins = [table, q, first, second, estimate, inverse]
        specs = [SMEM] + [VMEM] * 5
        if turn == 0:
            estimate, first, second = call(
                update_kernel, [volume, planes, planes], ins, specs, flops=30 * SZ * SY * NX
            )
            first, second = beside(first, second)
        else:
            estimate, own_moments = call(
                last_update_kernel,
                [volume, shape((DEVICES, 128), F32)],
                ins,
                specs,
                flops=30 * SZ * SY * NX,
            )
    moments = lax.all_to_all(own_moments, ("gz", "gy"), 0, 0, tiled=True)

    w1, w2, w3 = block_weights(w_first, b_first, w_mid, b_mid, w_last)
    (restored,) = call(
        bricks_kernel,
        [volume],
        [tissue.reshape(-1), estimate, moments, w1, w2, w3, b_last[:, None]],
        [SMEM] + [VMEM] * 6,
        scratch=[
            pltpu.SMEM((64,), jnp.int32),
            pltpu.VMEM((SZ * 8 * TALL, 128), F32),
            pltpu.VMEM((SZ, 10, 3 * CH, 128), BF16),
            pltpu.VMEM((SZ, 4, 3 * CH, 256), F32),
            pltpu.VMEM((SZ, 8, 128), F32),
        ],
        flops=1_000_000_000,
        limit=24,
    )
    return restored


def solution(mesh):
    return jax.shard_map(
        body,
        mesh=mesh,
        in_specs=(P("gz", "gy", None), P(), P(), P("gz", "gy", None), P(), P(), P(), P(), P(), P()),
        out_specs=P("gz", "gy", None),
        check_vma=False,
    )
```

time: 152 us -> 137 us (0.901)
  the two profiles are of different devices: /device:TPU:3 before, /device:TPU:1 now
where the time goes in v3:
time: 137 us
  starting transfers between devices  47.4 us (35%)
  Pallas kernels  37.4 us (27%)
  waiting for transfers between devices  33.8 us (25%)
  local copies, waits for them, and re-layouts  16.6 us (12%)
    pallas_call x9, Pallas kernels, call(): pl.pallas_call(kernel, out_shape=outs, in_specs=specs, out_specs=out_spec...  37.4 us
    ppermute x4, waiting for transfers between devices, beside(): lax.ppermute(first, 'gz', first_pairs)  22.6 us
    all_to_all x1, starting transfers between devices, body(): moments = lax.all_to_all(own_moments, ('gz', 'gy'), 0, 0, tiled=True)  20.4 us
    ppermute x4, starting transfers between devices, beside(): lax.ppermute(first, 'gz', first_pairs)  19.3 us
    unnamed x55, local copies, waits for them, and re-layouts  11 us
    all_to_all x1, waiting for transfers between devices, body(): moments = lax.all_to_all(own_moments, ('gz', 'gy'), 0, 0, tiled=True)  9.23 us
    ppermute x4, starting transfers between devices, beside(): lax.ppermute(second, 'gz', second_pairs)  4.35 us
  transfers between devices with their start and end apart: 12, of which 6 were waited for; matrix products, arithmetic and copies ran while one was open for 5% of the time, Pallas kernels for 8%

profile of v3, /device:TPU:1, one launch (start us, length us, event | category | flops | bytes accessed | tf_op | source)
XLA Modules:
  0.0 137.3 jit_solution(16254131130951833314)
XLA Ops:
  0.0 1.2 copy-done.1
  1.2 1.2 shard_map.101
  2.4 2.5 %collective-permute-start = (bf16[7,64,512]{2,1,0:T(8,128)(2,1)}, bf16[7,64,512]{2,1,0:T(8,128)(2,1)}, u32[]{:S(2)}, u32[]{:S(2)}) collective-permute-start(bf16[7,64,512]{2,1,0:T(8,128)(2,1)} %get-tuple-element.31), channel_id=1, source_target_pairs={{0,2},{2,0},{4,6},{6,4},{8,10},{10,8},{12,14},{14,12},{16,18},{18,... | collective-permute-start | bytes 1376264 | tf_op jit(solution)/shard_map/ppermute | solution.py:463
  4.9 1.4 %collective-permute-start.1 = (bf16[7,64,512]{2,1,0:T(8,128)(2,1)}, bf16[7,64,512]{2,1,0:T(8,128)(2,1)}, u32[]{:S(2)}, u32[]{:S(2)}) collective-permute-start(bf16[7,64,512]{2,1,0:T(8,128)(2,1)} %get-tuple-element.32), channel_id=1, source_target_pairs={{2,4},{4,2},{6,8},{8,6},{10,12},{12,10},{14,16},{16,14},{18,20},{2... | collective-permute-start | bytes 1376264 | tf_op jit(solution)/shard_map/ppermute | solution.py:463
  6.3 1.0 collective-permute-start.3
  7.3 0.2 fusion.1
  7.7 0.7 copy-done.19
  8.3 7.2 %shard_map.100 = (f32[352]{0:T(512)S(1)}, bf16[8,80,256]{2,1,0:T(8,128)(2,1)S(1)}, bf16[8,64,256]{2,1,0:T(8,128)(2,1)S(1)}, bf16[8,256,256]{2,1,0:T(8,128)(2,1)S...) custom-call(f32[360]{0:T(512)S(1)} %reshape.31.taps_ref, ...), custom_call_target="tpu_custom_call" | custom-call | flops 100000000 | bytes 6112032 | tf_op jit(solution)/shard_map/pallas_call | solution.py:40
  15.6 3.1 %shard_map.102 = (f32[8,64,512]{2,1,0:T(8,128)S(1)}, bf16[8,16,512]{2,1,0:T(8,128)(2,1)S(1)}) custom-call(f32[352]{0:T(512)S(1)} %get-tuple-element.30.table_ref, f32[8,64,512]{2,1,0:T(8,128)S(1)} %copy-done.2, bf16[7,64,512]{2,1,0:T(8,128)(2,1)} %collective-permute-done.first_ref, bf16[7,64,512]{2,1,0:T(8,128)(2,1)} %collective-permute-done.1.second_ref, ...), custom_call_target="tpu_custom_call" | custom-call | flops 7864320 | bytes 4195712 | tf_op jit(solution)/shard_map/pallas_call | solution.py:40
  18.7 0.4 collective-permute-start.2
  19.2 1.0 collective-permute-done.2.u_edge_ref
  20.2 2.7 %shard_map.103 = (f32[8,64,512]{2,1,0:T(8,128)S(1)}, bf16[7,64,512]{2,1,0:T(8,128)(2,1)S(1)}, bf16[7,64,512]{2,1,0:T(8,128)(2,1)S(1)}) custom-call(f32[8,64,512]{2,1,0:T(8,128)S(1)} %get-tuple-element.34.u_ref, bf16[8,16,512]{2,1,0:T(8,128)(2,1)S(1)} %collective-permute-done.2.u_edge_ref, f32[8,64,640]{2,1,0:T(8,128)S(1)} %get-tuple-element.36.observed_ref, ...), custom_call_target="tpu_custom_call" | custom-call | flops 1000000000 | bytes 7471104 | tf_op jit(solution)/shard_map/pallas_call | solution.py:40
  22.9 4.9 %collective-permute-start.4 = (bf16[7,64,512]{2,1,0:T(8,128)(2,1)S(1)}, bf16[7,64,512]{2,1,0:T(8,128)(2,1)S(1)}, u32[]{:S(2)}, u32[]{:S(2)}) collective-permute-start(bf16[7,64,512]{2,1,0:T(8,128)(2,1)S(1)} %get-tuple-element.43), channel_id=1, source_target_pairs={{0,2},{2,0},{4,6},{6,4},{8,10},{10,8},{12,14},{14,12},{16,18},{18,... | collective-permute-start | bytes 1376264 | tf_op jit(solution)/shard_map/ppermute | solution.py:463
  27.8 0.7 collective-permute-start.5
  28.5 9.9 %collective-permute-done.4.first_ref = bf16[7,64,512]{2,1,0:T(8,128)(2,1)S(1)} collective-permute-done((bf16[7,64,512]{2,1,0:T(8,128)(2,1)S(1)}, bf16[7,64,512]{2,1,0:T(8,128)(2,1)S(1)}, u32[]{:S(2)}, u32[]{:S(2)}) %collective-permute-start.4) | collective-permute-done | bytes 458784 | tf_op jit(solution)/shard_map/ppermute | solution.py:463
  38.4 3.0 %shard_map.104 = (f32[8,64,512]{2,1,0:T(8,128)S(1)}, bf16[7,64,512]{2,1,0:T(8,128)(2,1)}, bf16[7,64,512]{2,1,0:T(8,128)(2,1)}) custom-call(f32[352]{0:T(512)S(1)} %get-tuple-element.30.table_ref, f32[8,64,512]{2,1,0:T(8,128)S(1)} %get-tuple-element.42.own_ref, bf16[7,64,512]{2,1,0:T(8,128)(2,1)S(1)} %collective-permute-done.4.first_ref, ...), custom_call_target="tpu_custom_call" | custom-call | flops 7864320 | bytes 6030720 | tf_op jit(solution)/shard_map/pallas_call | solution.py:40
  41.4 1.0 copy-done.3
  42.4 5.2 %collective-permute-start.6 = (bf16[7,64,512]{2,1,0:T(8,128)(2,1)}, bf16[7,64,512]{2,1,0:T(8,128)(2,1)S(1)}, u32[]{:S(2)}, u32[]{:S(2)}) collective-permute-start(bf16[7,64,512]{2,1,0:T(8,128)(2,1)} %get-tuple-element.46), channel_id=1, source_target_pairs={{0,2},{2,0},{4,6},{6,4},{8,10},{10,8},{12,14},{14,12},{16,18},{18,... | collective-permute-start | bytes 1376264 | tf_op jit(solution)/shard_map/ppermute | solution.py:463
  47.6 0.7 collective-permute-start.7
  48.5 9.0 %collective-permute-done.6.first_ref = bf16[7,64,512]{2,1,0:T(8,128)(2,1)S(1)} collective-permute-done((bf16[7,64,512]{2,1,0:T(8,128)(2,1)}, bf16[7,64,512]{2,1,0:T(8,128)(2,1)S(1)}, u32[]{:S(2)}, u32[]{:S(2)}) %collective-permute-start.6) | collective-permute-done | bytes 458784 | tf_op jit(solution)/shard_map/ppermute | solution.py:463
  57.5 0.8 copy-done.15
  58.3 0.8 copy-done.17
  59.1 1.2 copy-done.4
  60.3 1.0 copy-done.16
  61.3 1.0 copy-done.18
  62.4 1.8 %shard_map.105 = (f32[8,64,512]{2,1,0:T(8,128)S(1)}, bf16[8,16,512]{2,1,0:T(8,128)(2,1)S(1)}) custom-call(f32[352]{0:T(512)S(1)} %get-tuple-element.30.table_ref, f32[8,64,512]{2,1,0:T(8,128)S(1)} %copy-done.4, bf16[7,64,512]{2,1,0:T(8,128)(2,1)S(1)} %copy-done.16, bf16[7,64,512]{2,1,0:T(8,128)(2,1)S(1)} %copy-done.18, ...), custom_call_target="tpu_custom_call" | custom-call | flops 7864320 | bytes 4195712 | tf_op jit(solution)/shard_map/pallas_call | solution.py:40
  64.2 1.9 %collective-permute-start.8 = (bf16[8,16,512]{2,1,0:T(8,128)(2,1)S(1)}, bf16[8,16,512]{2,1,0:T(8,128)(2,1)S(1)}, u32[]{:S(2)}, u32[]{:S(2)}) collective-permute-start(bf16[8,16,512]{2,1,0:T(8,128)(2,1)S(1)} %get-tuple-element.49), channel_id=1, source_target_pairs={{0,1},{1,0},{2,3},{3,2},{4,5},{5,4},{6,7},{7,6},{8,9},{9,8},{10,11... | collective-permute-start | bytes 393224 | tf_op jit(solution)/shard_map/ppermute | solution.py:507
  66.1 1.0 collective-permute-done.8.u_edge_ref
  67.1 3.6 %shard_map.106 = (f32[8,64,512]{2,1,0:T(8,128)S(1)}, bf16[7,64,512]{2,1,0:T(8,128)(2,1)}, bf16[7,64,512]{2,1,0:T(8,128)(2,1)}) custom-call(f32[8,64,512]{2,1,0:T(8,128)S(1)} %get-tuple-element.48.u_ref, bf16[8,16,512]{2,1,0:T(8,128)(2,1)S(1)} %collective-permute-done.8.u_edge_ref, f32[8,64,640]{2,1,0:T(8,128)S(1)} %get-tuple-element.36.observed_ref, ...), custom_call_target="tpu_custom_call" | custom-call | flops 1000000000 | bytes 7471104 | tf_op jit(solution)/shard_map/pallas_call | solution.py:40
  70.7 1.0 copy-done.11
  71.7 1.6 %collective-permute-start.10 = (bf16[7,64,512]{2,1,0:T(8,128)(2,1)}, bf16[7,64,512]{2,1,0:T(8,128)(2,1)}, u32[]{:S(2)}, u32[]{:S(2)}) collective-permute-start(bf16[7,64,512]{2,1,0:T(8,128)(2,1)} %get-tuple-element.52), channel_id=1, source_target_pairs={{2,4},{4,2},{6,8},{8,6},{10,12},{12,10},{14,16},{16,14},{18,20},{2... | collective-permute-start | bytes 1376264 | tf_op jit(solution)/shard_map/ppermute | solution.py:463
  73.3 6.7 %collective-permute-start.9 = (bf16[7,64,512]{2,1,0:T(8,128)(2,1)}, bf16[7,64,512]{2,1,0:T(8,128)(2,1)}, u32[]{:S(2)}, u32[]{:S(2)}) collective-permute-start(bf16[7,64,512]{2,1,0:T(8,128)(2,1)} %get-tuple-element.51), channel_id=1, source_target_pairs={{0,2},{2,0},{4,6},{6,4},{8,10},{10,8},{12,14},{14,12},{16,18},{18,... | collective-permute-start | bytes 1376264 | tf_op jit(solution)/shard_map/ppermute | solution.py:463
  80.5 0.7 concatenate.18
  81.1 0.7 concatenate.21
  82.0 0.7 copy.46
  82.7 1.1 copy.45
  83.8 0.2 reshape.38
  84.0 0.1 copy.47
  84.1 0.7 pad.34.w3_ref
  85.4 0.8 reshape.30.tissue_ref
  86.2 0.8 fusion.3.w2_ref
  86.9 3.6 %collective-permute-done.9.first_ref = bf16[7,64,512]{2,1,0:T(8,128)(2,1)} collective-permute-done((bf16[7,64,512]{2,1,0:T(8,128)(2,1)}, bf16[7,64,512]{2,1,0:T(8,128)(2,1)}, u32[]{:S(2)}, u32[]{:S(2)}) %collective-permute-start.9) | collective-permute-done | bytes 458784 | tf_op jit(solution)/shard_map/ppermute | solution.py:463
  90.6 3.6 %shard_map.107 = (f32[8,64,512]{2,1,0:T(8,128)S(1)}, f32[128,128]{1,0:T(8,128)}) custom-call(f32[352]{0:T(512)S(1)} %get-tuple-element.30.table_ref, f32[8,64,512]{2,1,0:T(8,128)S(1)} %copy-done.12, bf16[7,64,512]{2,1,0:T(8,128)(2,1)} %collective-permute-done.9.first_ref, bf16[7,64,512]{2,1,0:T(8,128)(2,1)} %collective-permute-done.10.second_ref, ...), custom_call_target="tpu_custom_call" | custom-call | flops 7864320 | bytes 5178752 | tf_op jit(solution)/shard_map/pallas_call | solution.py:40
  94.2 1.0 copy-done.20
  95.2 20.4 %all-to-all-start = ((f32[128,1,128]{2,1,0:T(1,128)}), f32[128,1,128]{2,1,0:T(1,128)S(1)}, u32[]{:S(2)}, u32[]{:S(2)}) async-start(f32[128,1,128]{2,1,0:T(1,128)} %bitcast.3), calls=%async_computation | async-start | bytes 131072 | tf_op jit(solution)/shard_map/all_to_all | solution.py:533
  115.7 9.2 %all-to-all-done = f32[128,1,128]{2,1,0:T(1,128)S(1)} async-done(((f32[128,1,128]{2,1,0:T(1,128)}), f32[128,1,128]{2,1,0:T(1,128)S(1)}, u32[]{:S(2)}, u32[]{:S(2)}) %all-to-all-start) | async-done | bytes 65568 | tf_op jit(solution)/shard_map/all_to_all | solution.py:533
  125.0 1.2 copy-done.21
  126.2 11.1 %shard_map.108 = f32[8,64,512]{2,1,0:T(8,128)} custom-call(s32[32]{0:T(128)S(1)} %reshape.30.tissue_ref, f32[8,64,512]{2,1,0:T(8,128)S(1)} %copy-done.21, f32[128,128]{1,0:T(8,128)S(1)} %bitcast.32, bf16[96,64]{1,0:T(8,128)(2,1)S(1)} %fusion.11.w1_ref, bf16[96,304]{1,0:T(8,128)(2,1)S(1)} %fusion.3.w2_ref, bf16[16,32]{1,0:T(8,128)(2,1)S(1)} %pad.34.w3_ref, ...), custom_call_target="tpu_custom_call" | custom-call | flops 1000000000 | bytes 2234500 | tf_op jit(solution)/shard_map/pallas_call | solution.py:40
  (69 shorter events, 1.0 us)
Async XLA Ops:
  0.0 7.3 %copy-start = (f32[8,3,15]{2,0,1:T(8,128)S(1)}, f32[8,3,15]{2,0,1:T(8,128)}, u32[]{:S(2)}) copy-start(f32[8,3,15]{2,0,1:T(8,128)} %param.11) | copy-start | bytes 4324
  0.0 1.2 copy-start.1
  1.2 6.4 %copy-start.2 = (f32[8,64,512]{2,1,0:T(8,128)S(1)}, f32[8,64,512]{2,1,0:T(8,128)}, u32[]{:S(2)}) copy-start(f32[8,64,512]{2,1,0:T(8,128)} %before_ref.1) | copy-start | bytes 3145732
  2.4 13.2 %collective-permute-start = (bf16[7,64,512]{2,1,0:T(8,128)(2,1)}, bf16[7,64,512]{2,1,0:T(8,128)(2,1)}, u32[]{:S(2)}, u32[]{:S(2)}) collective-permute-start(bf16[7,64,512]{2,1,0:T(8,128)(2,1)} %get-tuple-element.31), channel_id=1, source_target_pairs={{0,2},{2,0},{4,6},{6,4},{8,10},{10,8},{12,14},{14,12},{16,18},{18,... | collective-permute-start | bytes 1376264 | tf_op jit(solution)/shard_map/ppermute | solution.py:463
  4.9 10.7 %collective-permute-start.1 = (bf16[7,64,512]{2,1,0:T(8,128)(2,1)}, bf16[7,64,512]{2,1,0:T(8,128)(2,1)}, u32[]{:S(2)}, u32[]{:S(2)}) collective-permute-start(bf16[7,64,512]{2,1,0:T(8,128)(2,1)} %get-tuple-element.32), channel_id=1, source_target_pairs={{2,4},{4,2},{6,8},{8,6},{10,12},{12,10},{14,16},{16,14},{18,20},{2... | collective-permute-start | bytes 1376264 | tf_op jit(solution)/shard_map/ppermute | solution.py:463
  6.3 12.9 %collective-permute-start.3 = (f32[8,16,640]{2,1,0:T(8,128)}, f32[8,16,640]{2,1,0:T(8,128)}, u32[]{:S(2)}, u32[]{:S(2)}) collective-permute-start(f32[8,16,640]{2,1,0:T(8,128)} %get-tuple-element.37), channel_id=1, source_target_pairs={{0,1},{1,0},{2,3},{3,2},{4,5},{5,4},{6,7},{7,6},{8,9},{9,8},{10,11... | collective-permute-start | bytes 983048 | tf_op jit(solution)/shard_map/ppermute | solution.py:470
  7.6 0.7 copy-start.19
  15.5 4.6 %copy-start.5 = (bf16[8,256,256]{2,1,0:T(8,128)(2,1)}, bf16[8,256,256]{2,1,0:T(8,128)(2,1)S(1)}, u32[]{:S(2)}) copy-start(bf16[8,256,256]{2,1,0:T(8,128)(2,1)S(1)} %get-tuple-element.40.cols_f_ref) | copy-start | bytes 3145732
  15.6 4.6 %copy-start.7 = (bf16[8,256,256]{2,1,0:T(8,128)(2,1)}, bf16[8,256,256]{2,1,0:T(8,128)(2,1)S(1)}, u32[]{:S(2)}) copy-start(bf16[8,256,256]{2,1,0:T(8,128)(2,1)S(1)} %get-tuple-element.41.cols_a_ref) | copy-start | bytes 3145732
  15.6 4.6 %copy-start.9 = (bf16[8,80,256]{2,1,0:T(8,128)(2,1)}, bf16[8,80,256]{2,1,0:T(8,128)(2,1)S(1)}, u32[]{:S(2)}) copy-start(bf16[8,80,256]{2,1,0:T(8,128)(2,1)S(1)} %get-tuple-element.38.rows_f_ref) | copy-start | bytes 983044
  15.6 4.6 %copy-start.13 = (bf16[8,64,256]{2,1,0:T(8,128)(2,1)}, bf16[8,64,256]{2,1,0:T(8,128)(2,1)S(1)}, u32[]{:S(2)}) copy-start(bf16[8,64,256]{2,1,0:T(8,128)(2,1)S(1)} %get-tuple-element.39.rows_a_ref) | copy-start | bytes 786436
  18.7 1.4 %collective-permute-start.2 = (bf16[8,16,512]{2,1,0:T(8,128)(2,1)S(1)}, bf16[8,16,512]{2,1,0:T(8,128)(2,1)S(1)}, u32[]{:S(2)}, u32[]{:S(2)}) collective-permute-start(bf16[8,16,512]{2,1,0:T(8,128)(2,1)S(1)} %get-tuple-element.35), channel_id=1, source_target_pairs={{0,1},{1,0},{2,3},{3,2},{4,5},{5,4},{6,7},{7,6},{8,9},{9,8},{10,11... | collective-permute-start | bytes 393224 | tf_op jit(solution)/shard_map/ppermute | solution.py:507
  22.9 15.5 %collective-permute-start.4 = (bf16[7,64,512]{2,1,0:T(8,128)(2,1)S(1)}, bf16[7,64,512]{2,1,0:T(8,128)(2,1)S(1)}, u32[]{:S(2)}, u32[]{:S(2)}) collective-permute-start(bf16[7,64,512]{2,1,0:T(8,128)(2,1)S(1)} %get-tuple-element.43), channel_id=1, source_target_pairs={{0,2},{2,0},{4,6},{6,4},{8,10},{10,8},{12,14},{14,12},{16,18},{18,... | collective-permute-start | bytes 1376264 | tf_op jit(solution)/shard_map/ppermute | solution.py:463
  27.8 10.6 %collective-permute-start.5 = (bf16[7,64,512]{2,1,0:T(8,128)(2,1)S(1)}, bf16[7,64,512]{2,1,0:T(8,128)(2,1)S(1)}, u32[]{:S(2)}, u32[]{:S(2)}) collective-permute-start(bf16[7,64,512]{2,1,0:T(8,128)(2,1)S(1)} %get-tuple-element.44), channel_id=1, source_target_pairs={{2,4},{4,2},{6,8},{8,6},{10,12},{12,10},{14,16},{16,14},{18,20},{2... | collective-permute-start | bytes 1376264 | tf_op jit(solution)/shard_map/ppermute | solution.py:463
  38.4 9.9 %copy-start.24 = (bf16[32,27]{1,0:T(8,128)(2,1)S(1)}, bf16[32,27]{1,0:T(8,128)(2,1)}, u32[]{:S(2)}) copy-start(bf16[32,27]{1,0:T(8,128)(2,1)} %param.14) | copy-start | bytes 5188
  41.4 1.0 copy-start.3
  42.4 15.1 %collective-permute-start.6 = (bf16[7,64,512]{2,1,0:T(8,128)(2,1)}, bf16[7,64,512]{2,1,0:T(8,128)(2,1)S(1)}, u32[]{:S(2)}, u32[]{:S(2)}) collective-permute-start(bf16[7,64,512]{2,1,0:T(8,128)(2,1)} %get-tuple-element.46), channel_id=1, source_target_pairs={{0,2},{2,0},{4,6},{6,4},{8,10},{10,8},{12,14},{14,12},{16,18},{18,... | collective-permute-start | bytes 1376264 | tf_op jit(solution)/shard_map/ppermute | solution.py:463
  47.6 10.6 %collective-permute-start.7 = (bf16[7,64,512]{2,1,0:T(8,128)(2,1)}, bf16[7,64,512]{2,1,0:T(8,128)(2,1)S(1)}, u32[]{:S(2)}, u32[]{:S(2)}) collective-permute-start(bf16[7,64,512]{2,1,0:T(8,128)(2,1)} %get-tuple-element.47), channel_id=1, source_target_pairs={{2,4},{4,2},{6,8},{8,6},{10,12},{12,10},{14,16},{16,14},{18,20},{2... | collective-permute-start | bytes 1376264 | tf_op jit(solution)/shard_map/ppermute | solution.py:463
  57.5 0.8 copy-start.15
  58.3 0.8 copy-start.17
  59.1 1.2 copy-start.4
  60.3 1.0 copy-start.16
  61.3 1.0 copy-start.18
  62.3 3.8 %copy-start.25 = (f32[32]{0:T(128)S(1)}, f32[32]{0:T(128)}, u32[]{:S(2)}) copy-start(f32[32]{0:T(128)} %param.15) | copy-start | bytes 388
  62.3 4.7 %copy-start.6 = (bf16[8,256,256]{2,1,0:T(8,128)(2,1)S(1)}, bf16[8,256,256]{2,1,0:T(8,128)(2,1)}, u32[]{:S(2)}) copy-start(bf16[8,256,256]{2,1,0:T(8,128)(2,1)} %copy-done.5) | copy-start | bytes 3145732
  62.3 4.7 %copy-start.8 = (bf16[8,256,256]{2,1,0:T(8,128)(2,1)S(1)}, bf16[8,256,256]{2,1,0:T(8,128)(2,1)}, u32[]{:S(2)}) copy-start(bf16[8,256,256]{2,1,0:T(8,128)(2,1)} %copy-done.7) | copy-start | bytes 3145732
  62.3 4.7 %copy-start.10 = (bf16[8,80,256]{2,1,0:T(8,128)(2,1)S(1)}, bf16[8,80,256]{2,1,0:T(8,128)(2,1)}, u32[]{:S(2)}) copy-start(bf16[8,80,256]{2,1,0:T(8,128)(2,1)} %copy-done.9) | copy-start | bytes 983044
  62.4 4.7 %copy-start.14 = (bf16[8,64,256]{2,1,0:T(8,128)(2,1)S(1)}, bf16[8,64,256]{2,1,0:T(8,128)(2,1)}, u32[]{:S(2)}) copy-start(bf16[8,64,256]{2,1,0:T(8,128)(2,1)} %copy-done.13) | copy-start | bytes 786436
  64.2 2.9 %collective-permute-start.8 = (bf16[8,16,512]{2,1,0:T(8,128)(2,1)S(1)}, bf16[8,16,512]{2,1,0:T(8,128)(2,1)S(1)}, u32[]{:S(2)}, u32[]{:S(2)}) collective-permute-start(bf16[8,16,512]{2,1,0:T(8,128)(2,1)S(1)} %get-tuple-element.49), channel_id=1, source_target_pairs={{0,1},{1,0},{2,3},{3,2},{4,5},{5,4},{6,7},{7,6},{8,9},{9,8},{10,11... | collective-permute-start | bytes 393224 | tf_op jit(solution)/shard_map/ppermute | solution.py:507
  67.1 14.9 %copy-start.26 = (f32[32]{0:T(128)S(1)}, f32[32]{0:T(128)}, u32[]{:S(2)}) copy-start(f32[32]{0:T(128)} %param.17) | copy-start | bytes 388
  70.7 1.0 copy-start.11
  71.7 18.9 %copy-start.12 = (f32[8,64,512]{2,1,0:T(8,128)S(1)}, f32[8,64,512]{2,1,0:T(8,128)}, u32[]{:S(2)}) copy-start(f32[8,64,512]{2,1,0:T(8,128)} %copy-done.11) | copy-start | bytes 3145732
  71.7 15.2 %collective-permute-start.10 = (bf16[7,64,512]{2,1,0:T(8,128)(2,1)}, bf16[7,64,512]{2,1,0:T(8,128)(2,1)}, u32[]{:S(2)}, u32[]{:S(2)}) collective-permute-start(bf16[7,64,512]{2,1,0:T(8,128)(2,1)} %get-tuple-element.52), channel_id=1, source_target_pairs={{2,4},{4,2},{6,8},{8,6},{10,12},{12,10},{14,16},{16,14},{18,20},{2... | collective-permute-start | bytes 1376264 | tf_op jit(solution)/shard_map/ppermute | solution.py:463
  73.3 17.3 %collective-permute-start.9 = (bf16[7,64,512]{2,1,0:T(8,128)(2,1)}, bf16[7,64,512]{2,1,0:T(8,128)(2,1)}, u32[]{:S(2)}, u32[]{:S(2)}) collective-permute-start(bf16[7,64,512]{2,1,0:T(8,128)(2,1)} %get-tuple-element.51), channel_id=1, source_target_pairs={{0,2},{2,0},{4,6},{6,4},{8,10},{10,8},{12,14},{14,12},{16,18},{18,... | collective-permute-start | bytes 1376264 | tf_op jit(solution)/shard_map/ppermute | solution.py:463
  90.6 25.0 %copy-start.22 = (bf16[32,49]{1,0:T(8,128)(2,1)S(1)}, bf16[32,49]{1,0:T(8,128)(2,1)}, u32[]{:S(2)}) copy-start(bf16[32,49]{1,0:T(8,128)(2,1)} %concatenate.18) | copy-start | bytes 9412
  90.6 25.1 %copy-start.23 = (bf16[32,49]{1,0:T(8,128)(2,1)S(1)}, bf16[32,49]{1,0:T(8,128)(2,1)}, u32[]{:S(2)}) copy-start(bf16[32,49]{1,0:T(8,128)(2,1)} %concatenate.21) | copy-start | bytes 9412
  94.2 1.0 copy-start.20
  95.2 29.8 %all-to-all-start = ((f32[128,1,128]{2,1,0:T(1,128)}), f32[128,1,128]{2,1,0:T(1,128)S(1)}, u32[]{:S(2)}, u32[]{:S(2)}) async-start(f32[128,1,128]{2,1,0:T(1,128)} %bitcast.3), calls=%async_computation | async-start | bytes 131072 | tf_op jit(solution)/shard_map/all_to_all | solution.py:533
  125.0 1.2 copy-start.21

commit v4 on v3

--- a/solution.py
+++ b/solution.py
@@ -18,6 +18,7 @@
 ACROSS = NX // BX
 BRICKS = (SY // BY) * ACROSS
 TALL = 64
+DEEP = 9 * CH + 16
 WIDE = NX + 128
 SPAN = SZ + 2 * R
 COUNT = float(NZ * NY * NX)
@@ -90,8 +91,7 @@
 
 def setup_kernel(
     taps_ref, index_ref, rows_ref, observed_ref,
-    table_ref, rows_f_ref, rows_a_ref, cols_f_ref, cols_a_ref, inverse_ref, shifted_ref,
-    picked_y, picked_x, scaled,
+    table_ref, rows_f_ref, rows_a_ref, cols_f_ref, cols_a_ref, shifted_ref, picked_y, picked_x,
 ):
     gy = lax.axis_index("gy")
     base = lax.axis_index("gz") * SZ - R
@@ -155,23 +155,59 @@
             out[z, :, 128:] = rest
         shifted_ref[z] = shift_columns(observed_ref[z])
 
-    def exact(left, right, contract):
-        return lax.dot_general(
-            left, right, (contract, ((), ())),
-            precision=lax.Precision.HIGHEST, preferred_element_type=F32,
-        )
-
+def exact(left, right, contract):
+    return lax.dot_general(
+        left, right, (contract, ((), ())),
+        precision=lax.Precision.HIGHEST, preferred_element_type=F32,
+    )
+
+
+def column_of(row):
+    same = iota((CH, CH), 0) == iota((CH, CH), 1)
+    return jnp.sum(jnp.where(same, row, 0.0), axis=1, keepdims=True)
+
+
+def second_setup_kernel(
+    table_ref, picked_y_ref, picked_x_ref, w_first_ref, b_first_ref, w_mid_ref, b_mid_ref, after_ref,
+    inverse_ref, w1_ref, w2_ref, scaled,
+):
+    del after_ref
+    gy = lax.axis_index("gy")
     at_y = iota((SY, 128), 0) + gy * SY + R - iota((SY, 128), 1)
     at_x = iota((128, NX), 1) + R - iota((128, NX), 0)
     along = exact(
-        jnp.where((at_y >= 0) & (at_y < NY), 1.0, 0.0), picked_y[...], ((1,), (1,))
-    )
-    across = exact(picked_x[...], jnp.where((at_x >= 0) & (at_x < NX), 1.0, 0.0), ((1,), (0,)))
+        jnp.where((at_y >= 0) & (at_y < NY), 1.0, 0.0), picked_y_ref[...], ((1,), (1,))
+    )
+    across = exact(picked_x_ref[...], jnp.where((at_x >= 0) & (at_x < NX), 1.0, 0.0), ((1,), (0,)))
     for z in range(SZ):
         scaled[...] = jnp.zeros(scaled.shape, F32)
         for j in range(z, z + TAPS):
             scaled[j : j + 1, :] = across[j : j + 1, :] * table_ref[AT_ADJOINT + j * SZ + z]
         inverse_ref[z] = 1.0 / exact(along, scaled[...], ((1,), (0,)))
+
+    tap = iota((27, TALL), 0)
+    at = iota((27, TALL), 1)
+    lane = iota((CH, TALL), 1)
+    high, rest = split(column_of(b_first_ref[...]))
+    ends = jnp.where(lane == 45, high.astype(F32), 0.0) + jnp.where(lane == 46, rest.astype(F32), 0.0)
+    for c in range(3):
+        moved = (at == 5 * (tap // 3) + tap % 3 + c).astype(BF16)
+        block = jnp.dot(w_first_ref[...], moved, preferred_element_type=F32) + ends
+        if c != 1:
+            block += jnp.where(lane == (47 if c == 0 else 48), -1e30, 0.0)
+        w1_ref[CH * c : CH * (c + 1), :] = block.astype(BF16)
+
+    lane = iota((CH, DEEP), 1)
+    channel = iota((CH, DEEP), 0)
+    high, rest = split(column_of(b_mid_ref[...]))
+    ends = jnp.where(lane == 9 * CH, high.astype(F32), 0.0)
+    ends += jnp.where(lane == 9 * CH + 1, rest.astype(F32), 0.0)
+    for a in range(3):
+        block = ends if a == 1 else jnp.zeros((CH, DEEP), F32)
+        for t in range(9):
+            moved = (lane == CH * t + channel).astype(BF16)
+            block += jnp.dot(w_mid_ref[9 * a + t], moved, preferred_element_type=F32)
+        w2_ref[CH * a : CH * (a + 1), :] = block.astype(BF16)
 
 
 def plane_pass(coefficient, own_ref, first_ref, second_ref, emit):
@@ -202,10 +238,7 @@
         run(first_ref, second_ref)
 
 
-def forward_planes_kernel(
-    table_ref, own_ref, first_ref, second_ref, inverse_ref, out_ref, edge_ref
-):
-    del inverse_ref
+def forward_planes_kernel(table_ref, own_ref, first_ref, second_ref, out_ref, edge_ref):
     def emit(z, rows, lanes, value):
         out_ref[z, rows, lanes] = value
 
@@ -301,7 +334,7 @@
 def note_bricks(tissue_ref, listing):
     def note(b, count):
         listing[count] = b
-        return count + jnp.where(tissue_ref[b] > 0, 1, 0)
+        return count + jnp.where(tissue_ref[0, b // ACROSS, b % ACROSS] > 0, 1, 0)
 
     return lax.fori_loop(0, BRICKS, note, 0)
 
@@ -399,7 +432,8 @@
                         turned = pltpu.roll(value, 128 - BX, axis=1)
                         hidden[z, 9] = jnp.where(tall_group == 3, 0.0, turned).astype(BF16)
 
-        ones = jnp.ones((16, 256), BF16)
+        ones = jnp.ones((DEEP - 9 * CH, 256), BF16)
+        last_weights = jnp.broadcast_to(w3_ref[...].astype(F32), (16, CH)).astype(BF16)
         for z in range(SZ):
             for pair in range(4):
                 taps = [
@@ -416,45 +450,21 @@
                 if z < SZ - 1:
                     total += partial[z + 1, pair, 2 * CH :]
                 second = jnp.maximum(total, 0.0).astype(BF16)
-                last = jnp.dot(w3_ref[...], second, preferred_element_type=F32)
+                last = jnp.dot(last_weights, second, preferred_element_type=F32)
                 result[z, 2 * pair : 2 * pair + 1, :] = last[0:1, :128]
                 result[z, 2 * pair + 1 : 2 * pair + 2, :] = last[0:1, 128:]
 
         for z in range(SZ):
-            change = (result[z] + b3_ref[...]) * spread
+            change = (result[z] + b3_ref[0]) * spread
             for g in range(4):
                 turned = pltpu.roll(change, (BX * (quarter - g)) % 128, axis=1)
                 out_ref[z, rows_of(g), lanes] += jnp.where(group == quarter, turned, 0.0)
 
 
-def block_weights(w_first, b_first, w_mid, b_mid, w_last):
-    taps = w_first.reshape(CH, 9, 3)
-    closed = jnp.full((CH,), -1e30, BF16)
-    open_ = jnp.zeros((CH,), BF16)
-    parts = []
-
-    def two(value):
-        high = lax.reduce_precision(value, 8, 7)
-        return high.astype(BF16), (value - high).astype(BF16)
-
-    high, rest = two(b_first)
-    for c in range(3):
-        spread_taps = jnp.pad(taps, ((0, 0), (0, 0), (c, 2 - c))).reshape(CH, 45)
-        ends = [high, rest, closed if c == 0 else open_, closed if c == 2 else open_]
-        parts.append(jnp.concatenate([spread_taps, jnp.stack(ends, axis=1)], axis=1))
-    w1 = jnp.pad(jnp.concatenate(parts, axis=0), ((0, 0), (0, TALL - 49)))
-    w2 = w_mid.reshape(3, 9, CH, CH).transpose(0, 2, 1, 3).reshape(3 * CH, 9 * CH)
-    high, rest = two(b_mid)
-    bias = jnp.pad(jnp.stack([high, rest], axis=1), ((CH, CH), (0, 14)))
-    w2 = jnp.concatenate([w2, bias], axis=1)
-    w3 = jnp.pad(w_last[None, :], ((0, 15), (0, 0)))
-    return w1, w2, w3
-
-
 def body(observed, psf_taps, psf_index, tissue, w_first, b_first, w_mid, b_mid, w_last, b_last):
     slabs = NZ // SZ
     first_pairs = [(i, i ^ 1) for i in range(slabs)]
-    second_pairs = [(i, ((i + 1) ^ 1) - 1) for i in range(1, slabs - 1)]
+    second_pairs = [(i, ((((i + 1) % slabs) ^ 1) - 1) % slabs) for i in range(slabs)]
     swap = [(0, 1), (1, 0)]
     volume = shape((SZ, SY, NX), F32)
     planes = shape((R, SY, NX), BF16)
@@ -471,7 +481,7 @@
 
     normed = psf_taps.transpose(1, 0, 2)
     normed = normed / jnp.sum(normed, axis=2, keepdims=True)
-    table, rows_f, rows_a, cols_f, cols_a, inverse, shifted = call(
+    table, rows_f, rows_a, cols_f, cols_a, shifted, picked_y, picked_x = call(
         setup_kernel,
         [
             shape((2 * SZ * SPAN,), F32),
@@ -479,18 +489,16 @@
             shape((SZ, SY, 256), BF16),
             shape((SZ, 256, 256), BF16),
             shape((SZ, 256, 256), BF16),
-            volume,
             wide,
+            shape((128, 128), F32),
+            shape((128, 128), F32),
         ],
         [
             normed.reshape(-1), psf_index,
             jnp.pad(normed.reshape(3 * MODELS, TAPS), ((0, 0), (0, 128 - TAPS))), observed,
         ],
         [SMEM, SMEM, VMEM, VMEM],
-        out_specs=[SMEM] + [VMEM] * 6,
-        scratch=[
-            pltpu.VMEM((128, 128), F32), pltpu.VMEM((128, 128), F32), pltpu.VMEM((128, NX), F32)
-        ],
+        out_specs=[SMEM] + [VMEM] * 7,
         flops=100_000_000,
         limit=24,
     )
@@ -500,8 +508,8 @@
         u, u_edge = call(
             forward_planes_kernel,
             [volume, shape((SZ, HALO, NX), BF16)],
-            [table, estimate, first, second, inverse],
-            [SMEM] + [VMEM] * 4,
+            [table, estimate, first, second],
+            [SMEM] + [VMEM] * 3,
             flops=30 * SZ * SY * NX,
         )
         u_edge = lax.ppermute(u_edge, "gy", swap)
@@ -515,6 +523,17 @@
             limit=24,
         )
         first, second = beside(first, second)
+        if turn == 0:
+            inverse, w1, w2 = call(
+                second_setup_kernel,
+                [volume, shape((3 * CH, TALL), BF16), shape((3 * CH, DEEP), BF16)],
+                [
+                    table, picked_y, picked_x, w_first, b_first[None], w_mid, b_mid[None], q,
+                ],
+                [SMEM] + [VMEM] * 6 + [pl.BlockSpec(memory_space=pl.ANY)],
+                scratch=[pltpu.VMEM((128, NX), F32)],
+                flops=100_000_000,
+            )
         ins = [table, q, first, second, estimate, inverse]
         specs = [SMEM] + [VMEM] * 5
         if turn == 0:
@@ -532,12 +551,11 @@
             )
     moments = lax.all_to_all(own_moments, ("gz", "gy"), 0, 0, tiled=True)
 
-    w1, w2, w3 = block_weights(w_first, b_first, w_mid, b_mid, w_last)
     (restored,) = call(
         bricks_kernel,
         [volume],
-        [tissue.reshape(-1), estimate, moments, w1, w2, w3, b_last[:, None]],
-        [SMEM] + [VMEM] * 6,
+        [tissue, estimate, moments, w1, w2, w_last[None], b_last],
+        [SMEM] + [VMEM] * 5 + [SMEM],
         scratch=[
             pltpu.SMEM((64,), jnp.int32),
             pltpu.VMEM((SZ * 8 * TALL, 128), F32),

time: 137 us -> 119 us (0.87)
  the two profiles are of different devices: /device:TPU:1 before, /device:TPU:0 now
where the time goes in v4:
time: 119 us
  waiting for transfers between devices  43.4 us (36%)
  starting transfers between devices  39 us (33%)
  Pallas kernels  31.8 us (27%)
  local copies, waits for them, and re-layouts  3.46 us (3%)
    pallas_call x10, Pallas kernels, call(): pl.pallas_call(kernel, out_shape=outs, in_specs=specs, out_specs=out_spec...  31.8 us
    ppermute x4, starting transfers between devices, beside(): lax.ppermute(second, 'gz', second_pairs)  28.9 us
    ppermute x4, waiting for transfers between devices, beside(): lax.ppermute(second, 'gz', second_pairs)  23 us
    ppermute x4, waiting for transfers between devices, beside(): lax.ppermute(first, 'gz', first_pairs)  8.96 us
    all_to_all x1, waiting for transfers between devices, body(): moments = lax.all_to_all(own_moments, ('gz', 'gy'), 0, 0, tiled=True)  8.79 us
    all_to_all x1, starting transfers between devices, body(): moments = lax.all_to_all(own_moments, ('gz', 'gy'), 0, 0, tiled=True)  7.64 us
    ppermute x2, waiting for transfers between devices, body(): u_edge = lax.ppermute(u_edge, 'gy', swap)  2.66 us
  transfers between devices with their start and end apart: 12, of which 10 were waited for; matrix products, arithmetic and copies ran while one was open for 2% of the time, Pallas kernels for 9%

profile of v4, /device:TPU:0, one launch (start us, length us, event | category | flops | bytes accessed | tf_op | source)
XLA Modules:
  0.0 119.1 jit_solution(14648718629012575024)
XLA Ops:
  0.0 0.0 copy-start
  0.0 1.2 %copy-done.1 = f32[8,64,512]{2,1,0:T(8,128)S(1)} copy-done((f32[8,64,512]{2,1,0:T(8,128)S(1)}, f32[8,64,512]{2,1,0:T(8,128)}, u32[]{:S(2)}) %copy-start.1) | copy-done | bytes 1048600
  1.2 0.2 shard_map.101
  1.5 2.1 %collective-permute-start = (bf16[7,64,512]{2,1,0:T(8,128)(2,1)S(1)}, bf16[7,64,512]{2,1,0:T(8,128)(2,1)S(1)}, u32[]{:S(2)}, u32[]{:S(2)}) collective-permute-start(bf16[7,64,512]{2,1,0:T(8,128)(2,1)S(1)} %get-tuple-element.35), channel_id=1, source_target_pairs={{0,2},{2,0},{4,6},{6,4},{8,10},{10,8},{12,14},{14,12},{16,18},{18,... | collective-permute-start | bytes 1376264 | tf_op jit(solution)/shard_map/ppermute | solution.py:473
  3.6 7.2 %collective-permute-start.1 = (bf16[7,64,512]{2,1,0:T(8,128)(2,1)S(1)}, bf16[7,64,512]{2,1,0:T(8,128)(2,1)S(1)}, u32[]{:S(2)}, u32[]{:S(2)}) collective-permute-start(bf16[7,64,512]{2,1,0:T(8,128)(2,1)S(1)} %get-tuple-element.36), channel_id=1, source_target_pairs={{0,126},{2,4},{4,2},{6,8},{8,6},{10,12},{12,10},{14,16},{16,14},{1... | collective-permute-start | bytes 1376264 | tf_op jit(solution)/shard_map/ppermute | solution.py:473
  10.7 0.0 collective-permute-start.3
  10.7 0.0 copy-done
  10.7 0.7 fusion.1
  11.4 0.8 reshape.9.taps_ref
  12.2 0.7 pad.4.rows_ref
  12.9 0.0 copy-done.2
  12.9 0.7 copy-done.5
  13.6 6.2 %shard_map.100 = (f32[352]{0:T(512)S(1)}, bf16[8,80,256]{2,1,0:T(8,128)(2,1)S(1)}, bf16[8,64,256]{2,1,0:T(8,128)(2,1)S(1)}, bf16[8,256,256]{2,1,0:T(8,128)(2,1)S...) custom-call(f32[360]{0:T(512)S(1)} %reshape.9.taps_ref, ...), custom_call_target="tpu_custom_call" | custom-call | flops 100000000 | bytes 5194528 | tf_op jit(solution)/shard_map/pallas_call | solution.py:41
  19.9 0.0 collective-permute-done.first_ref
  19.9 1.1 collective-permute-done.1.second_ref
  21.0 1.8 %shard_map.102 = (f32[8,64,512]{2,1,0:T(8,128)S(1)}, bf16[8,16,512]{2,1,0:T(8,128)(2,1)S(1)}) custom-call(f32[352]{0:T(512)S(1)} %get-tuple-element.34.table_ref, f32[8,64,512]{2,1,0:T(8,128)S(1)} %copy-done.2, bf16[7,64,512]{2,1,0:T(8,128)(2,1)S(1)} %collective-permute-done.first_ref, bf16[7,64,512]{2,1,0:T(8,128)(2,1)S(1)} %collective-permute-done.1.second_ref), custom_call_target="tpu_custom_call" | custom-call | flops 7864320 | bytes 3147136 | tf_op jit(solution)/shard_map/pallas_call | solution.py:41
  22.8 0.1 collective-permute-start.2
  22.9 0.0 collective-permute-done.3.observed_edge_ref
  22.9 1.3 %collective-permute-done.2.u_edge_ref = bf16[8,16,512]{2,1,0:T(8,128)(2,1)S(1)} collective-permute-done((bf16[8,16,512]{2,1,0:T(8,128)(2,1)S(1)}, bf16[8,16,512]{2,1,0:T(8,128)(2,1)S(1)}, u32[]{:S(2)}, u32[]{:S(2)}) %collective-permute-start.2) | collective-permute-done | bytes 131104 | tf_op jit(solution)/shard_map/ppermute | solution.py:515
  24.3 1.7 %shard_map.103 = (f32[8,64,512]{2,1,0:T(8,128)S(1)}, bf16[7,64,512]{2,1,0:T(8,128)(2,1)S(1)}, bf16[7,64,512]{2,1,0:T(8,128)(2,1)S(1)}) custom-call(f32[8,64,512]{2,1,0:T(8,128)S(1)} %get-tuple-element.37.u_ref, bf16[8,16,512]{2,1,0:T(8,128)(2,1)S(1)} %collective-permute-done.2.u_edge_ref, f32[8,64,640]{2,1,0:T(8,128)S(1)} %get-tuple-element.39.observed_ref, ...), custom_call_target="tpu_custom_call" | custom-call | flops 1000000000 | bytes 7471104 | tf_op jit(solution)/shard_map/pallas_call | solution.py:41
  26.0 0.1 collective-permute-start.4
  26.0 7.2 %collective-permute-start.5 = (bf16[7,64,512]{2,1,0:T(8,128)(2,1)S(1)}, bf16[7,64,512]{2,1,0:T(8,128)(2,1)S(1)}, u32[]{:S(2)}, u32[]{:S(2)}) collective-permute-start(bf16[7,64,512]{2,1,0:T(8,128)(2,1)S(1)} %get-tuple-element.47), channel_id=1, source_target_pairs={{0,126},{2,4},{4,2},{6,8},{8,6},{10,12},{12,10},{14,16},{16,14},{1... | collective-permute-start | bytes 1376264 | tf_op jit(solution)/shard_map/ppermute | solution.py:473
  33.3 0.0 copy-done.3
  33.3 0.0 copy-done.4
  33.3 0.0 copy-done.6
  33.3 0.0 copy-done.7
  33.3 2.3 %shard_map.104 = (f32[8,64,512]{2,1,0:T(8,128)S(1)}, bf16[96,64]{1,0:T(8,128)(2,1)S(1)}, bf16[96,304]{1,0:T(8,128)(2,1)S(1)}) custom-call(f32[352]{0:T(512)S(1)} %get-tuple-element.34.table_ref, f32[128,128]{1,0:T(8,128)S(1)} %get-tuple-element.48.picked_y_ref, f32[128,128]{1,0:T(8,128)S(1)} %get-tuple-element.49.picked_x_ref, bf16[32,27]{1,0:T(8,128)(2,1)S(1)} %copy-done.4, ...), custom_call_target="tpu_custom_call" | custom-call | flops 100000000 | bytes 2357568 | tf_op jit(solution)/shard_map/pallas_call | solution.py:41
  35.6 3.0 %collective-permute-done.4.first_ref = bf16[7,64,512]{2,1,0:T(8,128)(2,1)S(1)} collective-permute-done((bf16[7,64,512]{2,1,0:T(8,128)(2,1)S(1)}, bf16[7,64,512]{2,1,0:T(8,128)(2,1)S(1)}, u32[]{:S(2)}, u32[]{:S(2)}) %collective-permute-start.4) | collective-permute-done | bytes 458784 | tf_op jit(solution)/shard_map/ppermute | solution.py:473
  38.6 5.5 %collective-permute-done.5.second_ref = bf16[7,64,512]{2,1,0:T(8,128)(2,1)S(1)} collective-permute-done((bf16[7,64,512]{2,1,0:T(8,128)(2,1)S(1)}, bf16[7,64,512]{2,1,0:T(8,128)(2,1)S(1)}, u32[]{:S(2)}, u32[]{:S(2)}) %collective-permute-start.5) | collective-permute-done | bytes 458784 | tf_op jit(solution)/shard_map/ppermute | solution.py:473
  44.1 2.0 %shard_map.105 = (f32[8,64,512]{2,1,0:T(8,128)S(1)}, bf16[7,64,512]{2,1,0:T(8,128)(2,1)S(1)}, bf16[7,64,512]{2,1,0:T(8,128)(2,1)S(1)}) custom-call(f32[352]{0:T(512)S(1)} %get-tuple-element.34.table_ref, f32[8,64,512]{2,1,0:T(8,128)S(1)} %get-tuple-element.45.after_ref.own_ref, bf16[7,64,512]{2,1,0:T(8,128)(2,1)S(1)} %collective-permute-done.4.first_ref, ...), custom_call_target="tpu_custom_call" | custom-call | flops 7864320 | bytes 6030720 | tf_op jit(solution)/shard_map/pallas_call | solution.py:41
  46.2 0.1 collective-permute-start.6
  46.2 7.2 %collective-permute-start.7 = (bf16[7,64,512]{2,1,0:T(8,128)(2,1)S(1)}, bf16[7,64,512]{2,1,0:T(8,128)(2,1)S(1)}, u32[]{:S(2)}, u32[]{:S(2)}) collective-permute-start(bf16[7,64,512]{2,1,0:T(8,128)(2,1)S(1)} %get-tuple-element.53), channel_id=1, source_target_pairs={{0,126},{2,4},{4,2},{6,8},{8,6},{10,12},{12,10},{14,16},{16,14},{1... | collective-permute-start | bytes 1376264 | tf_op jit(solution)/shard_map/ppermute | solution.py:473
  53.5 4.5 %collective-permute-done.6.first_ref = bf16[7,64,512]{2,1,0:T(8,128)(2,1)S(1)} collective-permute-done((bf16[7,64,512]{2,1,0:T(8,128)(2,1)S(1)}, bf16[7,64,512]{2,1,0:T(8,128)(2,1)S(1)}, u32[]{:S(2)}, u32[]{:S(2)}) %collective-permute-start.6) | collective-permute-done | bytes 458784 | tf_op jit(solution)/shard_map/ppermute | solution.py:473
  58.0 5.5 %collective-permute-done.7.second_ref = bf16[7,64,512]{2,1,0:T(8,128)(2,1)S(1)} collective-permute-done((bf16[7,64,512]{2,1,0:T(8,128)(2,1)S(1)}, bf16[7,64,512]{2,1,0:T(8,128)(2,1)S(1)}, u32[]{:S(2)}, u32[]{:S(2)}) %collective-permute-start.7) | collective-permute-done | bytes 458784 | tf_op jit(solution)/shard_map/ppermute | solution.py:473
  63.5 1.8 %shard_map.106 = (f32[8,64,512]{2,1,0:T(8,128)S(1)}, bf16[8,16,512]{2,1,0:T(8,128)(2,1)S(1)}) custom-call(f32[352]{0:T(512)S(1)} %get-tuple-element.34.table_ref, f32[8,64,512]{2,1,0:T(8,128)S(1)} %get-tuple-element.51.own_ref.before_ref, bf16[7,64,512]{2,1,0:T(8,128)(2,1)S(1)} %collective-permute-done.6.first_ref, ...), custom_call_target="tpu_custom_call" | custom-call | flops 7864320 | bytes 3147136 | tf_op jit(solution)/shard_map/pallas_call | solution.py:41
  65.3 0.1 collective-permute-start.8
  65.4 1.3 %collective-permute-done.8.u_edge_ref = bf16[8,16,512]{2,1,0:T(8,128)(2,1)S(1)} collective-permute-done((bf16[8,16,512]{2,1,0:T(8,128)(2,1)S(1)}, bf16[8,16,512]{2,1,0:T(8,128)(2,1)S(1)}, u32[]{:S(2)}, u32[]{:S(2)}) %collective-permute-start.8) | collective-permute-done | bytes 131104 | tf_op jit(solution)/shard_map/ppermute | solution.py:515
  66.8 1.7 %shard_map.107 = (f32[8,64,512]{2,1,0:T(8,128)S(1)}, bf16[7,64,512]{2,1,0:T(8,128)(2,1)S(1)}, bf16[7,64,512]{2,1,0:T(8,128)(2,1)S(1)}) custom-call(f32[8,64,512]{2,1,0:T(8,128)S(1)} %get-tuple-element.54.u_ref, bf16[8,16,512]{2,1,0:T(8,128)(2,1)S(1)} %collective-permute-done.8.u_edge_ref, f32[8,64,640]{2,1,0:T(8,128)S(1)} %get-tuple-element.39.observed_ref, ...), custom_call_target="tpu_custom_call" | custom-call | flops 1000000000 | bytes 7471104 | tf_op jit(solution)/shard_map/pallas_call | solution.py:41
  68.5 7.2 %collective-permute-start.10 = (bf16[7,64,512]{2,1,0:T(8,128)(2,1)S(1)}, bf16[7,64,512]{2,1,0:T(8,128)(2,1)S(1)}, u32[]{:S(2)}, u32[]{:S(2)}) collective-permute-start(bf16[7,64,512]{2,1,0:T(8,128)(2,1)S(1)} %get-tuple-element.58), channel_id=1, source_target_pairs={{0,126},{2,4},{4,2},{6,8},{8,6},{10,12},{12,10},{14,16},{16,14},{1... | collective-permute-start | bytes 1376264 | tf_op jit(solution)/shard_map/ppermute | solution.py:473
  75.7 0.0 collective-permute-start.9
  75.7 10.8 %collective-permute-done.10.second_ref = bf16[7,64,512]{2,1,0:T(8,128)(2,1)S(1)} collective-permute-done((bf16[7,64,512]{2,1,0:T(8,128)(2,1)S(1)}, bf16[7,64,512]{2,1,0:T(8,128)(2,1)S(1)}, u32[]{:S(2)}, u32[]{:S(2)}) %collective-permute-start.10) | collective-permute-done | bytes 458784 | tf_op jit(solution)/shard_map/ppermute | solution.py:473
  86.5 1.4 %collective-permute-done.9.first_ref = bf16[7,64,512]{2,1,0:T(8,128)(2,1)S(1)} collective-permute-done((bf16[7,64,512]{2,1,0:T(8,128)(2,1)S(1)}, bf16[7,64,512]{2,1,0:T(8,128)(2,1)S(1)}, u32[]{:S(2)}, u32[]{:S(2)}) %collective-permute-start.9) | collective-permute-done | bytes 458784 | tf_op jit(solution)/shard_map/ppermute | solution.py:473
  88.0 2.9 %shard_map.108 = (f32[8,64,512]{2,1,0:T(8,128)S(1)}, f32[128,128]{1,0:T(8,128)}) custom-call(f32[352]{0:T(512)S(1)} %get-tuple-element.34.table_ref, f32[8,64,512]{2,1,0:T(8,128)S(1)} %get-tuple-element.56.own_ref, bf16[7,64,512]{2,1,0:T(8,128)(2,1)S(1)} %collective-permute-done.9.first_ref, bf16[7,64,512]{2,1,0:T(8,128)(2,1)S(1)} %collective-permute-done.10.second_ref, ...), custom_call_target="tpu_custom_call" | custom-call | flops 7864320 | bytes 5178752 | tf_op jit(solution)/shard_map/pallas_call | solution.py:41
  90.9 7.6 %all-to-all-start = ((f32[128,1,128]{2,1,0:T(1,128)}), f32[128,1,128]{2,1,0:T(1,128)S(1)}, u32[]{:S(2)}, u32[]{:S(2)}) async-start(f32[128,1,128]{2,1,0:T(1,128)} %bitcast.5), calls=%async_computation | async-start | bytes 131072 | tf_op jit(solution)/shard_map/all_to_all | solution.py:552
  99.2 8.8 %all-to-all-done = f32[128,1,128]{2,1,0:T(1,128)S(1)} async-done(((f32[128,1,128]{2,1,0:T(1,128)}), f32[128,1,128]{2,1,0:T(1,128)S(1)}, u32[]{:S(2)}, u32[]{:S(2)}) %all-to-all-start) | async-done | bytes 65568 | tf_op jit(solution)/shard_map/all_to_all | solution.py:552
  108.0 0.0 copy-done.8
  108.0 0.0 copy-done.9
  108.0 11.1 %shard_map.109 = f32[8,64,512]{2,1,0:T(8,128)} custom-call(s32[1,2,16]{2,1,0:T(2,128)S(1)} %copy-done.8, f32[8,64,512]{2,1,0:T(8,128)S(1)} %get-tuple-element.59.estimate_ref, f32[128,128]{1,0:T(8,128)S(1)} %bitcast.12, bf16[96,64]{1,0:T(8,128)(2,1)S(1)} %get-tuple-element.61.w1_ref, bf16[96,304]{1,0:T(8,128)(2,1)S(1)} %get-tuple-element.62.w2_ref, ...), custom_call_target="tpu_custom_call" | custom-call | flops 1000000000 | bytes 2233540 | tf_op jit(solution)/shard_map/pallas_call | solution.py:41
  (9 shorter events, 0.0 us)
Async XLA Ops:
  0.0 10.7 %copy-start = (f32[8,3,15]{2,0,1:T(8,128)S(1)}, f32[8,3,15]{2,0,1:T(8,128)}, u32[]{:S(2)}) copy-start(f32[8,3,15]{2,0,1:T(8,128)} %param.11) | copy-start | bytes 4324
  0.0 1.2 %copy-start.1 = (f32[8,64,512]{2,1,0:T(8,128)S(1)}, f32[8,64,512]{2,1,0:T(8,128)}, u32[]{:S(2)}) copy-start(f32[8,64,512]{2,1,0:T(8,128)} %before_ref.1) | copy-start | bytes 3145732
  1.2 11.7 %copy-start.2 = (f32[8,64,512]{2,1,0:T(8,128)S(1)}, f32[8,64,512]{2,1,0:T(8,128)}, u32[]{:S(2)}) copy-start(f32[8,64,512]{2,1,0:T(8,128)} %before_ref.1) | copy-start | bytes 3145732
  1.5 18.4 %collective-permute-start = (bf16[7,64,512]{2,1,0:T(8,128)(2,1)S(1)}, bf16[7,64,512]{2,1,0:T(8,128)(2,1)S(1)}, u32[]{:S(2)}, u32[]{:S(2)}) collective-permute-start(bf16[7,64,512]{2,1,0:T(8,128)(2,1)S(1)} %get-tuple-element.35), channel_id=1, source_target_pairs={{0,2},{2,0},{4,6},{6,4},{8,10},{10,8},{12,14},{14,12},{16,18},{18,... | collective-permute-start | bytes 1376264 | tf_op jit(solution)/shard_map/ppermute | solution.py:473
  3.6 17.4 %collective-permute-start.1 = (bf16[7,64,512]{2,1,0:T(8,128)(2,1)S(1)}, bf16[7,64,512]{2,1,0:T(8,128)(2,1)S(1)}, u32[]{:S(2)}, u32[]{:S(2)}) collective-permute-start(bf16[7,64,512]{2,1,0:T(8,128)(2,1)S(1)} %get-tuple-element.36), channel_id=1, source_target_pairs={{0,126},{2,4},{4,2},{6,8},{8,6},{10,12},{12,10},{14,16},{16,14},{1... | collective-permute-start | bytes 1376264 | tf_op jit(solution)/shard_map/ppermute | solution.py:473
  10.7 12.2 %collective-permute-start.3 = (f32[8,16,640]{2,1,0:T(8,128)S(1)}, f32[8,16,640]{2,1,0:T(8,128)S(1)}, u32[]{:S(2)}, u32[]{:S(2)}) collective-permute-start(f32[8,16,640]{2,1,0:T(8,128)S(1)} %get-tuple-element.40), channel_id=1, source_target_pairs={{0,1},{1,0},{2,3},{3,2},{4,5},{5,4},{6,7},{7,6},{8,9},{9,8},{10,11... | collective-permute-start | bytes 983048 | tf_op jit(solution)/shard_map/ppermute | solution.py:480
  12.9 0.7 copy-start.5
  22.8 1.4 %collective-permute-start.2 = (bf16[8,16,512]{2,1,0:T(8,128)(2,1)S(1)}, bf16[8,16,512]{2,1,0:T(8,128)(2,1)S(1)}, u32[]{:S(2)}, u32[]{:S(2)}) collective-permute-start(bf16[8,16,512]{2,1,0:T(8,128)(2,1)S(1)} %get-tuple-element.38), channel_id=1, source_target_pairs={{0,1},{1,0},{2,3},{3,2},{4,5},{5,4},{6,7},{7,6},{8,9},{9,8},{10,11... | collective-permute-start | bytes 393224 | tf_op jit(solution)/shard_map/ppermute | solution.py:515
  24.2 9.1 %copy-start.3 = (bf16[27,32,32]{2,1,0:T(8,128)(2,1)S(1)}, bf16[27,32,32]{2,1,0:T(8,128)(2,1)}, u32[]{:S(2)}) copy-start(bf16[27,32,32]{2,1,0:T(8,128)(2,1)} %w_mid_ref.1) | copy-start | bytes 165892
  24.2 9.1 %copy-start.4 = (bf16[32,27]{1,0:T(8,128)(2,1)S(1)}, bf16[32,27]{1,0:T(8,128)(2,1)}, u32[]{:S(2)}) copy-start(bf16[32,27]{1,0:T(8,128)(2,1)} %w_first_ref.1) | copy-start | bytes 5188
  24.2 9.1 %copy-start.6 = (f32[32]{0:T(128)S(1)}, f32[32]{0:T(128)}, u32[]{:S(2)}) copy-start(f32[32]{0:T(128)} %param.15) | copy-start | bytes 388
  24.2 9.1 %copy-start.7 = (f32[32]{0:T(128)S(1)}, f32[32]{0:T(128)}, u32[]{:S(2)}) copy-start(f32[32]{0:T(128)} %param.17) | copy-start | bytes 388
  26.0 12.7 %collective-permute-start.4 = (bf16[7,64,512]{2,1,0:T(8,128)(2,1)S(1)}, bf16[7,64,512]{2,1,0:T(8,128)(2,1)S(1)}, u32[]{:S(2)}, u32[]{:S(2)}) collective-permute-start(bf16[7,64,512]{2,1,0:T(8,128)(2,1)S(1)} %get-tuple-element.46), channel_id=1, source_target_pairs={{0,2},{2,0},{4,6},{6,4},{8,10},{10,8},{12,14},{14,12},{16,18},{18,... | collective-permute-start | bytes 1376264 | tf_op jit(solution)/shard_map/ppermute | solution.py:473
  26.0 18.1 %collective-permute-start.5 = (bf16[7,64,512]{2,1,0:T(8,128)(2,1)S(1)}, bf16[7,64,512]{2,1,0:T(8,128)(2,1)S(1)}, u32[]{:S(2)}, u32[]{:S(2)}) collective-permute-start(bf16[7,64,512]{2,1,0:T(8,128)(2,1)S(1)} %get-tuple-element.47), channel_id=1, source_target_pairs={{0,126},{2,4},{4,2},{6,8},{8,6},{10,12},{12,10},{14,16},{16,14},{1... | collective-permute-start | bytes 1376264 | tf_op jit(solution)/shard_map/ppermute | solution.py:473
  46.2 11.8 %collective-permute-start.6 = (bf16[7,64,512]{2,1,0:T(8,128)(2,1)S(1)}, bf16[7,64,512]{2,1,0:T(8,128)(2,1)S(1)}, u32[]{:S(2)}, u32[]{:S(2)}) collective-permute-start(bf16[7,64,512]{2,1,0:T(8,128)(2,1)S(1)} %get-tuple-element.52), channel_id=1, source_target_pairs={{0,2},{2,0},{4,6},{6,4},{8,10},{10,8},{12,14},{14,12},{16,18},{18,... | collective-permute-start | bytes 1376264 | tf_op jit(solution)/shard_map/ppermute | solution.py:473
  46.2 17.3 %collective-permute-start.7 = (bf16[7,64,512]{2,1,0:T(8,128)(2,1)S(1)}, bf16[7,64,512]{2,1,0:T(8,128)(2,1)S(1)}, u32[]{:S(2)}, u32[]{:S(2)}) collective-permute-start(bf16[7,64,512]{2,1,0:T(8,128)(2,1)S(1)} %get-tuple-element.53), channel_id=1, source_target_pairs={{0,126},{2,4},{4,2},{6,8},{8,6},{10,12},{12,10},{14,16},{16,14},{1... | collective-permute-start | bytes 1376264 | tf_op jit(solution)/shard_map/ppermute | solution.py:473
  65.3 1.4 %collective-permute-start.8 = (bf16[8,16,512]{2,1,0:T(8,128)(2,1)S(1)}, bf16[8,16,512]{2,1,0:T(8,128)(2,1)S(1)}, u32[]{:S(2)}, u32[]{:S(2)}) collective-permute-start(bf16[8,16,512]{2,1,0:T(8,128)(2,1)S(1)} %get-tuple-element.55), channel_id=1, source_target_pairs={{0,1},{1,0},{2,3},{3,2},{4,5},{5,4},{6,7},{7,6},{8,9},{9,8},{10,11... | collective-permute-start | bytes 393224 | tf_op jit(solution)/shard_map/ppermute | solution.py:515
  68.5 18.1 %collective-permute-start.10 = (bf16[7,64,512]{2,1,0:T(8,128)(2,1)S(1)}, bf16[7,64,512]{2,1,0:T(8,128)(2,1)S(1)}, u32[]{:S(2)}, u32[]{:S(2)}) collective-permute-start(bf16[7,64,512]{2,1,0:T(8,128)(2,1)S(1)} %get-tuple-element.58), channel_id=1, source_target_pairs={{0,126},{2,4},{4,2},{6,8},{8,6},{10,12},{12,10},{14,16},{16,14},{1... | collective-permute-start | bytes 1376264 | tf_op jit(solution)/shard_map/ppermute | solution.py:473
  75.7 12.3 %collective-permute-start.9 = (bf16[7,64,512]{2,1,0:T(8,128)(2,1)S(1)}, bf16[7,64,512]{2,1,0:T(8,128)(2,1)S(1)}, u32[]{:S(2)}, u32[]{:S(2)}) collective-permute-start(bf16[7,64,512]{2,1,0:T(8,128)(2,1)S(1)} %get-tuple-element.57), channel_id=1, source_target_pairs={{0,2},{2,0},{4,6},{6,4},{8,10},{10,8},{12,14},{14,12},{16,18},{18,... | collective-permute-start | bytes 1376264 | tf_op jit(solution)/shard_map/ppermute | solution.py:473
  88.0 20.0 %copy-start.8 = (s32[1,2,16]{2,1,0:T(2,128)S(1)}, s32[1,2,16]{2,1,0:T(2,128)}, u32[]{:S(2)}) copy-start(s32[1,2,16]{2,1,0:T(2,128)} %tissue_ref.1) | copy-start | bytes 388
  88.0 20.0 %copy-start.9 = (bf16[32]{0:T(256)(128)(2,1)S(1)}, bf16[32]{0:T(256)(128)(2,1)}, u32[]{:S(2)}) copy-start(bf16[32]{0:T(256)(128)(2,1)} %param.18) | copy-start | bytes 196
  90.9 17.1 %all-to-all-start = ((f32[128,1,128]{2,1,0:T(1,128)}), f32[128,1,128]{2,1,0:T(1,128)S(1)}, u32[]{:S(2)}, u32[]{:S(2)}) async-start(f32[128,1,128]{2,1,0:T(1,128)} %bitcast.5), calls=%async_computation | async-start | bytes 131072 | tf_op jit(solution)/shard_map/all_to_all | solution.py:552
